TPU v7x, 32 devices: a whole 2x2x4 slice. The times are simulated.
32 devices in a mesh: gx: 4 (over z), gy: 8 (over y, x, core).
Axes of the slice: x: 2, y: 2, z: 4, core: 2. Of those that a mesh axis runs over, the one named last changes fastest.
Arguments:
- child_coef: bfloat16 [64, 16, 128, 128], P(('gx', 'gy')), may hold values from -6 to 6
- transfer: bfloat16 [64, 64, 2, 128, 128], P(('gx', 'gy')), may hold values from -0.125 to 0.125
- child_dir: int32 [64, 64], P(('gx', 'gy')), may hold values from 0 to 15, as said below
- couple_src: int32 [8, 64, 7], P('gx', 'gy'), may hold values from 0 to 7, as said below
- couple_kind: int32 [8, 64, 7], P('gx', 'gy'), may hold values from 0 to 7
- couple_count: int32 [8, 64], P('gx', 'gy'), may hold values from 1 to 7, as said below
- couple_table: bfloat16 [64, 8, 2, 128, 128], P('gy'), may hold values from -0.1875 to 0.1875
Outputs:
- child_local: bfloat16 [64, 16, 128, 128], P(('gx', 'gy'))
Inputs may be any that keep to these rules, and one draw needn't show every extreme that they name: `child_dir`: in every row each child direction is named by exactly four parent directions. `couple_src`: the entries of one block row are distinct and never the row's own parent cluster. `couple_count`: some row holds 7.
All inputs are finite; a program needn't handle non-finite values.
Results may differ from a plain program's by a relative error of at most 0.015.
Values may be sent and summed in bfloat16 or wider, within the bound.
No kernel may reach another device: no remote copies, remote signals or barrier semaphores. Data moves between devices by JAX's collectives and lax.ppermute only.
A program may use at most 128 MiB of HBM per device.

v0:
```python
import jax
import jax.numpy as jnp
from jax import lax
from jax.sharding import PartitionSpec as P

CPD = 2


def complex_apply(real_part, imag_part, vectors, pattern):
    halfway = vectors.shape[-1] // 2
    real_term = jnp.einsum(pattern, real_part, vectors, preferred_element_type=jnp.float32)
    imag_term = jnp.einsum(pattern, imag_part, vectors, preferred_element_type=jnp.float32)
    return jnp.concatenate(
        [
            real_term[..., :halfway] - imag_term[..., halfway:],
            real_term[..., halfway:] + imag_term[..., :halfway],
        ],
        axis=-1,
    )


def sum_children(received):
    groups = received.shape[0] // 8
    merged = received.reshape((groups, 8 // CPD, CPD) + received.shape[1:])
    partial_sums = jnp.sum(merged, axis=2).astype(jnp.bfloat16)
    return jnp.sum(partial_sums.astype(jnp.float32), axis=1).astype(jnp.bfloat16)


def body(child_coef, transfer, child_dir, couple_src, couple_kind, couple_count, couple_table):
    picked = jnp.take_along_axis(child_coef, child_dir[:, :, None, None], axis=1)
    upward = complex_apply(transfer[:, :, 0], transfer[:, :, 1], picked, "cers,cesa->cera")
    parent = sum_children(
        lax.all_to_all(
            upward.astype(jnp.bfloat16), "gy", split_axis=1, concat_axis=0, tiled=True
        ).astype(upward.dtype)
    )
    everything = lax.all_gather(parent, "gx", axis=0, tiled=True)
    dir_local = jnp.arange(parent.shape[1], dtype=jnp.int32)[None, :, None]
    sources = everything[couple_src, dir_local]
    matrices = couple_table[dir_local, couple_kind]
    products = complex_apply(
        matrices[:, :, :, 0], matrices[:, :, :, 1], sources, "uemrs,uemsa->uemra"
    )
    active = jnp.arange(couple_src.shape[-1], dtype=jnp.int32) < couple_count[..., None]
    parent_local = jnp.sum(jnp.where(active[..., None, None], products, 0.0), axis=2).astype(
        jnp.bfloat16
    )
    copies = jnp.repeat(parent_local, 8 // CPD, axis=0)
    parent_row = lax.all_to_all(copies, "gy", split_axis=0, concat_axis=1, tiled=True)[0]
    descent = complex_apply(transfer[:, :, 0], transfer[:, :, 1], parent_row, "cesr,esa->cera")
    child_index = jnp.arange(child_coef.shape[1], dtype=jnp.int32)
    onehot = (child_dir[:, None, :] == child_index[None, :, None]).astype(jnp.float32)
    child_local = jnp.einsum("cie,cera->cira", onehot, descent, precision=lax.Precision.HIGHEST)
    return child_local.astype(jnp.bfloat16)


def solution(mesh):
    return jax.shard_map(
        body,
        mesh=mesh,
        in_specs=(
            P(("gx", "gy"), None, None, None),
            P(("gx", "gy"), None, None, None, None),
            P(("gx", "gy"), None),
            P("gx", "gy", None),
            P("gx", "gy", None),
            P("gx", "gy"),
            P("gy", None, None, None, None),
        ),
        out_specs=P(("gx", "gy"), None, None, None),
        check_vma=False,
    )
```

profile of v0, /device:TPU:0, one launch (start us, length us, event | category | flops | bytes accessed | tf_op | source)
XLA Modules:
  0.0 246.8 jit_solution(4372071762388587843)
XLA Ops:
  6.5 0.0 copy-start
  6.5 0.0 all-gather.2.cloned.1.call-start
  6.5 0.8 bitcast_or_fusion
  7.3 0.7 compare_and_fusion
  8.0 0.1 reshape.55
  8.1 0.0 copy-done
  8.1 3.1 %gather_fusion.2 = bf16[128,128,128]{2,1,0:T(8,128)(2,1)} fusion(bf16[2,16,128,128]{3,2,1,0:T(8,128)(2,1)S(1)} %copy-done, s32[128]{0:T(128)S(1)} %reshape.55), kind=kCustom, calls=%fused_computation.2 | custom fusion | bytes 8389632 | tf_op jit(solution)/shard_map/jit(take_along_axis)/gather | solution.py:30
  11.2 6.4 %copy.46 = bf16[2,64,128,128]{2,3,1,0:T(8,128)(2,1)} copy(bf16[2,64,128,128]{3,2,1,0:T(8,128)(2,1)} %bitcast.70) | data formatting | bytes 8388608 | tf_op jit(solution)/shard_map/jit(take_along_axis)/gather | solution.py:30
  17.5 6.7 %fusion.11 = f32[2,64,128,128]{2,3,1,0:T(8,128)S(1)} fusion(bf16[2,64,128,128]{2,3,1,0:T(8,128)(2,1)} %copy.46, pred[2,64]{1,0:T(4,128)(4,1)S(1)} %compare_and_fusion, bf16[2,64,2,128,128]{4,3,2,1,0:T(8,128)(2,1)} %param.8), kind=kOutput, calls=%fused_computation.28 | convolution fusion | flops 538968064 | bytes 16777344 | tf_op jit(solution)/shard_map/cers,cesa->cera/dot_general | solution.py:11
  24.2 0.0 copy-done.2
  24.2 4.9 %fusion.12 = f32[2,64,128,128]{2,3,1,0:T(8,128)S(1)} fusion(bf16[2,64,128,128]{2,3,1,0:T(8,128)(2,1)S(1)} %copy-done.2, pred[2,64]{1,0:T(4,128)(4,1)S(1)} %compare_and_fusion, bf16[2,64,2,128,128]{4,3,2,1,0:T(8,128)(2,1)} %param.8), kind=kOutput, calls=%fused_computation.29 | convolution fusion | flops 538968064 | bytes 16777344 | tf_op jit(solution)/shard_map/cers,cesa->cera/dot_general | solution.py:12
  29.1 2.1 fusion.2
  31.3 0.4 pad_maximum_fusion.1
  31.7 0.3 copy.49
  32.0 54.1 %all_to_all.8 = bf16[2,64,128,128]{2,3,0,1:T(8,128)(2,1)} all-to-all(bf16[2,64,128,128]{2,3,0,1:T(8,128)(2,1)S(1)} %copy.49), channel_id=1, replica_groups=mesh['gx'=4,'gy'=8] {'gy'}, dimensions={1} | all-to-all | bytes 8388608 | tf_op jit(solution)/shard_map/all_to_all | solution.py:33
  86.1 3.4 %reduce_sum.33 = bf16[64,128,128]{1,2,0:T(8,128)(2,1)S(1)} reduce(bf16[2,64,128,128]{2,3,0,1:T(8,128)(2,1)} %all_to_all.8, bf16[]{:T(256)} %constant.25.clone.1), dimensions={0}, to_apply=%region_0.0 | reduce | flops 1048576 | bytes 6291458 | tf_op jit(solution)/shard_map/reduce_sum | solution.py:25
  89.5 0.4 reduce_sum.34
  90.0 1.0 copy.51
  91.0 0.0 all-gather.2.cloned.1.call-update
  91.0 0.0 copy-done.6
  91.0 0.1 copy.52
  91.1 0.1 reshape.49
  91.2 0.0 copy-done.7
  91.2 0.1 copy.44
  91.3 0.1 reshape.43
  91.4 10.0 %gather_fusion = bf16[112,2,128,128]{3,2,1,0:T(8,128)(2,1)} fusion(bf16[8,8,2,128,128]{4,3,2,1,0:T(8,128)(2,1)} %param.13, s32[112]{0:T(128)S(1)} %reshape.43), kind=kCustom, calls=%fused_computation | custom fusion | bytes 14680960 | tf_op jit(solution)/shard_map/gather | solution.py:40
  101.4 9.2 %copy.45 = bf16[112,2,128,128]{3,2,0,1:T(8,128)(2,1)} copy(bf16[112,2,128,128]{3,2,1,0:T(8,128)(2,1)} %gather_fusion) | data formatting | bytes 14680064 | tf_op jit(solution)/shard_map/gather | solution.py:40
  110.7 0.1 iota_compare_fusion.1
  110.7 25.7 %all-gather.2.cloned.1.call-done = bf16[8,8,128,128]{3,2,1,0:T(8,128)(2,1)} async-done(((bf16[2,8,128,128]{3,2,1,0:T(8,128)(2,1)}), bf16[8,8,128,128]{3,2,1,0:T(8,128)(2,1)}) %all-gather.2.cloned.1.call-update) | async-done | bytes 2097168 | tf_op jit(solution)/shard_map/all_gather | solution.py:37
  136.5 4.9 %gather_fusion.1 = bf16[112,128,128]{2,1,0:T(8,128)(2,1)} fusion(bf16[8,8,128,128]{3,2,1,0:T(8,128)(2,1)} %all-gather.2.cloned.1.call-done, s32[112]{0:T(128)S(1)} %reshape.49), kind=kCustom, calls=%fused_computation.1 | custom fusion | bytes 7340928 | tf_op jit(solution)/shard_map/gather | solution.py:39
  141.4 6.0 %fusion.10 = f32[2,8,7,128,128]{3,4,2,1,0:T(8,128)S(1)} fusion(bf16[2,8,7,128,128]{4,3,2,1,0:T(8,128)(2,1)} %bitcast.64, bf16[2,8,7,2,128,128]{5,4,2,1,0,3:T(8,128)(2,1)} %bitcast.66), kind=kOutput, calls=%fused_computation.27 | convolution fusion | flops 469762048 | bytes 14680064 | tf_op jit(solution)/shard_map/uemrs,uemsa->uemra/dot_general | solution.py:11
  147.4 0.3 copy-done.4
  147.7 5.6 %fusion.9 = f32[2,8,7,128,128]{3,4,2,1,0:T(8,128)} fusion(bf16[2,8,7,128,128]{4,3,2,1,0:T(8,128)(2,1)S(1)} %bitcast.65, bf16[2,8,7,2,128,128]{5,4,2,1,0,3:T(8,128)(2,1)S(1)} %bitcast.67), kind=kOutput, calls=%fused_computation.25 | convolution fusion | flops 469762048 | bytes 14680064 | tf_op jit(solution)/shard_map/uemrs,uemsa->uemra/dot_general | solution.py:12
  153.4 7.7 %slice_subtract_fusion.2 = (f32[2,8,7,128,64]{3,4,2,1,0:T(8,128)S(1)}, f32[2,8,7,128,64]{3,4,2,1,0:T(8,128)}) fusion(f32[2,8,7,128,128]{3,4,2,1,0:T(8,128)} %fusion.9, f32[2,8,7,128,128]{3,4,2,1,0:T(8,128)S(1)} %fusion.10), kind=kLoop, calls=%fused_computation.23 | loop fusion | flops 1835008 | bytes 22020096 | tf_op jit(solution)/shard_map/sub | solution.py:15
  161.1 2.6 %fusion = bf16[2,8,128,128]{2,3,1,0:T(8,128)(2,1)S(1)} fusion(f32[2,8,7,128,64]{3,4,2,1,0:T(8,128)} %get-tuple-element.10, f32[2,8,7,128,64]{3,4,2,1,0:T(8,128)S(1)} %get-tuple-element.9, pred[2,8,7]{2,1,0:T(8,128)(4,1)S(1)} %iota_compare_fusion.1), kind=kLoop, calls=%fused_computation.5 | loop fusion | flops 5242880 | bytes 7864432 | tf_op jit(solution)/shard_map/reduce_sum | solution.py:45
  163.7 1.8 broadcast_in_dim.54
  165.5 3.8 %all-to-all-start.1 = ((bf16[8,8,128,128]{2,3,1,0:T(8,128)(2,1)}), bf16[8,8,128,128]{2,3,1,0:T(8,128)(2,1)S(1)}, u32[]{:S(2)}, u32[]{:S(2)}) async-start(bf16[8,8,128,128]{2,3,1,0:T(8,128)(2,1)} %bitcast.72), calls=%async_computation.1 | async-start | bytes 4194304 | tf_op jit(solution)/shard_map/all_to_all | solution.py:49
  169.4 6.0 %slice_bitcast_fusion.1 = (bf16[2,64,128,128]{3,2,1,0:T(8,128)(2,1)}, bf16[2,64,128,128]{3,2,1,0:T(8,128)(2,1)}) fusion(bf16[2,64,2,128,128]{4,3,2,1,0:T(8,128)(2,1)} %param.8), kind=kLoop, calls=%fused_computation.18 | loop fusion | bytes 16777216 | tf_op jit(solution)/shard_map/squeeze | solution.py:31
  175.4 20.3 %all-to-all-done.1 = bf16[8,8,128,128]{2,3,1,0:T(8,128)(2,1)S(1)} async-done(((bf16[8,8,128,128]{2,3,1,0:T(8,128)(2,1)}), bf16[8,8,128,128]{2,3,1,0:T(8,128)(2,1)S(1)}, u32[]{:S(2)}, u32[]{:S(2)}) %all-to-all-start.1) | async-done | bytes 2097184 | tf_op jit(solution)/shard_map/all_to_all | solution.py:49
  195.7 6.8 %fusion.13 = f32[2,64,128,128]{2,3,0,1:T(8,128)} fusion(bf16[64,128,128,1]{1,2,3,0:T(8,128)(2,1)S(1)} %bitcast.68, bf16[2,64,128,128]{3,2,1,0:T(8,128)(2,1)} %get-tuple-element.11), kind=kOutput, calls=%fused_computation.30 | convolution fusion | flops 536870912 | bytes 14680064 | tf_op jit(solution)/shard_map/cesr,esa->cera/dot_general | solution.py:11
  202.5 4.5 %fusion.16 = f32[2,64,128,128]{2,3,0,1:T(8,128)} fusion(bf16[64,128,128,1]{1,2,3,0:T(8,128)(2,1)S(1)} %bitcast.69, bf16[2,64,128,128]{3,2,1,0:T(8,128)(2,1)S(1)} %copy-done.5), kind=kOutput, calls=%fused_computation.31 | convolution fusion | flops 536870912 | bytes 14680064 | tf_op jit(solution)/shard_map/cesr,esa->cera/dot_general | solution.py:12
  207.0 10.3 %slice_subtract_fusion = (f32[2,64,128,64]{2,3,0,1:T(8,128)S(1)}, f32[2,64,128,64]{2,3,0,1:T(8,128)}) fusion(f32[2,64,128,128]{2,3,0,1:T(8,128)} %fusion.16, f32[2,64,128,128]{2,3,0,1:T(8,128)} %fusion.13), kind=kLoop, calls=%fused_computation.7 | loop fusion | flops 2097152 | bytes 25165824 | tf_op jit(solution)/shard_map/sub | solution.py:15
  217.4 6.3 %pad_maximum_fusion = f32[2,64,128,128]{2,3,0,1:T(8,128)} fusion(f32[2,64,128,64]{2,3,0,1:T(8,128)} %get-tuple-element.6, f32[2,64,128,64]{2,3,0,1:T(8,128)S(1)} %get-tuple-element.5), kind=kLoop, calls=%fused_computation.3 | loop fusion | flops 2097152 | bytes 16777216 | tf_op jit(solution)/shard_map/concatenate | solution.py:13
  223.6 8.8 %copy.57 = f32[2,64,128,128]{3,1,2,0:T(8,128)} copy(f32[2,64,128,128]{2,3,0,1:T(8,128)} %pad_maximum_fusion) | data formatting | bytes 16777216 | tf_op jit(solution)/shard_map/concatenate | solution.py:13
  232.4 0.0 copy-done.8
  232.4 6.3 %convolution_convert_fusion = bf16[2,16,128,128]{3,1,2,0:T(8,128)(2,1)S(1)} fusion(f32[2,64,128,128]{3,1,2,0:T(8,128)} %copy.57, s32[2,64]{1,0:T(2,128)S(1)} %copy-done.8), kind=kOutput, calls=%fused_computation.34 | convolution fusion | flops 403179520 | bytes 9437696 | tf_op jit(solution)/shard_map/cie,cera->cira/dot_general | solution.py:53
  238.7 1.2 copy.58
  239.9 0.0 copy-done.1
  (14 shorter events, 0.0 us)
Async XLA Ops:
  6.5 1.5 copy-start
  6.5 129.9 %all-gather.2.cloned.1.call-start = ((), (), s32[]{:S(2)}) async-start(), calls=%async_computation.2 | async-start | bytes 2621440 | tf_op jit(solution)/shard_map/all_gather | solution.py:37
  17.5 6.7 %copy-start.2 = (bf16[2,64,128,128]{2,3,1,0:T(8,128)(2,1)S(1)}, bf16[2,64,128,128]{2,3,1,0:T(8,128)(2,1)}, u32[]{:S(2)}) copy-start(bf16[2,64,128,128]{2,3,1,0:T(8,128)(2,1)} %copy.46) | copy-start | bytes 12582916
  86.1 4.9 %copy-start.6 = (s32[2,8,7]{1,0,2:T(2,128)S(1)}, s32[2,8,7]{1,0,2:T(2,128)}, u32[]{:S(2)}) copy-start(s32[2,8,7]{1,0,2:T(2,128)} %param.10) | copy-start | bytes 1348
  86.1 5.1 %copy-start.7 = (s32[2,8,7]{1,0,2:T(2,128)S(1)}, s32[2,8,7]{1,0,2:T(2,128)}, u32[]{:S(2)}) copy-start(s32[2,8,7]{1,0,2:T(2,128)} %param.11) | copy-start | bytes 1348
  101.4 9.2 %copy-start.9 = (s32[2,8]{1,0:T(2,128)S(1)}, s32[2,8]{1,0:T(2,128)}, u32[]{:S(2)}) copy-start(s32[2,8]{1,0:T(2,128)} %param.12) | copy-start | bytes 196
  141.4 6.0 %copy-start.3 = (bf16[112,128,128]{2,1,0:T(8,128)(2,1)S(1)}, bf16[112,128,128]{2,1,0:T(8,128)(2,1)}, u32[]{:S(2)}) copy-start(bf16[112,128,128]{2,1,0:T(8,128)(2,1)} %gather_fusion.1) | copy-start | bytes 11010052
  141.4 6.3 %copy-start.4 = (bf16[112,2,128,128]{3,2,0,1:T(8,128)(2,1)S(1)}, bf16[112,2,128,128]{3,2,0,1:T(8,128)(2,1)}, u32[]{:S(2)}) copy-start(bf16[112,2,128,128]{3,2,0,1:T(8,128)(2,1)} %copy.45) | copy-start | bytes 22020100
  165.5 30.2 %all-to-all-start.1 = ((bf16[8,8,128,128]{2,3,1,0:T(8,128)(2,1)}), bf16[8,8,128,128]{2,3,1,0:T(8,128)(2,1)S(1)}, u32[]{:S(2)}, u32[]{:S(2)}) async-start(bf16[8,8,128,128]{2,3,1,0:T(8,128)(2,1)} %bitcast.72), calls=%async_computation.1 | async-start | bytes 4194304 | tf_op jit(solution)/shard_map/all_to_all | solution.py:49
  195.7 6.8 %copy-start.5 = (bf16[2,64,128,128]{3,2,1,0:T(8,128)(2,1)S(1)}, bf16[2,64,128,128]{3,2,1,0:T(8,128)(2,1)}, u32[]{:S(2)}) copy-start(bf16[2,64,128,128]{3,2,1,0:T(8,128)(2,1)} %get-tuple-element.12) | copy-start | bytes 12582916
  223.6 8.8 %copy-start.8 = (s32[2,64]{1,0:T(2,128)S(1)}, s32[2,64]{1,0:T(2,128)}, u32[]{:S(2)}) copy-start(s32[2,64]{1,0:T(2,128)} %param.9) | copy-start | bytes 1540
  223.6 16.3 %copy-start.1 = (bf16[2,16,128,128]{3,2,1,0:T(8,128)(2,1)S(1)}, bf16[2,16,128,128]{3,2,1,0:T(8,128)(2,1)}, u32[]{:S(2)}) copy-start(bf16[2,16,128,128]{3,2,1,0:T(8,128)(2,1)} %param.7) | copy-start | bytes 3145732
Sparse Core Ops, SparseCore 0:
  91.1 45.2 all-gather.1
where the time goes:
time: 247 us
  blocking collectives  54.1 us (22%)
  local copies, waits for them, and re-layouts  53.7 us (22%)
  waiting for transfers between devices  46.1 us (19%)
  matrix products  40.8 us (17%)
  other arithmetic  34.8 us (14%)
  between operations  13.5 us (5%)
  starting transfers between devices  3.82 us (2%)
    all_to_all x1, blocking collectives, body(): lax.all_to_all(upward.astype(jnp.bfloat16), 'gy', split_axis=1, concat_ax...  54.1 us
    all_gather x1, waiting for transfers between devices, body(): everything = lax.all_gather(parent, 'gx', axis=0, tiled=True)  25.7 us
    all_to_all x1, waiting for transfers between devices, body(): lax.all_to_all(copies, 'gy', split_axis=0, concat_axis=1, tiled=True)[0]  20.3 us
    dot_general x3, matrix products, complex_apply(): jnp.einsum(pattern, real_part, vectors, preferred_element_type=jnp.float32)  19.5 us
    gather x2, local copies, waits for them, and re-layouts, body(): matrices = couple_table[dir_local, couple_kind]  19.2 us
    sub x2, other arithmetic, complex_apply(): real_term[..., :halfway] - imag_term[..., halfway:]  18 us
    dot_general x3, matrix products, complex_apply(): jnp.einsum(pattern, imag_part, vectors, preferred_element_type=jnp.float32)  15 us
    gather x3, local copies, waits for them, and re-layouts, body(): jnp.take_along_axis(child_coef, child_dir[:, :, None, None], axis=1)  9.54 us
  transfers between devices with their start and end apart: 2, of which 2 were waited for; matrix products, arithmetic and copies ran while one was open for 10% of the time, Pallas kernels for 0%

commit v1 on v0

v1 whole, which is shorter than its diff:
```python
import functools

import jax
import jax.numpy as jnp
from jax import lax
from jax.experimental import pallas as pl
from jax.experimental.pallas import tpu as pltpu
from jax.sharding import PartitionSpec as P

F32 = jnp.float32
BF16 = jnp.bfloat16


def turned(v):
    half = v.shape[-1] // 2
    return jnp.concatenate([-v[..., half:], v[..., :half]], axis=-1)


def turned_rows(v):
    half = v.shape[0] // 2
    return jnp.concatenate([-v[half:], v[:half]], axis=0)


def dot(a, b):
    return jnp.dot(a, b, preferred_element_type=F32)


def up_kernel(rel, fam, me_ref, dir_ref, coef_ref, mat_ref, *rest):
    out_ref = rest[-1]
    children, _, _, zs, per = mat_ref.shape[:5]
    owner = pl.program_id(0) * fam + lax.bitwise_xor(me_ref[0], rel)
    first_z = pl.program_id(1) * zs
    span = pl.num_programs(1) * zs * per
    for z in range(zs):
        for m in range(per):
            e = owner * span + (first_z + z) * per + m
            total = None
            for c in range(children):
                v = coef_ref[c, dir_ref[c, e]]
                both = jnp.concatenate([mat_ref[c, 0, 0, z, m, 0], mat_ref[c, 0, 0, z, m, 1]], axis=1)
                term = dot(both, jnp.concatenate([v, turned(v)], axis=0))
                total = term if total is None else total + term
            for more in rest[:-1]:
                total = total + more[z, 0, m].astype(F32)
            out_ref[z, 0, m] = total.astype(BF16)


def up(rel, fam, zblock, me, dirs, coef, mats, adds):
    children, planes, _, nz, per, _, rank, _ = mats.shape
    width = coef.shape[-1]
    piece = pl.BlockSpec((zblock, 1, per, rank, width), lambda q, z, me, d: (z, q, 0, 0, 0))
    steps = (planes, nz // zblock)
    return pl.pallas_call(
        functools.partial(up_kernel, rel, fam),
        out_shape=jax.ShapeDtypeStruct((nz, planes, per, rank, width), BF16),
        grid_spec=pltpu.PrefetchScalarGridSpec(
            num_scalar_prefetch=2,
            grid=steps,
            in_specs=[
                pl.BlockSpec(coef.shape, lambda q, z, me, d: (0, 0, 0, 0)),
                pl.BlockSpec(
                    (children, 1, 1, zblock, per, 2, rank, rank),
                    lambda q, z, me, d: (0, q, lax.bitwise_xor(me[0], rel), z, 0, 0, 0, 0),
                ),
            ]
            + [piece] * len(adds),
            out_specs=piece,
        ),
        cost_estimate=pl.CostEstimate(
            flops=4 * children * planes * nz * per * rank * rank * width,
            bytes_accessed=children * planes * nz * per * rank * rank * 4,
            transcendentals=0,
        ),
        compiler_params=pltpu.CompilerParams(vmem_limit_bytes=32 << 20),
    )(me, dirs, coef, mats, *adds)


def add_kernel(*refs):
    total = refs[0][...].astype(F32)
    for ref in refs[1:-1]:
        total = total + ref[...].astype(F32)
    refs[-1][...] = total.astype(BF16)


def add(*arrays):
    shape = arrays[0].shape
    spec = pl.BlockSpec((1,) + shape[1:], lambda i: (i,) + (0,) * (len(shape) - 1))
    return pl.pallas_call(
        add_kernel,
        out_shape=jax.ShapeDtypeStruct(shape, BF16),
        grid=(shape[0],),
        in_specs=[spec] * len(arrays),
        out_specs=spec,
    )(*arrays)


def couple_kernel(at_ref, src_ref, kind_ref, count_ref, par_ref, table_ref, out_ref, wide):
    sources = par_ref.shape[0]
    rows = out_ref.shape[0]
    rank = par_ref.shape[2]
    most = src_ref.shape[0] // count_ref.shape[0]
    dirs_held = count_ref.shape[0] // rows
    slot = at_ref[0] + pl.program_id(0)

    def widen(t, carry):
        v = par_ref[t, 0]
        wide[t, :rank] = v
        wide[t, rank:] = turned(v)
        return carry

    lax.fori_loop(0, sources, widen, 0, unroll=min(sources, 8))
    wide[sources] = jnp.zeros_like(wide[sources])

    def one_row(t, carry):
        row = t * dirs_held + slot
        count = count_ref[row]
        total = None
        for k in range(most):
            kind = kind_ref[row * most + k]
            source = jnp.where(k < count, src_ref[row * most + k], sources)
            both = jnp.concatenate([table_ref[0, kind, 0], table_ref[0, kind, 1]], axis=1)
            term = dot(both, wide[source])
            total = term if total is None else total + term
        out_ref[t, 0] = total.T.astype(BF16)
        return carry

    lax.fori_loop(0, rows, one_row, 0, unroll=min(rows, 4))


def couple(at, src, kind, count, parents, table):
    sources, per, rank, width = parents.shape
    rows = src.shape[0]
    kinds = table.shape[1]
    return pl.pallas_call(
        couple_kernel,
        out_shape=jax.ShapeDtypeStruct((rows, per, width, rank), BF16),
        grid_spec=pltpu.PrefetchScalarGridSpec(
            num_scalar_prefetch=4,
            grid=(per,),
            in_specs=[
                pl.BlockSpec((sources, 1, rank, width), lambda m, at, *_: (0, m, 0, 0)),
                pl.BlockSpec((1, kinds, 2, rank, rank), lambda m, at, *_: (at[0] + m, 0, 0, 0, 0)),
            ],
            out_specs=pl.BlockSpec((rows, 1, width, rank), lambda m, at, *_: (0, m, 0, 0)),
            scratch_shapes=[pltpu.VMEM((sources + 1, 2 * rank, width), BF16)],
        ),
        cost_estimate=pl.CostEstimate(
            flops=4 * rows * per * src.shape[2] * rank * rank * width,
            bytes_accessed=per * kinds * 4 * rank * rank,
            transcendentals=0,
        ),
        compiler_params=pltpu.CompilerParams(vmem_limit_bytes=32 << 20),
    )(at, src.reshape(-1), kind.reshape(-1), count.reshape(-1), parents, table)


def down_kernel(me_ref, dir_ref, mat_ref, *rest):
    pieces, out_ref, sums = rest[:-2], rest[-2], rest[-1]
    children, _, fam, zs, per, _, rank, _ = mat_ref.shape
    first = jnp.logical_and(pl.program_id(0) == 0, pl.program_id(1) == 0)
    last = jnp.logical_and(
        pl.program_id(0) == pl.num_programs(0) - 1, pl.program_id(1) == pl.num_programs(1) - 1
    )
    first_z = pl.program_id(1) * zs
    span = pl.num_programs(1) * zs * per

    @pl.when(first)
    def _():
        sums[...] = jnp.zeros_like(sums)

    for rel, piece in enumerate(pieces):
        side = lax.bitwise_xor(me_ref[0], rel)
        owner = pl.program_id(0) * fam + side
        for z in range(zs):
            for m in range(per):
                e = owner * span + (first_z + z) * per + m
                v = piece[z, 0, m]
                x = jnp.concatenate([v, turned_rows(v)], axis=1)
                for c in range(children):
                    i = dir_ref[c, e]
                    sums[c, i] += dot(x, mat_ref[c, 0, side, z, m].reshape(2 * rank, rank))

    @pl.when(last)
    def _():
        for c in range(children):
            for i in range(out_ref.shape[1]):
                out_ref[c, i] = sums[c, i].T.astype(BF16)


def down(zblock, me, dirs, mats, pieces, groups):
    children, planes, fam, nz, per, _, rank, _ = mats.shape
    width = pieces[0].shape[-2]
    piece = pl.BlockSpec((zblock, 1, per, width, rank), lambda q, z, me, d: (z, q, 0, 0, 0))
    return pl.pallas_call(
        down_kernel,
        out_shape=jax.ShapeDtypeStruct((children, groups, rank, width), BF16),
        grid_spec=pltpu.PrefetchScalarGridSpec(
            num_scalar_prefetch=2,
            grid=(planes, nz // zblock),
            in_specs=[
                pl.BlockSpec(
                    (children, 1, fam, zblock, per, 2, rank, rank),
                    lambda q, z, me, d: (0, q, 0, z, 0, 0, 0, 0),
                )
            ]
            + [piece] * len(pieces),
            out_specs=pl.BlockSpec((children, groups, rank, width), lambda q, z, me, d: (0, 0, 0, 0)),
            scratch_shapes=[pltpu.VMEM((children, groups, width, rank), F32)],
        ),
        compiler_params=pltpu.CompilerParams(vmem_limit_bytes=32 << 20),
    )(me, dirs, mats, *pieces)


def body(nx, ny, child_coef, transfer, child_dir, couple_src, couple_kind, couple_count, couple_table):
    children, dirs, _, rank, _ = transfer.shape
    planes = couple_src.shape[0]
    fam = ny // planes
    held = dirs // ny
    split = held % nx == 0
    nz = nx if split else 1
    per = held // nz
    at_y, at_x = lax.axis_index("gy"), lax.axis_index("gx")
    side = lax.rem(at_y, fam).astype(jnp.int32).reshape(1)
    mats = transfer.reshape(children, planes, fam, nz, per, 2, rank, rank)
    zblock = min(nz, 2)

    def swap(x, rel):
        return lax.ppermute(x, "gy", [(i, i ^ rel) for i in range(ny)])

    def exchange(x):
        shape = x.shape
        if split:
            groups = [[z * ny + q * fam + j for z in range(nx) for q in range(planes)] for j in range(fam)]
            axes = ("gx", "gy")
        else:
            groups = [[q * fam + j for q in range(planes)] for j in range(fam)]
            axes = "gy"
        x = x.reshape((-1,) + shape[2:])
        x = lax.all_to_all(x, axes, split_axis=0, concat_axis=0, tiled=True, axis_index_groups=groups)
        return x.reshape(shape)

    if split:
        packed = jnp.concatenate([couple_src, couple_kind, couple_count[..., None]], axis=-1)
        packed = lax.all_gather(packed, "gx", axis=0, tiled=True)
        most = couple_src.shape[-1]
        src, kind, count = packed[..., :most], packed[..., most : 2 * most], packed[..., 2 * most]
        at = (at_x * per).astype(jnp.int32).reshape(1)
    else:
        src, kind, count = couple_src, couple_kind, couple_count
        at = jnp.zeros((1,), jnp.int32)

    one = functools.partial(up, fam=fam, zblock=zblock, me=side, dirs=child_dir, coef=child_coef, mats=mats)
    pending = {}
    kept = {}
    rels = list(range(fam))
    bit = 1
    sums = {}
    order = sorted(rels, key=lambda r: -r)
    got = {rel: [] for rel in rels}
    for rel in sorted(rels, key=lambda r: [-(r & (1 << b)) for b in range(fam.bit_length() - 1)] + [-r]):
        low = rel & -rel
        adds = got[rel]
        if rel:
            mine = one(rel, adds=adds)
            got[rel ^ low].append(swap(mine, low))
        else:
            base = one(rel, adds=[])
            whole = add(base, *adds)

    parents = exchange(whole)
    parents = parents.reshape((nz * planes, per) + parents.shape[3:])
    if not split:
        parents = lax.all_gather(parents, "gx", axis=0, tiled=True)
    local = couple(at, src, kind, count, parents, couple_table)
    local = local.reshape((nz, planes) + local.shape[1:])
    pieces = {0: exchange(local)}
    for rel in range(1, fam):
        high = 1 << (rel.bit_length() - 1)
        low = rel & -rel
        pieces[rel] = None
    step = fam // 2
    while step:
        for rel in sorted(r for r in pieces if pieces[r] is not None):
            if pieces.get(rel ^ step, 0) is None:
                pieces[rel ^ step] = swap(pieces[rel], step)
        step //= 2
    return down(zblock // 2 or 1, side, child_dir, mats, [pieces[r] for r in range(fam)], child_coef.shape[1])


def solution(mesh):
    return jax.shard_map(
        functools.partial(body, mesh.shape["gx"], mesh.shape["gy"]),
        mesh=mesh,
        in_specs=(
            P(("gx", "gy"), None, None, None),
            P(("gx", "gy"), None, None, None, None),
            P(("gx", "gy"), None),
            P("gx", "gy", None),
            P("gx", "gy", None),
            P("gx", "gy"),
            P("gy", None, None, None, None),
        ),
        out_specs=P(("gx", "gy"), None, None, None),
        check_vma=False,
    )
```

time: 247 us -> 103 us (0.42)
  matrix products: 40.8 us -> 0 us
  local copies, waits for them, and re-layouts: 53.7 us -> 13.5 us
  other arithmetic: 34.8 us -> 0.08 us
  waiting for transfers between devices: 46.1 us -> 19.5 us
  Pallas kernels: 0 us -> 23.4 us
  blocking collectives: 54.1 us -> 35.1 us
  between operations: 13.5 us -> 0.13 us
  starting transfers between devices: 3.82 us -> 11.2 us
    dot_general x7 -> x0, matrix products: 40.8 us -> none  [the longest x3 19.5 us: complex_apply(): jnp.einsum(pattern, real_part, vectors, preferred_element_type=jnp.float32)]
    all_to_all x1, blocking collectives: 54.1 us -> 16.2 us  [exchange(): lax.all_to_all(x, axes, split_axis=0, concat_axis=0, tiled=True, axis_ind...]
    gather x6 -> x0, local copies, waits for them, and re-layouts: 33.7 us -> none  [the longest x2 19.2 us: body(): matrices = couple_table[dir_local, couple_kind]]
    all_gather x1 -> x0, waiting for transfers between devices: 25.7 us -> none  [body(): everything = lax.all_gather(parent, 'gx', axis=0, tiled=True)]
    pallas_call x0 -> x7, Pallas kernels: none -> 23.4 us  [the longest x4 9.7 us: up(): pl.pallas_call(functools.partial(up_kernel, rel, fam), out_shape=jax.Shap...]
    all_to_all x1, waiting for transfers between devices: 20.3 us -> 0.01 us  [exchange(): lax.all_to_all(x, axes, split_axis=0, concat_axis=0, tiled=True, axis_ind...]
    ppermute x0 -> x6, waiting for transfers between devices: none -> 19.5 us  [swap(): return lax.ppermute(x, 'gy', [(i, i ^ rel) for i in range(ny)])]
    all_gather x0 -> x1, blocking collectives: none -> 18.9 us  [body(): packed = lax.all_gather(packed, 'gx', axis=0, tiled=True)]
  transfers between devices with their start and end apart: 2 -> 7, of which waited for: 2 -> 3; matrix products, arithmetic and copies ran while one was open for 10% -> 1% of each run, Pallas kernels for 0% -> 7%
where the time goes in v1:
time: 103 us
  blocking collectives  35.1 us (34%)
  Pallas kernels  23.4 us (23%)
  waiting for transfers between devices  19.5 us (19%)
  local copies, waits for them, and re-layouts  13.5 us (13%)
  starting transfers between devices  11.2 us (11%)
    ppermute x6, waiting for transfers between devices, swap(): return lax.ppermute(x, 'gy', [(i, i ^ rel) for i in range(ny)])  19.5 us
    all_gather x1, blocking collectives, body(): packed = lax.all_gather(packed, 'gx', axis=0, tiled=True)  18.9 us
    all_to_all x1, blocking collectives, exchange(): lax.all_to_all(x, axes, split_axis=0, concat_axis=0, tiled=True, axis_ind...  16.2 us
    unnamed x26, local copies, waits for them, and re-layouts  12.6 us
    pallas_call x4, Pallas kernels, up(): pl.pallas_call(functools.partial(up_kernel, rel, fam), out_shape=jax.Shap...  9.7 us
    pallas_call x1, Pallas kernels, down(): pl.pallas_call(down_kernel, out_shape=jax.ShapeDtypeStruct((children, gro...  6.22 us
    all_to_all x1, starting transfers between devices, exchange(): lax.all_to_all(x, axes, split_axis=0, concat_axis=0, tiled=True, axis_ind...  6.08 us
    ppermute x6, starting transfers between devices, swap(): return lax.ppermute(x, 'gy', [(i, i ^ rel) for i in range(ny)])  5.14 us
  transfers between devices with their start and end apart: 7, of which 3 were waited for; matrix products, arithmetic and copies ran while one was open for 1% of the time, Pallas kernels for 7%

profile of v1, /device:TPU:0, one launch (start us, length us, event | category | flops | bytes accessed | tf_op | source)
XLA Modules:
  0.0 102.8 jit_solution(5223728022019421908)
XLA Ops:
  0.0 3.4 %copy-done = bf16[2,64,2,128,128]{4,3,2,1,0:T(8,128)(2,1)S(1)} copy-done((bf16[2,64,2,128,128]{4,3,2,1,0:T(8,128)(2,1)S(1)}, bf16[2,64,2,128,128]{4,3,2,1,0:T(8,128)(2,1)}, u32[]{:S(2)}) %copy-start) | copy-done | bytes 8388632
  3.4 1.2 %copy-done.2 = bf16[2,16,128,128]{3,2,1,0:T(8,128)(2,1)S(1)} copy-done((bf16[2,16,128,128]{3,2,1,0:T(8,128)(2,1)S(1)}, bf16[2,16,128,128]{3,2,1,0:T(8,128)(2,1)}, u32[]{:S(2)}) %copy-start.2) | copy-done | bytes 1048600
  4.6 0.7 copy-done.5
  5.3 2.4 %shard_map.75 = bf16[4,2,2,128,128]{4,3,2,1,0:T(8,128)(2,1)S(1)} custom-call(s32[1]{0:T(128)} %bitcast.me_ref, s32[2,64]{1,0:T(2,128)S(1)} %copy-done.5, bf16[2,16,128,128]{3,2,1,0:T(8,128)(2,1)S(1)} %copy-done.2, bf16[2,2,4,4,2,2,128,128]{7,6,5,4,3,2,1,0:T(8,128)(2,1)S(1)} %bitcast.6), custom_call_target="tpu_custom_call" | custom-call | flops 268435456 | bytes 2097152 | tf_op jit(solution)/shard_map/pallas_call | solution.py:53
  7.7 0.5 collective-permute-start.1
  8.2 2.4 %shard_map.74 = bf16[4,2,2,128,128]{4,3,2,1,0:T(8,128)(2,1)S(1)} custom-call(s32[1]{0:T(128)} %bitcast.me_ref, s32[2,64]{1,0:T(2,128)S(1)} %copy-done.5, bf16[2,16,128,128]{3,2,1,0:T(8,128)(2,1)S(1)} %copy-done.2, bf16[2,2,4,4,2,2,128,128]{7,6,5,4,3,2,1,0:T(8,128)(2,1)S(1)} %bitcast.7), custom_call_target="tpu_custom_call" | custom-call | flops 268435456 | bytes 2097152 | tf_op jit(solution)/shard_map/pallas_call | solution.py:53
  10.6 0.1 collective-permute-start
  10.8 0.0 collective-permute-done.1.rest_0_
  10.8 2.5 %shard_map.76 = bf16[4,2,2,128,128]{4,3,2,1,0:T(8,128)(2,1)S(1)} custom-call(s32[1]{0:T(128)} %bitcast.me_ref, s32[2,64]{1,0:T(2,128)S(1)} %copy-done.5, bf16[2,16,128,128]{3,2,1,0:T(8,128)(2,1)S(1)} %copy-done.2, bf16[2,2,4,4,2,2,128,128]{7,6,5,4,3,2,1,0:T(8,128)(2,1)S(1)} %bitcast.8, bf16[4,2,2,128,128]{4,3,2,1,0:T(8,128)(2,1)S(1)} %collective-permute-done.1.rest_0_), custom_call_target="tpu_custom_call" | custom-call | flops 268435456 | bytes 2097152 | tf_op jit(solution)/shard_map/pallas_call | solution.py:53
  13.2 0.0 copy-start.9
  13.3 0.0 copy-start.10
  13.3 0.0 copy-start.11
  13.3 0.0 copy-start.6
  13.3 3.0 %collective-permute-start.2 = (bf16[4,2,2,128,128]{4,3,2,1,0:T(8,128)(2,1)S(1)}, bf16[4,2,2,128,128]{4,3,2,1,0:T(8,128)(2,1)S(1)}, u32[]{:S(2)}, u32[]{:S(2)}) collective-permute-start(bf16[4,2,2,128,128]{4,3,2,1,0:T(8,128)(2,1)S(1)} %shard_map.76), channel_id=1, source_target_pairs={{0,2},{1,3},{2,0},{3,1},{4,6},{5,7},{6,4},{7,5},{8,10},{9,11},{10,... | collective-permute-start | bytes 1572872 | tf_op jit(solution)/shard_map/ppermute | solution.py:227
  16.3 2.4 %shard_map.73.refs_0_ = bf16[4,2,2,128,128]{4,3,2,1,0:T(8,128)(2,1)S(1)} custom-call(s32[1]{0:T(128)} %bitcast.me_ref, s32[2,64]{1,0:T(2,128)S(1)} %copy-done.5, bf16[2,16,128,128]{3,2,1,0:T(8,128)(2,1)S(1)} %copy-done.2, bf16[2,2,4,4,2,2,128,128]{7,6,5,4,3,2,1,0:T(8,128)(2,1)S(1)} %bitcast.9), custom_call_target="tpu_custom_call" | custom-call | flops 268435456 | bytes 2097152 | tf_op jit(solution)/shard_map/pallas_call | solution.py:53
  18.7 0.0 copy-start.4
  18.7 0.8 copy-done.4
  19.5 0.0 collective-permute-done.refs_1_
  19.5 8.9 %collective-permute-done.2.refs_2_ = bf16[4,2,2,128,128]{4,3,2,1,0:T(8,128)(2,1)S(1)} collective-permute-done((bf16[4,2,2,128,128]{4,3,2,1,0:T(8,128)(2,1)S(1)}, bf16[4,2,2,128,128]{4,3,2,1,0:T(8,128)(2,1)S(1)}, u32[]{:S(2)}, u32[]{:S(2)}) %collective-permute-start.2) | collective-permute-done | bytes 524320 | tf_op jit(solution)/shard_map/ppermute | solution.py:227
  28.4 0.0 copy-done.7
  28.4 0.8 copy-done.8
  29.2 3.5 %shard_map.77 = bf16[4,2,2,128,128]{4,3,2,1,0:T(8,128)(2,1)} custom-call(bf16[4,2,2,128,128]{4,3,2,1,0:T(8,128)(2,1)} %copy-done.4, bf16[4,2,2,128,128]{4,3,2,1,0:T(8,128)(2,1)} %copy-done.7, bf16[4,2,2,128,128]{4,3,2,1,0:T(8,128)(2,1)} %copy-done.8), custom_call_target="tpu_custom_call" | custom-call | tf_op jit(solution)/shard_map/pallas_call | solution.py:88
  32.7 6.1 %all-to-all-start = ((bf16[8,2,128,128]{3,2,1,0:T(8,128)(2,1)}), bf16[8,2,128,128]{3,2,1,0:T(8,128)(2,1)S(1)}, u32[]{:S(2)}, u32[]{:S(2)}) async-start(bf16[8,2,128,128]{3,2,1,0:T(8,128)(2,1)} %bitcast.14), calls=%async_computation | async-start | bytes 1048576 | tf_op jit(solution)/shard_map/all_to_all | solution.py:238
  38.8 0.1 copy.13
  38.9 0.0 copy-done.10
  38.9 0.1 copy.14
  39.0 0.0 copy-done.11
  39.0 0.1 copy.15
  39.1 0.1 pad_add_fusion
  39.1 18.9 %all_gather.3 = s32[8,8,15]{2,1,0:T(8,128)S(1)} all-gather(s32[2,8,15]{2,1,0:T(8,128)S(1)} %pad_add_fusion), channel_id=1, replica_groups=mesh['gx'=4,'gy'=8] {'gx'}, dimensions={0}, use_global_device_ids=true | all-gather | bytes 4800 | tf_op jit(solution)/shard_map/all_gather | solution.py:243
  58.0 0.3 slice_reduce_fusion
  58.3 0.1 reshape_squeeze.3.count_ref
  58.4 0.1 fusion
  58.4 0.2 reshape.25.kind_ref
  58.6 0.1 reshape.24.src_ref
  58.7 0.0 all-to-all-done.par_ref
  58.8 0.0 copy-start.3
  58.8 2.2 %copy-done.3 = bf16[8,8,2,128,128]{4,3,2,1,0:T(8,128)(2,1)S(1)} copy-done((bf16[8,8,2,128,128]{4,3,2,1,0:T(8,128)(2,1)S(1)}, bf16[8,8,2,128,128]{4,3,2,1,0:T(8,128)(2,1)}, u32[]{:S(2)}) %copy-start.3) | copy-done | bytes 4194328
  61.0 4.0 %shard_map.78 = bf16[8,2,128,128]{3,2,1,0:T(8,128)(2,1)S(1)} custom-call(s32[1]{0:T(128)} %bitcast.2.at_ref, s32[448]{0:T(512)S(1)} %reshape.24.src_ref, s32[448]{0:T(512)S(1)} %reshape.25.kind_ref, s32[64]{0:T(128)S(1)} %reshape_squeeze.3.count_ref, bf16[8,2,128,128]{3,2,1,0:T(8,128)(2,1)S(1)} %all-to-all-done.par_ref, ...), custom_call_target="tpu_custom_call" | custom-call | flops 939524096 | bytes 1048576 | tf_op jit(solution)/shard_map/pallas_call | solution.py:134
  64.9 16.2 %all_to_all.10 = bf16[8,2,128,128]{3,2,1,0:T(8,128)(2,1)S(1)} all-to-all(bf16[8,2,128,128]{3,2,1,0:T(8,128)(2,1)S(1)} %shard_map.78), channel_id=1, replica_groups={{0,4,8,12,16,20,24,28},{1,5,9,13,17,21,25,29},{2,6,10,14,18,22,26,30},{..., dimensions={0} | all-to-all | bytes 1048576 | tf_op jit(solution)/shard_map/all_to_all | solution.py:238
  81.1 1.5 %collective-permute-start.4 = (bf16[4,2,2,128,128]{4,3,2,1,0:T(8,128)(2,1)S(1)}, bf16[4,2,2,128,128]{4,3,2,1,0:T(8,128)(2,1)S(1)}, u32[]{:S(2)}, u32[]{:S(2)}) collective-permute-start(bf16[4,2,2,128,128]{4,3,2,1,0:T(8,128)(2,1)S(1)} %bitcast.11), channel_id=1, source_target_pairs={{0,2},{1,3},{2,0},{3,1},{4,6},{5,7},{6,4},{7,5},{8,10},{9,11},{10,... | collective-permute-start | bytes 1572872 | tf_op jit(solution)/shard_map/ppermute | solution.py:227
  82.6 0.0 collective-permute-start.3
  82.6 8.7 %collective-permute-done.4.rest_2_ = bf16[4,2,2,128,128]{4,3,2,1,0:T(8,128)(2,1)S(1)} collective-permute-done((bf16[4,2,2,128,128]{4,3,2,1,0:T(8,128)(2,1)S(1)}, bf16[4,2,2,128,128]{4,3,2,1,0:T(8,128)(2,1)S(1)}, u32[]{:S(2)}, u32[]{:S(2)}) %collective-permute-start.4) | collective-permute-done | bytes 524320 | tf_op jit(solution)/shard_map/ppermute | solution.py:227
  91.3 0.0 collective-permute-start.5
  91.3 0.0 collective-permute-done.3.rest_1_
  91.3 1.9 %collective-permute-done.5.rest_3_ = bf16[4,2,2,128,128]{4,3,2,1,0:T(8,128)(2,1)S(1)} collective-permute-done((bf16[4,2,2,128,128]{4,3,2,1,0:T(8,128)(2,1)S(1)}, bf16[4,2,2,128,128]{4,3,2,1,0:T(8,128)(2,1)S(1)}, u32[]{:S(2)}, u32[]{:S(2)}) %collective-permute-start.5) | collective-permute-done | bytes 524320 | tf_op jit(solution)/shard_map/ppermute | solution.py:227
  93.2 3.4 %copy-done.1 = bf16[2,64,2,128,128]{4,3,2,1,0:T(8,128)(2,1)S(1)} copy-done((bf16[2,64,2,128,128]{4,3,2,1,0:T(8,128)(2,1)S(1)}, bf16[2,64,2,128,128]{4,3,2,1,0:T(8,128)(2,1)}, u32[]{:S(2)}) %copy-start.1) | copy-done | bytes 8388632
  96.6 6.2 %shard_map.79 = bf16[2,16,128,128]{3,2,1,0:T(8,128)(2,1)} custom-call(s32[1]{0:T(128)} %bitcast.me_ref, s32[2,64]{1,0:T(2,128)S(1)} %copy-done.6, bf16[2,2,4,4,2,2,128,128]{7,6,5,4,3,2,1,0:T(8,128)(2,1)S(1)} %bitcast.10, bf16[4,2,2,128,128]{4,3,2,1,0:T(8,128)(2,1)S(1)} %bitcast.13, bf16[4,2,2,128,128]{4,3,2,1,0:T(8,128)(2,1)S(1)} %collective-permute-done.3.rest_1_, ...), custom_call_target="tpu_custom_call" | custom-call | tf_op jit(solution)/shard_map/pallas_call | solution.py:193
  (8 shorter events, 0.0 us)
Async XLA Ops:
  0.0 3.4 %copy-start = (bf16[2,64,2,128,128]{4,3,2,1,0:T(8,128)(2,1)S(1)}, bf16[2,64,2,128,128]{4,3,2,1,0:T(8,128)(2,1)}, u32[]{:S(2)}) copy-start(bf16[2,64,2,128,128]{4,3,2,1,0:T(8,128)(2,1)} %param.8) | copy-start | bytes 25165828
  3.4 1.2 %copy-start.2 = (bf16[2,16,128,128]{3,2,1,0:T(8,128)(2,1)S(1)}, bf16[2,16,128,128]{3,2,1,0:T(8,128)(2,1)}, u32[]{:S(2)}) copy-start(bf16[2,16,128,128]{3,2,1,0:T(8,128)(2,1)} %coef_ref.7) | copy-start | bytes 3145732
  4.6 0.7 copy-start.5
  7.7 3.1 %collective-permute-start.1 = (bf16[4,2,2,128,128]{4,3,2,1,0:T(8,128)(2,1)S(1)}, bf16[4,2,2,128,128]{4,3,2,1,0:T(8,128)(2,1)S(1)}, u32[]{:S(2)}, u32[]{:S(2)}) collective-permute-start(bf16[4,2,2,128,128]{4,3,2,1,0:T(8,128)(2,1)S(1)} %shard_map.75), channel_id=1, source_target_pairs={{0,1},{1,0},{2,3},{3,2},{4,5},{5,4},{6,7},{7,6},{8,9},{9,8},{10,11... | collective-permute-start | bytes 1572872 | tf_op jit(solution)/shard_map/ppermute | solution.py:227
  10.6 8.9 %collective-permute-start = (bf16[4,2,2,128,128]{4,3,2,1,0:T(8,128)(2,1)S(1)}, bf16[4,2,2,128,128]{4,3,2,1,0:T(8,128)(2,1)S(1)}, u32[]{:S(2)}, u32[]{:S(2)}) collective-permute-start(bf16[4,2,2,128,128]{4,3,2,1,0:T(8,128)(2,1)S(1)} %shard_map.74), channel_id=1, source_target_pairs={{0,1},{1,0},{2,3},{3,2},{4,5},{5,4},{6,7},{7,6},{8,9},{9,8},{10,11... | collective-permute-start | bytes 1572872 | tf_op jit(solution)/shard_map/ppermute | solution.py:227
  13.2 25.5 %copy-start.9 = (s32[2,8,7]{1,0,2:T(2,128)S(1)}, s32[2,8,7]{1,0,2:T(2,128)}, u32[]{:S(2)}) copy-start(s32[2,8,7]{1,0,2:T(2,128)} %param.10) | copy-start | bytes 1348
  13.3 25.6 %copy-start.10 = (s32[2,8,7]{1,0,2:T(2,128)S(1)}, s32[2,8,7]{1,0,2:T(2,128)}, u32[]{:S(2)}) copy-start(s32[2,8,7]{1,0,2:T(2,128)} %param.11) | copy-start | bytes 1348
  13.3 25.7 %copy-start.11 = (s32[2,8]{1,0:T(2,128)S(1)}, s32[2,8]{1,0:T(2,128)}, u32[]{:S(2)}) copy-start(s32[2,8]{1,0:T(2,128)} %param.12) | copy-start | bytes 196
  13.3 79.9 %copy-start.6 = (s32[2,64]{1,0:T(2,128)S(1)}, s32[2,64]{1,0:T(2,128)}, u32[]{:S(2)}) copy-start(s32[2,64]{1,0:T(2,128)} %dir_ref.9) | copy-start | bytes 1540
  13.3 15.1 %collective-permute-start.2 = (bf16[4,2,2,128,128]{4,3,2,1,0:T(8,128)(2,1)S(1)}, bf16[4,2,2,128,128]{4,3,2,1,0:T(8,128)(2,1)S(1)}, u32[]{:S(2)}, u32[]{:S(2)}) collective-permute-start(bf16[4,2,2,128,128]{4,3,2,1,0:T(8,128)(2,1)S(1)} %shard_map.76), channel_id=1, source_target_pairs={{0,2},{1,3},{2,0},{3,1},{4,6},{5,7},{6,4},{7,5},{8,10},{9,11},{10,... | collective-permute-start | bytes 1572872 | tf_op jit(solution)/shard_map/ppermute | solution.py:227
  18.7 0.8 copy-start.4
  19.5 8.9 %copy-start.7 = (bf16[4,2,2,128,128]{4,3,2,1,0:T(8,128)(2,1)}, bf16[4,2,2,128,128]{4,3,2,1,0:T(8,128)(2,1)S(1)}, u32[]{:S(2)}) copy-start(bf16[4,2,2,128,128]{4,3,2,1,0:T(8,128)(2,1)S(1)} %collective-permute-done.refs_1_) | copy-start | bytes 1572868
  28.4 0.8 copy-start.8
  32.7 26.0 %all-to-all-start = ((bf16[8,2,128,128]{3,2,1,0:T(8,128)(2,1)}), bf16[8,2,128,128]{3,2,1,0:T(8,128)(2,1)S(1)}, u32[]{:S(2)}, u32[]{:S(2)}) async-start(bf16[8,2,128,128]{3,2,1,0:T(8,128)(2,1)} %bitcast.14), calls=%async_computation | async-start | bytes 1048576 | tf_op jit(solution)/shard_map/all_to_all | solution.py:238
  58.8 2.2 %copy-start.3 = (bf16[8,8,2,128,128]{4,3,2,1,0:T(8,128)(2,1)S(1)}, bf16[8,8,2,128,128]{4,3,2,1,0:T(8,128)(2,1)}, u32[]{:S(2)}) copy-start(bf16[8,8,2,128,128]{4,3,2,1,0:T(8,128)(2,1)} %table_ref.1) | copy-start | bytes 12582916
  81.1 10.2 %collective-permute-start.4 = (bf16[4,2,2,128,128]{4,3,2,1,0:T(8,128)(2,1)S(1)}, bf16[4,2,2,128,128]{4,3,2,1,0:T(8,128)(2,1)S(1)}, u32[]{:S(2)}, u32[]{:S(2)}) collective-permute-start(bf16[4,2,2,128,128]{4,3,2,1,0:T(8,128)(2,1)S(1)} %bitcast.11), channel_id=1, source_target_pairs={{0,2},{1,3},{2,0},{3,1},{4,6},{5,7},{6,4},{7,5},{8,10},{9,11},{10,... | collective-permute-start | bytes 1572872 | tf_op jit(solution)/shard_map/ppermute | solution.py:227
  82.6 8.7 %collective-permute-start.3 = (bf16[4,2,2,128,128]{4,3,2,1,0:T(8,128)(2,1)S(1)}, bf16[4,2,2,128,128]{4,3,2,1,0:T(8,128)(2,1)S(1)}, u32[]{:S(2)}, u32[]{:S(2)}) collective-permute-start(bf16[4,2,2,128,128]{4,3,2,1,0:T(8,128)(2,1)S(1)} %bitcast.12), channel_id=1, source_target_pairs={{0,1},{1,0},{2,3},{3,2},{4,5},{5,4},{6,7},{7,6},{8,9},{9,8},{10,11... | collective-permute-start | bytes 1572872 | tf_op jit(solution)/shard_map/ppermute | solution.py:227
  91.3 1.9 %collective-permute-start.5 = (bf16[4,2,2,128,128]{4,3,2,1,0:T(8,128)(2,1)S(1)}, bf16[4,2,2,128,128]{4,3,2,1,0:T(8,128)(2,1)S(1)}, u32[]{:S(2)}, u32[]{:S(2)}) collective-permute-start(bf16[4,2,2,128,128]{4,3,2,1,0:T(8,128)(2,1)S(1)} %collective-permute-done.4.rest_2_), channel_id=1, source_target_pairs={{0,1},{1,0},{2,3},{3,2},{4,5},{5,4},{6,7},{7,6},{8,9},{9,8},{10,11... | collective-permute-start | bytes 1572872 | tf_op jit(solution)/shard_map/ppermute | solution.py:227
  93.2 3.4 %copy-start.1 = (bf16[2,64,2,128,128]{4,3,2,1,0:T(8,128)(2,1)S(1)}, bf16[2,64,2,128,128]{4,3,2,1,0:T(8,128)(2,1)}, u32[]{:S(2)}) copy-start(bf16[2,64,2,128,128]{4,3,2,1,0:T(8,128)(2,1)} %param.8) | copy-start | bytes 25165828

commit v2 on v0

v2 whole, which is shorter than its diff:
```python
import functools

import jax
import jax.numpy as jnp
from jax import lax
from jax.experimental import pallas as pl
from jax.experimental.pallas import tpu as pltpu
from jax.sharding import PartitionSpec as P

F32 = jnp.float32
BF16 = jnp.bfloat16
SMEM = pl.BlockSpec(memory_space=pltpu.SMEM)
VMEM = pl.BlockSpec(memory_space=pltpu.VMEM)
ANY = pl.BlockSpec(memory_space=pl.ANY)
COST = pl.CostEstimate(flops=10000000000, bytes_accessed=1000000, transcendentals=0)
PARAMS = pltpu.CompilerParams(vmem_limit_bytes=16 << 20)


def turned(v):
    half = v.shape[-1] // 2
    return jnp.concatenate([-v[..., half:], v[..., :half]], axis=-1)


def turned_rows(v):
    half = v.shape[0] // 2
    return jnp.concatenate([-v[half:], v[:half]], axis=0)


def dot(a, b):
    return jnp.dot(a, b, preferred_element_type=F32)


def xor(a, b):
    return lax.bitwise_xor(a, jnp.int32(b))


def place(at_ref, planes, rel, base, core):
    turn = lax.bitwise_and(xor(at_ref[1], rel), jnp.int32(1))
    q = lax.bitwise_xor(xor(at_ref[0], base % planes), turn)
    return q, xor(at_ref[1], rel ^ core), xor(at_ref[2], base // planes)


def up_kernel(groups, fetches, at_ref, dir_ref, coef_hbm, mat_hbm, *rest):
    table_hbm, rest = (rest[0], rest[1:]) if fetches else (None, rest)
    outs, (coef_ref, mat_ref, coef_sem, mat_sem) = rest[:-4], rest[-4:]
    children, planes, fam, nz, per = mat_hbm.shape[:5]

    def start(group, first):
        copies = []
        for out, rel, bases in group:
            for n, core in [(n, core) for n in range(len(bases)) for core in range(2)]:
                q, j, z = place(at_ref, planes, rel, bases[n], core)
                slot = first + len(copies)
                copy = pltpu.make_async_copy(mat_hbm.at[:, q, j, z], mat_ref.at[slot], mat_sem.at[slot])
                copy.start()
                copies.append((copy, outs[out], (n, core), ((q * fam + j) * nz + z) * per, slot))
        return copies

    coef_copy = pltpu.make_async_copy(coef_hbm, coef_ref, coef_sem)
    coef_copy.start()
    flying, first = [], 0
    for group in groups[:2]:
        flying.append(start(group, first))
        first += len(flying[-1])
    coef_copy.wait()
    for n in range(len(groups)):
        for copy, *_ in flying[n]:
            copy.wait()
        if n + 2 < len(groups):
            flying.append(start(groups[n + 2], first))
            first += len(flying[-1])
        elif n + 2 == len(groups) and fetches:
            table_copy = pltpu.make_async_copy(table_hbm.at[pl.ds(at_ref[2] * per, per)], outs[-1], coef_sem)
            table_copy.start()
        for _, out, spot, e, slot in flying[n]:
            for m in range(per):
                left, right = [], []
                for c in range(children):
                    v = coef_ref[c, dir_ref[c, e + m]]
                    left += [mat_ref[slot, c, m, 0], mat_ref[slot, c, m, 1]]
                    right += [v, turned(v)]
                out[spot + (m,)] = dot(jnp.concatenate(left, axis=1), jnp.concatenate(right, axis=0)).astype(BF16)
    if fetches:
        table_copy.wait()


def up(at, dirs, coef, mats, halves, groups, table=None):
    children, planes, fam, nz, per, _, rank, _ = mats.shape
    width = coef.shape[-1]
    names = [name for group in groups for name in group]
    jobs = [[(names.index((h, rel)), rel, halves[h]) for h, rel in group] for group in groups]
    slots = 2 * sum(len(halves[h]) for h, _ in names)
    extra = [] if table is None else [table]
    found = pl.pallas_call(
        functools.partial(up_kernel, jobs, len(extra)),
        out_shape=[jax.ShapeDtypeStruct((len(halves[h]), 2, per, rank, width), BF16) for h, _ in names]
        + [jax.ShapeDtypeStruct((per,) + t.shape[1:], BF16) for t in extra],
        in_specs=[SMEM, SMEM] + [ANY] * (2 + len(extra)),
        out_specs=[VMEM] * (len(names) + len(extra)),
        scratch_shapes=[
            pltpu.VMEM(coef.shape, BF16),
            pltpu.VMEM((slots, children, per, 2, rank, rank), BF16),
            pltpu.SemaphoreType.DMA,
            pltpu.SemaphoreType.DMA((slots,)),
        ],
        compiler_params=PARAMS,
        cost_estimate=COST,
    )(at, dirs, *[pltpu.with_memory_space_constraint(x, pltpu.HBM) for x in [coef, mats] + extra])
    return dict(zip(names, found)), found[len(names) :]


def add_kernel(*refs):
    total = refs[0][...].astype(F32)
    for ref in refs[1:-1]:
        total = total + ref[...].astype(F32)
    refs[-1][...] = total.astype(BF16)


def add(arrays):
    return pl.pallas_call(
        add_kernel,
        out_shape=jax.ShapeDtypeStruct(arrays[0].shape, BF16),
        in_specs=[VMEM] * len(arrays),
        out_specs=VMEM,
        compiler_params=PARAMS,
        cost_estimate=COST,
    )(*arrays)


def part_kernel(count, *refs):
    lists, outs = refs[:2], refs[2 + count :]
    total = refs[2][...].astype(F32)
    for ref in refs[3 : 2 + count]:
        total = total + ref[...].astype(F32)
    total = total.astype(BF16)
    rows = total.shape[2] * total.shape[3]
    for n, out in enumerate(outs):
        for core in range(2):
            out[core, :rows] = total[n, core].reshape(rows, total.shape[4])
            out[core, rows:] = lists[core][...]


def part(arrays, lists):
    count, _, per, rank, width = arrays[0].shape
    return pl.pallas_call(
        functools.partial(part_kernel, len(arrays)),
        out_shape=[jax.ShapeDtypeStruct((2, per * rank + lists[0].shape[0], width), BF16)] * count,
        in_specs=[VMEM] * (2 + len(arrays)),
        out_specs=[VMEM] * count,
        compiler_params=PARAMS,
        cost_estimate=COST,
    )(*lists, *arrays)


def stack_kernel(core, *refs):
    for n, ref in enumerate(refs[:-1]):
        refs[-1][n] = ref[...] if core is None else ref[core]


def stack(arrays, core=None):
    shape = arrays[0].shape if core is None else arrays[0].shape[1:]
    return pl.pallas_call(
        functools.partial(stack_kernel, core),
        out_shape=jax.ShapeDtypeStruct((len(arrays),) + shape, arrays[0].dtype),
        in_specs=[VMEM] * len(arrays),
        out_specs=VMEM,
        compiler_params=PARAMS,
        cost_estimate=COST,
    )(*arrays)


def join_kernel(own_ref, other_ref, *outs):
    for n, out in enumerate(outs):
        out[0] = own_ref[n]
        out[1] = other_ref[n]


def join(own, other):
    return pl.pallas_call(
        join_kernel,
        out_shape=[jax.ShapeDtypeStruct((2,) + own.shape[1:], own.dtype)] * own.shape[0],
        in_specs=[VMEM] * 2,
        out_specs=[VMEM] * own.shape[0],
        compiler_params=PARAMS,
        cost_estimate=COST,
    )(own, other)


def couple_kernel(sizes, jobs, at_ref, *refs):
    planes, nz, most, held, halves, given = sizes
    me = lax.bitwise_and(at_ref[1], jnp.int32(1))
    first = given > 0
    if first:
        table_ref, own_ref = refs[:2]
        sources, refs = refs[2 : 2 + given], refs[2 + given :]
        rows, (wide, numbers, lists, sem) = refs[:-4], refs[-4:]
    else:
        lists, table_ref, wide = refs[:3]
        rows = refs[3:]
    per, _, _, rank, _ = table_ref.shape
    count = wide.shape[0] - 1
    if first:
        held_by, gathered = {}, []
        pos = 0
        for bases in halves:
            other = sources[pos + len(bases)]
            for n, base in enumerate(bases):
                held_by[base] = (sources[pos + n].at[0], other.at[n])
            pos += len(bases) + 1
        gathered = sources[pos:]
        numbers[0] = own_ref[...].astype(F32).astype(jnp.int32)
        for z in range(1, nz):
            mine, theirs = (ref[per * rank :].astype(F32) for ref in held_by[z * planes])
            numbers[z] = jnp.where(me == 0, mine, theirs).astype(jnp.int32)
        copy = pltpu.make_async_copy(numbers, lists, sem)
        copy.start()
        parts = []
        if gathered:
            parts = [(t, gathered[0].at[t]) for t in range(gathered[0].shape[0])]
        else:
            for base, pair in held_by.items():
                for s, source in enumerate(pair):
                    q = lax.bitwise_xor(xor(at_ref[0], base % planes), xor(me, s))
                    parts.append((xor(at_ref[2], base // planes) * planes + q, source))
        for t, source in parts:
            for m in range(per):
                v = source[m * rank : (m + 1) * rank]
                wide[t, m, :rank] = v
                wide[t, m, rank:] = turned(v)
        wide[count] = jnp.zeros_like(wide[count])
        copy.wait()
    for row, (bases, s) in zip(rows, jobs):
        for n, base in enumerate(bases):
            q, z = lax.bitwise_xor(xor(at_ref[0], base % planes), xor(me, s)), at_ref[2]
            for m in range(per):
                entry = (base // planes, q * held + z * per + m)
                active = lists[entry + (2 * most,)]
                total = None
                for k in range(most):
                    kind = lists[entry + (most + k,)]
                    source = jnp.where(k < active, lists[entry + (k,)], count)
                    both = jnp.concatenate([table_ref[m, kind, 0], table_ref[m, kind, 1]], axis=1)
                    term = dot(both, wide[source, m])
                    total = term if total is None else total + term
                row[n, m] = total.T.astype(BF16)


def couple(at, table, jobs, sizes, own=None, sources=(), total=0, lists=None, wide=None):
    per, _, _, rank, _ = table.shape
    width = (sources[0] if sources else wide).shape[-1]
    rows = [jax.ShapeDtypeStruct((len(bases), per, width, rank), BF16) for bases, _ in jobs]
    grown, scratch = [], []
    if sources:
        listed = (sizes[1],) + own.shape
        grown = [
            jax.ShapeDtypeStruct((total + 1, per, 2 * rank, width), BF16),
            jax.ShapeDtypeStruct(listed, jnp.int32),
        ]
        scratch = [pltpu.SMEM(listed, jnp.int32), pltpu.SemaphoreType.DMA]
    return pl.pallas_call(
        functools.partial(couple_kernel, sizes + (len(sources),), jobs),
        out_shape=rows + grown,
        in_specs=[SMEM] + ([VMEM] * (2 + len(sources)) if sources else [SMEM, VMEM, VMEM]),
        out_specs=[VMEM] * (len(rows) + len(grown)),
        scratch_shapes=scratch,
        compiler_params=PARAMS,
        cost_estimate=COST,
    )(at, *((table, own, *sources) if sources else (lists, table, wide)))


def down_kernel(jobs, last, at_ref, dir_ref, mat_ref, *rest):
    pieces = rest[: len(jobs)]
    if last:
        before, out_ref, sums = rest[len(jobs) :]
    else:
        (sums,) = rest[len(jobs) :]
    children, planes, fam, nz, per, _, rank, _ = mat_ref.shape
    sums[...] = jnp.zeros_like(sums)
    for piece, (rel, bases) in zip(pieces, jobs):
        for n, core in [(n, core) for n in range(len(bases)) for core in range(2)]:
            q, j, z = place(at_ref, planes, rel, bases[n], core)
            for m in range(per):
                e = ((q * fam + j) * nz + z) * per + m
                v = piece[n, core, m]
                x = jnp.concatenate([v, turned_rows(v)], axis=1)
                both = [mat_ref[c, q, j, z, m].reshape(2 * rank, rank) for c in range(children)]
                y = dot(x, jnp.concatenate(both, axis=1))
                for c in range(children):
                    sums[c, dir_ref[c, e]] += y[:, c * rank : (c + 1) * rank]
    if last:
        for c in range(children):
            for i in range(out_ref.shape[1]):
                out_ref[c, i] = (sums[c, i] + before[c, i]).T.astype(BF16)


def down(at, dirs, mats, jobs, pieces, groups, before=None):
    children, rank = mats.shape[0], mats.shape[-1]
    width = pieces[0].shape[-2]
    last = before is not None
    sums = (children, groups, width, rank)
    return pl.pallas_call(
        functools.partial(down_kernel, jobs, last),
        out_shape=jax.ShapeDtypeStruct((children, groups, rank, width), BF16) if last else jax.ShapeDtypeStruct(sums, F32),
        in_specs=[SMEM, SMEM] + [VMEM] * (1 + len(pieces) + (1 if last else 0)),
        out_specs=VMEM,
        scratch_shapes=[pltpu.VMEM(sums, F32)] if last else [],
        compiler_params=PARAMS,
        cost_estimate=COST,
    )(at, dirs, mats, *pieces, *([before] if last else []))


def body(nx, ny, child_coef, transfer, child_dir, couple_src, couple_kind, couple_count, couple_table):
    children, dirs, _, rank, _ = transfer.shape
    planes, held, most = couple_src.shape
    fam = ny // planes
    split = held % nx == 0
    nz = nx if split else 1
    per = held // nz
    partners = nz * planes
    at_y, at_x = lax.axis_index("gy"), lax.axis_index("gx")
    at = jnp.stack([at_y // fam, at_y % fam, at_x if split else jnp.zeros_like(at_x)]).astype(jnp.int32)
    mats = transfer.reshape(children, planes, fam, nz, per, 2, rank, rank)
    bases = tuple(range(partners - 2, -1, -2))
    far, near = bases[: len(bases) // 2], bases[len(bases) // 2 :]
    halves = (far, near)

    def family(x, rel):
        return lax.ppermute(x, "gy", [(i, i ^ rel) for i in range(ny)])

    def partner(x, base):
        moves = [(r // planes) * ny + (r % planes) * fam for r in (base, base ^ 1)]
        axes, size = (("gx", "gy"), nx * ny) if split else ("gy", ny)
        return lax.ppermute(x, axes, [(i, i ^ moves[i & 1]) for i in range(size)])

    lists = jnp.concatenate([couple_src, couple_kind, couple_count[..., None]], axis=-1).reshape(planes * held, -1)
    lists = jnp.pad(lists, ((0, -planes * held % 16), (0, rank - lists.shape[1]))).astype(BF16)
    odd = [rel for rel in range(fam) if rel & 1]
    lead = [(0, odd[-1])]
    soon = [[(0, odd[-1] ^ 1), (1, odd[-1])], [(0, rel) for rel in odd[:-1]]]
    early = lead + soon[0] + soon[1]
    late = [(h, rel) for h in (1, 0) for rel in sorted(range(fam), reverse=True) if (h, rel) not in early]
    got = {}
    sums, _ = up(at, child_dir, child_coef, mats, halves, [lead] + [group for group in soon if group])
    got.update({key: [value] for key, value in sums.items()})

    def reduce_step(h, rel):
        terms = got.pop((h, rel))
        low = rel & -rel
        got.setdefault((h, rel ^ low), []).append(family(add(terms) if len(terms) > 1 else terms[0], low))

    for key in early:
        if key[1] & 1:
            reduce_step(*key)
    key = (0, odd[-1] ^ 1)
    if key[1]:
        got[key] = [add(got[key])]
        got[key][0], at_late, lists = lax.optimization_barrier((got[key][0], at, lists))
        both_lists = (lists, family(lists, 1))
        reduce_step(*key)
    else:
        at_late = at
    late = [late[:1], late[1:3], late[3:5], late[5:]]
    sums, (table,) = up(at_late, child_dir, child_coef, mats, halves, [group for group in late if group], couple_table)
    for key, value in sums.items():
        got.setdefault(key, []).append(value)
    for rel in sorted((r for r in range(1, fam)), key=lambda r: (-(r & 1), -r)):
        if (0, rel) in got:
            reduce_step(0, rel)
        if rel & 1 and (1, rel) in got:
            reduce_step(1, rel)
    far_sent = part(got[(0, 0)], both_lists)
    for rel in range(fam - 2, 0, -2):
        got[(1, rel)], far_sent = lax.optimization_barrier((got[(1, rel)], far_sent))
        reduce_step(1, rel)
    sources = []
    for h, sent in ((0, far_sent), (1, part(got[(1, 0)], both_lists))):
        arrived = [partner(x, base) for x, base in zip(sent, halves[h])]
        sources += arrived + [family(stack(arrived, core=1), 1)]
    if not split:
        own = jnp.zeros((partners,) + sources[0].shape[1:], BF16)
        pos = 0
        for h in range(2):
            for n, base in enumerate(halves[h]):
                for s, value in enumerate((sources[pos + n][0], sources[pos + len(halves[h])][n])):
                    spot = lax.bitwise_xor(at[0], jnp.int32(base ^ s)) ^ (at[1] & 1)
                    own = lax.dynamic_update_index_in_dim(own, value, spot, 0)
            pos += len(halves[h]) + 1
        sources.append(lax.all_gather(own, "gx", axis=0, tiled=True))
    sizes = (planes, nz, most, held, halves)
    theirs, wide, numbers = couple(at, table, ((far, 1),), sizes, lists, sources, nx * planes)
    rows = {}
    theirs = family(theirs, 1)
    (mine,) = couple(at, table, ((far, 0),), sizes, lists=numbers, wide=wide)
    rows[0] = (mine, theirs)
    theirs, mine = couple(at, table, ((near, 1), (near, 0)), sizes, lists=numbers, wide=wide)
    rows[1] = (mine, family(theirs, 1))
    local = {}
    for h in range(2):
        for base, x in zip(halves[h], join(*rows[h])):
            local[base] = partner(x, base)
    pieces = {}
    for h in (1, 0):
        pieces[(h, 0)] = stack([local[r] for r in halves[h]])
    groups = child_coef.shape[1]

    def jobs(keys):
        return tuple((rel, halves[h]) for h, rel in keys)

    def spread(h, bit):
        for rel in sorted(r for g, r in pieces if g == h):
            pieces[(h, rel ^ bit)] = family(pieces[(h, rel)], bit)

    bits = [1 << n for n in range(fam.bit_length() - 1)]
    high = bits[-1]
    spread(1, high)
    for bit in bits[-2::-1]:
        pieces[(1, bit)] = family(pieces[(1, 0)], bit)
        pieces[(0, 0)], pieces[(1, bit)] = lax.optimization_barrier((pieces[(0, 0)], pieces[(1, bit)]))
    spread(0, high)
    for bit in bits[-2::-1]:
        for rel in sorted(r for g, r in pieces if g == 1):
            if (1, rel ^ bit) not in pieces:
                pieces[(1, rel ^ bit)] = family(pieces[(1, rel)], bit)
    straight = family(pieces[(0, 0)], 1) if fam > 2 else None
    first_keys = [key for key in pieces if key != (0, high)]
    values = [pieces[key] for key in first_keys]
    first_jobs = jobs(first_keys)
    if straight is not None:
        values.append(straight)
        first_jobs += ((1, far),)
    first = down(at, child_dir, mats, first_jobs, values, groups)
    pieces[(0, high)], first = lax.optimization_barrier((pieces[(0, high)], first))
    for bit in bits[-2::-1]:
        for rel in sorted(r for g, r in pieces if g == 0):
            if (0, rel ^ bit) not in pieces and not (bit == 1 and rel == 0):
                pieces[(0, rel ^ bit)] = family(pieces[(0, rel)], bit)
    last_keys = [key for key in pieces if key not in first_keys]
    return down(at, child_dir, mats, jobs(last_keys), [pieces[key] for key in last_keys], groups, before=first)


def solution(mesh):
    return jax.shard_map(
        functools.partial(body, mesh.shape["gx"], mesh.shape["gy"]),
        mesh=mesh,
        in_specs=(
            P(("gx", "gy"), None, None, None),
            P(("gx", "gy"), None, None, None, None),
            P(("gx", "gy"), None),
            P("gx", "gy", None),
            P("gx", "gy", None),
            P("gx", "gy"),
            P("gy", None, None, None, None),
        ),
        out_specs=P(("gx", "gy"), None, None, None),
        check_vma=False,
    )
```

time: 247 us -> 73.4 us (0.30)
  blocking collectives: 54.1 us -> 0 us
  local copies, waits for them, and re-layouts: 53.7 us -> 1 us
  matrix products: 40.8 us -> 0 us
  other arithmetic: 34.8 us -> 0.17 us
  Pallas kernels: 0 us -> 21.8 us
  starting transfers between devices: 3.82 us -> 21.2 us
  waiting for transfers between devices: 46.1 us -> 28.8 us
  between operations: 13.5 us -> 0.2 us
    all_to_all x1 -> x0, blocking collectives: 54.1 us -> none  [body(): lax.all_to_all(upward.astype(jnp.bfloat16), 'gy', split_axis=1, concat_ax...]
    dot_general x7 -> x0, matrix products: 40.8 us -> none  [the longest x3 19.5 us: complex_apply(): jnp.einsum(pattern, real_part, vectors, preferred_element_type=jnp.float32)]
    gather x6 -> x0, local copies, waits for them, and re-layouts: 33.7 us -> none  [the longest x2 19.2 us: body(): matrices = couple_table[dir_local, couple_kind]]
    ppermute x0 -> x25, waiting for transfers between devices: none -> 28.8 us  [the longest x8 16.7 us: partner(): return lax.ppermute(x, axes, [(i, i ^ moves[i & 1]) for i in range(size)])]
    all_gather x1 -> x0, waiting for transfers between devices: 25.7 us -> none  [body(): everything = lax.all_gather(parent, 'gx', axis=0, tiled=True)]
    pallas_call x0 -> x17, Pallas kernels: none -> 21.8 us  [the longest x2 9.91 us: up(): pl.pallas_call(functools.partial(up_kernel, jobs, len(extra)), out_shape=...]
    ppermute x0 -> x25, starting transfers between devices: none -> 21.2 us  [the longest x17 11.5 us: family(): return lax.ppermute(x, 'gy', [(i, i ^ rel) for i in range(ny)])]
    all_to_all x1 -> x0, waiting for transfers between devices: 20.3 us -> none  [body(): lax.all_to_all(copies, 'gy', split_axis=0, concat_axis=1, tiled=True)[0]]
  transfers between devices with their start and end apart: 2 -> 25, of which waited for: 2 -> 14; matrix products, arithmetic and copies ran while one was open for 10% -> 1% of each run, Pallas kernels for 0% -> 13%
where the time goes in v2:
time: 73.4 us; the launch traced here: 73.2 us
  waiting for transfers between devices  28.8 us (39%)
  Pallas kernels  21.8 us (30%)
  starting transfers between devices  21.2 us (29%)
  local copies, waits for them, and re-layouts  1 us (1%)
    ppermute x8, waiting for transfers between devices, partner(): return lax.ppermute(x, axes, [(i, i ^ moves[i & 1]) for i in range(size)])  16.7 us
    ppermute x17, waiting for transfers between devices, family(): return lax.ppermute(x, 'gy', [(i, i ^ rel) for i in range(ny)])  12.1 us
    ppermute x17, starting transfers between devices, family(): return lax.ppermute(x, 'gy', [(i, i ^ rel) for i in range(ny)])  11.5 us
    pallas_call x2, Pallas kernels, up(): pl.pallas_call(functools.partial(up_kernel, jobs, len(extra)), out_shape=...  9.91 us
    ppermute x8, starting transfers between devices, partner(): return lax.ppermute(x, axes, [(i, i ^ moves[i & 1]) for i in range(size)])  9.69 us
    pallas_call x3, Pallas kernels, couple(): pl.pallas_call(functools.partial(couple_kernel, sizes + (len(sources),),...  6.67 us
    pallas_call x2, Pallas kernels, down(): pl.pallas_call(functools.partial(down_kernel, jobs, last), out_shape=jax....  4.75 us
  transfers between devices with their start and end apart: 25, of which 14 were waited for; matrix products, arithmetic and copies ran while one was open for 1% of the time, Pallas kernels for 13%

profile of v2, /device:TPU:0, one launch (start us, length us, event | category | flops | bytes accessed | tf_op | source)
XLA Modules:
  0.0 73.2 jit_solution(6871073738698640741)
XLA Ops:
  0.1 0.7 copy-done
  0.8 4.8 %shard_map.73 = (bf16[2,2,2,128,128]{4,3,2,1,0:T(8,128)(2,1)S(1)}, bf16[2,2,2,128,128]{4,3,2,1,0:T(8,128)(2,1)S(1)}, bf16[2,2,2,128,128]{4,3,2,1,0:T(8,128)(2,1)S(1)}, bf16[2,2,2,128,128]{4,3,2,1,0:T(8,128)(2,1)S(1)}) custom-call(s32[3]{0:T(128)S(1)} %pad_add_fusion.at_ref, s32[2,64]{1,0:T(2,128)S(1)} %copy-done, bf16[2,16,128,128]{3,2,1,0:T(8,128)(2,1)} %coef_hbm.3, ...), custom_call_target="tpu_custom_call" | custom-call | flops 10000000000 | bytes 1000000 | tf_op jit(solution)/shard_map/pallas_call | solution.py:94
  5.5 0.5 collective-permute-start
  6.1 0.1 collective-permute-start.3
  6.1 0.4 collective-permute-start.1
  6.6 0.1 copy.11
  6.7 0.1 copy.12
  6.8 0.1 concatenate.15
  6.9 0.1 fusion.4.refs_0_.refs_1_
  7.0 0.2 collective-permute-done.refs_1_
  7.3 2.9 %collective-permute-start.4 = (bf16[2,2,2,128,128]{4,3,2,1,0:T(8,128)(2,1)S(1)}, bf16[2,2,2,128,128]{4,3,2,1,0:T(8,128)(2,1)S(1)}, u32[]{:S(2)}, u32[]{:S(2)}) collective-permute-start(bf16[2,2,2,128,128]{4,3,2,1,0:T(8,128)(2,1)S(1)} %shard_map.74), channel_id=1, source_target_pairs={{0,2},{1,3},{2,0},{3,1},{4,6},{5,7},{6,4},{7,5},{8,10},{9,11},{10,... | collective-permute-start | bytes 786440 | tf_op jit(solution)/shard_map/ppermute | solution.py:328
  10.2 5.1 %shard_map.75 = (bf16[2,2,2,128,128]{4,3,2,1,0:T(8,128)(2,1)S(1)}, bf16[2,2,2,128,128]{4,3,2,1,0:T(8,128)(2,1)S(1)}, bf16[2,2,2,128,128]{4,3,2,1,0:T(8,128)(2,1)...) custom-call(s32[3]{0:T(128)S(1)} %pad_add_fusion.at_ref, s32[2,64]{1,0:T(2,128)S(1)} %copy-done.1, ...), custom_call_target="tpu_custom_call" | custom-call | flops 10000000000 | bytes 1000000 | tf_op jit(solution)/shard_map/pallas_call | solution.py:94
  15.4 0.6 collective-permute-start.8
  15.9 0.9 %collective-permute-done.4.refs_3_ = bf16[2,2,2,128,128]{4,3,2,1,0:T(8,128)(2,1)S(1)} collective-permute-done((bf16[2,2,2,128,128]{4,3,2,1,0:T(8,128)(2,1)S(1)}, bf16[2,2,2,128,128]{4,3,2,1,0:T(8,128)(2,1)S(1)}, u32[]{:S(2)}, u32[]{:S(2)}) %collective-permute-start.4) | collective-permute-done | bytes 262176 | tf_op jit(solution)/shard_map/ppermute | solution.py:328
  16.8 0.1 shard_map.76
  17.0 1.8 %collective-permute-start.9 = (bf16[2,2,2,128,128]{4,3,2,1,0:T(8,128)(2,1)S(1)}, bf16[2,2,2,128,128]{4,3,2,1,0:T(8,128)(2,1)S(1)}, u32[]{:S(2)}, u32[]{:S(2)}) collective-permute-start(bf16[2,2,2,128,128]{4,3,2,1,0:T(8,128)(2,1)S(1)} %shard_map.78), channel_id=1, source_target_pairs={{0,2},{1,3},{2,0},{3,1},{4,6},{5,7},{6,4},{7,5},{8,10},{9,11},{10,... | collective-permute-start | bytes 786440 | tf_op jit(solution)/shard_map/ppermute | solution.py:328
  18.8 3.6 %collective-permute-start.5 = (bf16[2,272,128]{2,1,0:T(8,128)(2,1)S(1)}, bf16[2,272,128]{2,1,0:T(8,128)(2,1)S(1)}, u32[]{:S(2)}, u32[]{:S(2)}) collective-permute-start(bf16[2,272,128]{2,1,0:T(8,128)(2,1)S(1)} %get-tuple-element.50), channel_id=1, source_target_pairs={{0,24},{1,29},{2,26},{3,31},{4,28},{5,25},{6,30},{7,27},{8,16},{9,... | collective-permute-start | bytes 417800 | tf_op jit(solution)/shard_map/ppermute | solution.py:333
  22.4 2.5 %collective-permute-done.9.refs_4_ = bf16[2,2,2,128,128]{4,3,2,1,0:T(8,128)(2,1)S(1)} collective-permute-done((bf16[2,2,2,128,128]{4,3,2,1,0:T(8,128)(2,1)S(1)}, bf16[2,2,2,128,128]{4,3,2,1,0:T(8,128)(2,1)S(1)}, u32[]{:S(2)}, u32[]{:S(2)}) %collective-permute-start.9) | collective-permute-done | bytes 262176 | tf_op jit(solution)/shard_map/ppermute | solution.py:328
  24.9 0.1 shard_map.79
  25.0 1.6 %collective-permute-start.10 = (bf16[2,272,128]{2,1,0:T(8,128)(2,1)S(1)}, bf16[2,272,128]{2,1,0:T(8,128)(2,1)S(1)}, u32[]{:S(2)}, u32[]{:S(2)}) collective-permute-start(bf16[2,272,128]{2,1,0:T(8,128)(2,1)S(1)} %get-tuple-element.56), channel_id=1, source_target_pairs={{0,8},{1,13},{2,10},{3,15},{4,12},{5,9},{6,14},{7,11},{8,0},{9,5},... | collective-permute-start | bytes 417800 | tf_op jit(solution)/shard_map/ppermute | solution.py:333
  26.6 0.7 collective-permute-start.11
  27.2 7.1 %collective-permute-done.6.refs_1_.refs_3_ = bf16[2,272,128]{2,1,0:T(8,128)(2,1)S(1)} collective-permute-done((bf16[2,272,128]{2,1,0:T(8,128)(2,1)S(1)}, bf16[2,272,128]{2,1,0:T(8,128)(2,1)S(1)}, u32[]{:S(2)}, u32[]{:S(2)}) %collective-permute-start.6) | collective-permute-done | bytes 139296 | tf_op jit(solution)/shard_map/ppermute | solution.py:333
  34.5 0.5 collective-permute-start.12
  35.0 0.8 %collective-permute-done.7.refs_4_ = bf16[2,272,128]{2,1,0:T(8,128)(2,1)S(1)} collective-permute-done((bf16[2,272,128]{2,1,0:T(8,128)(2,1)S(1)}, bf16[2,272,128]{2,1,0:T(8,128)(2,1)S(1)}, u32[]{:S(2)}, u32[]{:S(2)}) %collective-permute-start.7) | collective-permute-done | bytes 139296 | tf_op jit(solution)/shard_map/ppermute | solution.py:328
  35.8 0.2 collective-permute-done.12.refs_7_
  36.0 2.6 %shard_map.81 = (bf16[2,2,128,128]{3,2,1,0:T(8,128)(2,1)S(1)}, bf16[9,2,256,128]{3,2,1,0:T(8,128)(2,1)S(1)}, s32[4,16,128]{2,1,0:T(8,128)S(1)}) custom-call(s32[3]{0:T(128)S(1)} %pad_add_fusion.at_ref, bf16[2,8,2,128,128]{4,3,2,1,0:T(8,128)(2,1)S(1)} %get-tuple-element.41.refs_0_.refs_1_, bf16[16,128]{1,0:T(8,128)(2,1)S(1)} %fusion.4.refs_0_.refs_1_, ...), custom_call_target="tpu_custom_call" | custom-call | flops 10000000000 | bytes 1000000 | tf_op jit(solution)/shard_map/pallas_call | solution.py:260
  38.6 2.3 %shard_map.85 = (bf16[2,2,128,128]{3,2,1,0:T(8,128)(2,1)S(1)}, bf16[2,2,128,128]{3,2,1,0:T(8,128)(2,1)S(1)}) custom-call(s32[3]{0:T(128)S(1)} %pad_add_fusion.at_ref, s32[4,16,128]{2,1,0:T(8,128)S(1)} %get-tuple-element.58.refs_0_, bf16[2,8,2,128,128]{4,3,2,1,0:T(8,128)(2,1)S(1)} %get-tuple-element.41.refs_0_.refs_1_, ...), custom_call_target="tpu_custom_call" | custom-call | flops 10000000000 | bytes 1000000 | tf_op jit(solution)/shard_map/pallas_call | solution.py:260
  40.9 0.4 collective-permute-start.16
  41.3 1.8 %shard_map.82.own_ref = bf16[2,2,128,128]{3,2,1,0:T(8,128)(2,1)S(1)} custom-call(s32[3]{0:T(128)S(1)} %pad_add_fusion.at_ref, s32[4,16,128]{2,1,0:T(8,128)S(1)} %get-tuple-element.58.refs_0_, bf16[2,8,2,128,128]{4,3,2,1,0:T(8,128)(2,1)S(1)} %get-tuple-element.41.refs_0_.refs_1_, bf16[9,2,256,128]{3,2,1,0:T(8,128)(2,1)S(1)} %get-tuple-element.59.refs_2_), custom_call_target="tpu_custom_call" | custom-call | flops 10000000000 | bytes 1000000 | tf_op jit(solution)/shard_map/pallas_call | solution.py:260
  43.1 0.2 collective-permute-start.13
  43.4 0.7 collective-permute-start.18
  44.1 0.4 collective-permute-done.13.other_ref
  44.6 2.5 %collective-permute-start.14 = (bf16[2,2,128,128]{3,2,1,0:T(8,128)(2,1)S(1)}, bf16[2,2,128,128]{3,2,1,0:T(8,128)(2,1)S(1)}, u32[]{:S(2)}, u32[]{:S(2)}) collective-permute-start(bf16[2,2,128,128]{3,2,1,0:T(8,128)(2,1)S(1)} %get-tuple-element.61), channel_id=1, source_target_pairs={{0,24},{1,29},{2,26},{3,31},{4,28},{5,25},{6,30},{7,27},{8,16},{9,... | collective-permute-start | bytes 393224 | tf_op jit(solution)/shard_map/ppermute | solution.py:333
  47.1 0.6 collective-permute-start.15
  47.7 1.4 %collective-permute-done.17.refs_0_ = bf16[2,2,128,128]{3,2,1,0:T(8,128)(2,1)S(1)} collective-permute-done((bf16[2,2,128,128]{3,2,1,0:T(8,128)(2,1)S(1)}, bf16[2,2,128,128]{3,2,1,0:T(8,128)(2,1)S(1)}, u32[]{:S(2)}, u32[]{:S(2)}) %collective-permute-start.17) | collective-permute-done | bytes 131104 | tf_op jit(solution)/shard_map/ppermute | solution.py:333
  49.2 1.6 %collective-permute-start.19 = (bf16[2,2,2,128,128]{4,3,2,1,0:T(8,128)(2,1)S(1)}, bf16[2,2,2,128,128]{4,3,2,1,0:T(8,128)(2,1)S(1)}, u32[]{:S(2)}, u32[]{:S(2)}) collective-permute-start(bf16[2,2,2,128,128]{4,3,2,1,0:T(8,128)(2,1)S(1)} %shard_map.87.rest_0_), channel_id=1, source_target_pairs={{0,1},{1,0},{2,3},{3,2},{4,5},{5,4},{6,7},{7,6},{8,9},{9,8},{10,11... | collective-permute-start | bytes 786440 | tf_op jit(solution)/shard_map/ppermute | solution.py:328
  50.8 0.6 collective-permute-start.21
  51.3 0.1 collective-permute-done.14.refs_0_
  51.5 8.0 %collective-permute-done.15.refs_1_ = bf16[2,2,128,128]{3,2,1,0:T(8,128)(2,1)S(1)} collective-permute-done((bf16[2,2,128,128]{3,2,1,0:T(8,128)(2,1)S(1)}, bf16[2,2,128,128]{3,2,1,0:T(8,128)(2,1)S(1)}, u32[]{:S(2)}, u32[]{:S(2)}) %collective-permute-start.15) | collective-permute-done | bytes 131104 | tf_op jit(solution)/shard_map/ppermute | solution.py:333
  59.6 0.8 %collective-permute-start.23 = (bf16[2,2,2,128,128]{4,3,2,1,0:T(8,128)(2,1)S(1)}, bf16[2,2,2,128,128]{4,3,2,1,0:T(8,128)(2,1)S(1)}, u32[]{:S(2)}, u32[]{:S(2)}) collective-permute-start(bf16[2,2,2,128,128]{4,3,2,1,0:T(8,128)(2,1)S(1)} %shard_map.84.rest_1_), channel_id=1, source_target_pairs={{0,1},{1,0},{2,3},{3,2},{4,5},{5,4},{6,7},{7,6},{8,9},{9,8},{10,11... | collective-permute-start | bytes 786440 | tf_op jit(solution)/shard_map/ppermute | solution.py:328
  60.3 0.1 collective-permute-start.22
  60.4 0.9 %collective-permute-start.20 = (bf16[2,2,2,128,128]{4,3,2,1,0:T(8,128)(2,1)S(1)}, bf16[2,2,2,128,128]{4,3,2,1,0:T(8,128)(2,1)S(1)}, u32[]{:S(2)}, u32[]{:S(2)}) collective-permute-start(bf16[2,2,2,128,128]{4,3,2,1,0:T(8,128)(2,1)S(1)} %shard_map.84.rest_1_), channel_id=1, source_target_pairs={{0,2},{1,3},{2,0},{3,1},{4,6},{5,7},{6,4},{7,5},{8,10},{9,11},{10,... | collective-permute-start | bytes 786440 | tf_op jit(solution)/shard_map/ppermute | solution.py:328
  61.3 0.1 collective-permute-done.23.rest_5_
  61.5 0.4 collective-permute-done.22.rest_4_
  61.9 2.2 %shard_map.88.rest_2_ = f32[2,16,128,128]{3,2,1,0:T(8,128)S(1)} custom-call(s32[3]{0:T(128)S(1)} %pad_add_fusion.at_ref, s32[2,64]{1,0:T(2,128)S(1)} %copy-done.1, bf16[2,2,4,4,2,2,128,128]{7,6,5,4,3,2,1,0:T(8,128)(2,1)S(1)} %bitcast.10, bf16[2,2,2,128,128]{4,3,2,1,0:T(8,128)(2,1)S(1)} %shard_map.87.rest_0_, ...), custom_call_target="tpu_custom_call" | custom-call | flops 10000000000 | bytes 1000000 | tf_op jit(solution)/shard_map/pallas_call | solution.py:301
  64.1 5.0 %collective-permute-done.20.rest_0_ = bf16[2,2,2,128,128]{4,3,2,1,0:T(8,128)(2,1)S(1)} collective-permute-done((bf16[2,2,2,128,128]{4,3,2,1,0:T(8,128)(2,1)S(1)}, bf16[2,2,2,128,128]{4,3,2,1,0:T(8,128)(2,1)S(1)}, u32[]{:S(2)}, u32[]{:S(2)}) %collective-permute-start.20) | collective-permute-done | bytes 262176 | tf_op jit(solution)/shard_map/ppermute | solution.py:328
  69.1 1.5 %collective-permute-done.24.rest_1_ = bf16[2,2,2,128,128]{4,3,2,1,0:T(8,128)(2,1)S(1)} collective-permute-done((bf16[2,2,2,128,128]{4,3,2,1,0:T(8,128)(2,1)S(1)}, bf16[2,2,2,128,128]{4,3,2,1,0:T(8,128)(2,1)S(1)}, u32[]{:S(2)}, u32[]{:S(2)}) %collective-permute-start.24) | collective-permute-done | bytes 262176 | tf_op jit(solution)/shard_map/ppermute | solution.py:328
  70.6 2.6 %shard_map.89 = bf16[2,16,128,128]{3,2,1,0:T(8,128)(2,1)} custom-call(s32[3]{0:T(128)S(1)} %pad_add_fusion.at_ref, s32[2,64]{1,0:T(2,128)S(1)} %copy-done.1, bf16[2,2,4,4,2,2,128,128]{7,6,5,4,3,2,1,0:T(8,128)(2,1)S(1)} %bitcast.11, bf16[2,2,2,128,128]{4,3,2,1,0:T(8,128)(2,1)S(1)} %collective-permute-done.20.rest_0_, ...), custom_call_target="tpu_custom_call" | custom-call | flops 10000000000 | bytes 1000000 | tf_op jit(solution)/shard_map/pallas_call | solution.py:301
  (42 shorter events, 0.5 us)
Async XLA Ops:
  0.1 0.7 copy-start
  0.8 5.8 %copy-start.2 = (s32[2,8,7]{1,0,2:T(2,128)S(1)}, s32[2,8,7]{1,0,2:T(2,128)}, u32[]{:S(2)}) copy-start(s32[2,8,7]{1,0,2:T(2,128)} %param.10) | copy-start | bytes 1348
  0.8 5.9 %copy-start.3 = (s32[2,8,7]{1,0,2:T(2,128)S(1)}, s32[2,8,7]{1,0,2:T(2,128)}, u32[]{:S(2)}) copy-start(s32[2,8,7]{1,0,2:T(2,128)} %param.11) | copy-start | bytes 1348
  0.8 6.0 %copy-start.4 = (s32[2,8]{1,0:T(2,128)S(1)}, s32[2,8]{1,0:T(2,128)}, u32[]{:S(2)}) copy-start(s32[2,8]{1,0:T(2,128)} %param.12) | copy-start | bytes 196
  5.5 1.7 %collective-permute-start = (bf16[2,2,2,128,128]{4,3,2,1,0:T(8,128)(2,1)S(1)}, bf16[2,2,2,128,128]{4,3,2,1,0:T(8,128)(2,1)S(1)}, u32[]{:S(2)}, u32[]{:S(2)}) collective-permute-start(bf16[2,2,2,128,128]{4,3,2,1,0:T(8,128)(2,1)S(1)} %get-tuple-element.39), channel_id=1, source_target_pairs={{0,1},{1,0},{2,3},{3,2},{4,5},{5,4},{6,7},{7,6},{8,9},{9,8},{10,11... | collective-permute-start | bytes 786440 | tf_op jit(solution)/shard_map/ppermute | solution.py:328
  6.1 9.9 %collective-permute-start.3 = (bf16[2,2,2,128,128]{4,3,2,1,0:T(8,128)(2,1)S(1)}, bf16[2,2,2,128,128]{4,3,2,1,0:T(8,128)(2,1)S(1)}, u32[]{:S(2)}, u32[]{:S(2)}) collective-permute-start(bf16[2,2,2,128,128]{4,3,2,1,0:T(8,128)(2,1)S(1)} %get-tuple-element.45), channel_id=1, source_target_pairs={{0,1},{1,0},{2,3},{3,2},{4,5},{5,4},{6,7},{7,6},{8,9},{9,8},{10,11... | collective-permute-start | bytes 786440 | tf_op jit(solution)/shard_map/ppermute | solution.py:328
  6.1 10.8 %collective-permute-start.1 = (bf16[2,2,2,128,128]{4,3,2,1,0:T(8,128)(2,1)S(1)}, bf16[2,2,2,128,128]{4,3,2,1,0:T(8,128)(2,1)S(1)}, u32[]{:S(2)}, u32[]{:S(2)}) collective-permute-start(bf16[2,2,2,128,128]{4,3,2,1,0:T(8,128)(2,1)S(1)} %get-tuple-element.43), channel_id=1, source_target_pairs={{0,1},{1,0},{2,3},{3,2},{4,5},{5,4},{6,7},{7,6},{8,9},{9,8},{10,11... | collective-permute-start | bytes 786440 | tf_op jit(solution)/shard_map/ppermute | solution.py:328
  7.2 3.0 %copy-start.1 = (s32[2,64]{1,0:T(2,128)S(1)}, s32[2,64]{1,0:T(2,128)}, u32[]{:S(2)}) copy-start(s32[2,64]{1,0:T(2,128)} %dir_ref.7) | copy-start | bytes 1540
  7.3 9.5 %collective-permute-start.4 = (bf16[2,2,2,128,128]{4,3,2,1,0:T(8,128)(2,1)S(1)}, bf16[2,2,2,128,128]{4,3,2,1,0:T(8,128)(2,1)S(1)}, u32[]{:S(2)}, u32[]{:S(2)}) collective-permute-start(bf16[2,2,2,128,128]{4,3,2,1,0:T(8,128)(2,1)S(1)} %shard_map.74), channel_id=1, source_target_pairs={{0,2},{1,3},{2,0},{3,1},{4,6},{5,7},{6,4},{7,5},{8,10},{9,11},{10,... | collective-permute-start | bytes 786440 | tf_op jit(solution)/shard_map/ppermute | solution.py:328
  10.2 5.7 %collective-permute-start.2 = (bf16[16,128]{1,0:T(8,128)(2,1)S(1)}, bf16[16,128]{1,0:T(8,128)(2,1)S(1)}, u32[]{:S(2)}, u32[]{:S(2)}) collective-permute-start(bf16[16,128]{1,0:T(8,128)(2,1)S(1)} %fusion.4.refs_0_.refs_1_), channel_id=1, source_target_pairs={{0,1},{1,0},{2,3},{3,2},{4,5},{5,4},{6,7},{7,6},{8,9},{9,8},{10,11... | collective-permute-start | bytes 12296 | tf_op jit(solution)/shard_map/ppermute | solution.py:328
  15.4 7.0 %collective-permute-start.8 = (bf16[2,2,2,128,128]{4,3,2,1,0:T(8,128)(2,1)S(1)}, bf16[2,2,2,128,128]{4,3,2,1,0:T(8,128)(2,1)S(1)}, u32[]{:S(2)}, u32[]{:S(2)}) collective-permute-start(bf16[2,2,2,128,128]{4,3,2,1,0:T(8,128)(2,1)S(1)} %get-tuple-element.53), channel_id=1, source_target_pairs={{0,1},{1,0},{2,3},{3,2},{4,5},{5,4},{6,7},{7,6},{8,9},{9,8},{10,11... | collective-permute-start | bytes 786440 | tf_op jit(solution)/shard_map/ppermute | solution.py:328
  17.0 7.9 %collective-permute-start.9 = (bf16[2,2,2,128,128]{4,3,2,1,0:T(8,128)(2,1)S(1)}, bf16[2,2,2,128,128]{4,3,2,1,0:T(8,128)(2,1)S(1)}, u32[]{:S(2)}, u32[]{:S(2)}) collective-permute-start(bf16[2,2,2,128,128]{4,3,2,1,0:T(8,128)(2,1)S(1)} %shard_map.78), channel_id=1, source_target_pairs={{0,2},{1,3},{2,0},{3,1},{4,6},{5,7},{6,4},{7,5},{8,10},{9,11},{10,... | collective-permute-start | bytes 786440 | tf_op jit(solution)/shard_map/ppermute | solution.py:328
  18.8 8.4 %collective-permute-start.5 = (bf16[2,272,128]{2,1,0:T(8,128)(2,1)S(1)}, bf16[2,272,128]{2,1,0:T(8,128)(2,1)S(1)}, u32[]{:S(2)}, u32[]{:S(2)}) collective-permute-start(bf16[2,272,128]{2,1,0:T(8,128)(2,1)S(1)} %get-tuple-element.50), channel_id=1, source_target_pairs={{0,24},{1,29},{2,26},{3,31},{4,28},{5,25},{6,30},{7,27},{8,16},{9,... | collective-permute-start | bytes 417800 | tf_op jit(solution)/shard_map/ppermute | solution.py:333
  22.4 11.9 %collective-permute-start.6 = (bf16[2,272,128]{2,1,0:T(8,128)(2,1)S(1)}, bf16[2,272,128]{2,1,0:T(8,128)(2,1)S(1)}, u32[]{:S(2)}, u32[]{:S(2)}) collective-permute-start(bf16[2,272,128]{2,1,0:T(8,128)(2,1)S(1)} %get-tuple-element.51), channel_id=1, source_target_pairs={{0,16},{1,21},{2,18},{3,23},{4,20},{5,17},{6,22},{7,19},{8,24},{9,... | collective-permute-start | bytes 417800 | tf_op jit(solution)/shard_map/ppermute | solution.py:333
  25.0 9.4 %collective-permute-start.10 = (bf16[2,272,128]{2,1,0:T(8,128)(2,1)S(1)}, bf16[2,272,128]{2,1,0:T(8,128)(2,1)S(1)}, u32[]{:S(2)}, u32[]{:S(2)}) collective-permute-start(bf16[2,272,128]{2,1,0:T(8,128)(2,1)S(1)} %get-tuple-element.56), channel_id=1, source_target_pairs={{0,8},{1,13},{2,10},{3,15},{4,12},{5,9},{6,14},{7,11},{8,0},{9,5},... | collective-permute-start | bytes 417800 | tf_op jit(solution)/shard_map/ppermute | solution.py:333
  26.6 7.9 %collective-permute-start.11 = (bf16[2,272,128]{2,1,0:T(8,128)(2,1)S(1)}, bf16[2,272,128]{2,1,0:T(8,128)(2,1)S(1)}, u32[]{:S(2)}, u32[]{:S(2)}) collective-permute-start(bf16[2,272,128]{2,1,0:T(8,128)(2,1)S(1)} %get-tuple-element.57), channel_id=1, source_target_pairs={{0,0},{1,5},{2,2},{3,7},{4,4},{5,1},{6,6},{7,3},{8,8},{9,13},{10,1... | collective-permute-start | bytes 417800 | tf_op jit(solution)/shard_map/ppermute | solution.py:333
  34.3 1.4 %collective-permute-start.7 = (bf16[2,272,128]{2,1,0:T(8,128)(2,1)S(1)}, bf16[2,272,128]{2,1,0:T(8,128)(2,1)S(1)}, u32[]{:S(2)}, u32[]{:S(2)}) collective-permute-start(bf16[2,272,128]{2,1,0:T(8,128)(2,1)S(1)} %shard_map.77), channel_id=1, source_target_pairs={{0,1},{1,0},{2,3},{3,2},{4,5},{5,4},{6,7},{7,6},{8,9},{9,8},{10,11... | collective-permute-start | bytes 417800 | tf_op jit(solution)/shard_map/ppermute | solution.py:328
  34.5 1.5 %collective-permute-start.12 = (bf16[2,272,128]{2,1,0:T(8,128)(2,1)S(1)}, bf16[2,272,128]{2,1,0:T(8,128)(2,1)S(1)}, u32[]{:S(2)}, u32[]{:S(2)}) collective-permute-start(bf16[2,272,128]{2,1,0:T(8,128)(2,1)S(1)} %shard_map.80), channel_id=1, source_target_pairs={{0,1},{1,0},{2,3},{3,2},{4,5},{5,4},{6,7},{7,6},{8,9},{9,8},{10,11... | collective-permute-start | bytes 417800 | tf_op jit(solution)/shard_map/ppermute | solution.py:328
  40.9 2.4 %collective-permute-start.16 = (bf16[2,2,128,128]{3,2,1,0:T(8,128)(2,1)S(1)}, bf16[2,2,128,128]{3,2,1,0:T(8,128)(2,1)S(1)}, u32[]{:S(2)}, u32[]{:S(2)}) collective-permute-start(bf16[2,2,128,128]{3,2,1,0:T(8,128)(2,1)S(1)} %get-tuple-element.64), channel_id=1, source_target_pairs={{0,1},{1,0},{2,3},{3,2},{4,5},{5,4},{6,7},{7,6},{8,9},{9,8},{10,11... | collective-permute-start | bytes 393224 | tf_op jit(solution)/shard_map/ppermute | solution.py:328
  43.1 1.4 %collective-permute-start.13 = (bf16[2,2,128,128]{3,2,1,0:T(8,128)(2,1)S(1)}, bf16[2,2,128,128]{3,2,1,0:T(8,128)(2,1)S(1)}, u32[]{:S(2)}, u32[]{:S(2)}) collective-permute-start(bf16[2,2,128,128]{3,2,1,0:T(8,128)(2,1)S(1)} %get-tuple-element.60), channel_id=1, source_target_pairs={{0,1},{1,0},{2,3},{3,2},{4,5},{5,4},{6,7},{7,6},{8,9},{9,8},{10,11... | collective-permute-start | bytes 393224 | tf_op jit(solution)/shard_map/ppermute | solution.py:328
  43.4 5.8 %collective-permute-start.17 = (bf16[2,2,128,128]{3,2,1,0:T(8,128)(2,1)S(1)}, bf16[2,2,128,128]{3,2,1,0:T(8,128)(2,1)S(1)}, u32[]{:S(2)}, u32[]{:S(2)}) collective-permute-start(bf16[2,2,128,128]{3,2,1,0:T(8,128)(2,1)S(1)} %get-tuple-element.65), channel_id=1, source_target_pairs={{0,8},{1,13},{2,10},{3,15},{4,12},{5,9},{6,14},{7,11},{8,0},{9,5},... | collective-permute-start | bytes 393224 | tf_op jit(solution)/shard_map/ppermute | solution.py:333
  43.4 5.7 %collective-permute-start.18 = (bf16[2,2,128,128]{3,2,1,0:T(8,128)(2,1)S(1)}, bf16[2,2,128,128]{3,2,1,0:T(8,128)(2,1)S(1)}, u32[]{:S(2)}, u32[]{:S(2)}) collective-permute-start(bf16[2,2,128,128]{3,2,1,0:T(8,128)(2,1)S(1)} %get-tuple-element.66), channel_id=1, source_target_pairs={{0,0},{1,5},{2,2},{3,7},{4,4},{5,1},{6,6},{7,3},{8,8},{9,13},{10,1... | collective-permute-start | bytes 393224 | tf_op jit(solution)/shard_map/ppermute | solution.py:333
  44.6 6.9 %collective-permute-start.14 = (bf16[2,2,128,128]{3,2,1,0:T(8,128)(2,1)S(1)}, bf16[2,2,128,128]{3,2,1,0:T(8,128)(2,1)S(1)}, u32[]{:S(2)}, u32[]{:S(2)}) collective-permute-start(bf16[2,2,128,128]{3,2,1,0:T(8,128)(2,1)S(1)} %get-tuple-element.61), channel_id=1, source_target_pairs={{0,24},{1,29},{2,26},{3,31},{4,28},{5,25},{6,30},{7,27},{8,16},{9,... | collective-permute-start | bytes 393224 | tf_op jit(solution)/shard_map/ppermute | solution.py:333
  47.1 12.4 %collective-permute-start.15 = (bf16[2,2,128,128]{3,2,1,0:T(8,128)(2,1)S(1)}, bf16[2,2,128,128]{3,2,1,0:T(8,128)(2,1)S(1)}, u32[]{:S(2)}, u32[]{:S(2)}) collective-permute-start(bf16[2,2,128,128]{3,2,1,0:T(8,128)(2,1)S(1)} %get-tuple-element.62), channel_id=1, source_target_pairs={{0,16},{1,21},{2,18},{3,23},{4,20},{5,17},{6,22},{7,19},{8,24},{9,... | collective-permute-start | bytes 393224 | tf_op jit(solution)/shard_map/ppermute | solution.py:333
  49.1 12.7 %slice-start = ((s8[8388608]{0:T(1024)(128)(4,1)}), s8[4194304]{0:T(1024)(128)(4,1)S(1)}, s32[]{:S(2)}) async-start(s8[8388608]{0:T(1024)(128)(4,1)} %bitcast.8), calls=%async_computation | async-start | bytes 8388608
  49.2 12.7 %slice-start.1 = ((s8[8388608]{0:T(1024)(128)(4,1)}), s8[4194304]{0:T(1024)(128)(4,1)S(1)}, s32[]{:S(2)}) async-start(s8[8388608]{0:T(1024)(128)(4,1)} %bitcast.8), calls=%async_computation.1 | async-start | bytes 8388608
  49.2 10.4 %collective-permute-start.19 = (bf16[2,2,2,128,128]{4,3,2,1,0:T(8,128)(2,1)S(1)}, bf16[2,2,2,128,128]{4,3,2,1,0:T(8,128)(2,1)S(1)}, u32[]{:S(2)}, u32[]{:S(2)}) collective-permute-start(bf16[2,2,2,128,128]{4,3,2,1,0:T(8,128)(2,1)S(1)} %shard_map.87.rest_0_), channel_id=1, source_target_pairs={{0,1},{1,0},{2,3},{3,2},{4,5},{5,4},{6,7},{7,6},{8,9},{9,8},{10,11... | collective-permute-start | bytes 786440 | tf_op jit(solution)/shard_map/ppermute | solution.py:328
  50.8 9.6 %collective-permute-start.21 = (bf16[2,2,2,128,128]{4,3,2,1,0:T(8,128)(2,1)S(1)}, bf16[2,2,2,128,128]{4,3,2,1,0:T(8,128)(2,1)S(1)}, u32[]{:S(2)}, u32[]{:S(2)}) collective-permute-start(bf16[2,2,2,128,128]{4,3,2,1,0:T(8,128)(2,1)S(1)} %shard_map.87.rest_0_), channel_id=1, source_target_pairs={{0,2},{1,3},{2,0},{3,1},{4,6},{5,7},{6,4},{7,5},{8,10},{9,11},{10,... | collective-permute-start | bytes 786440 | tf_op jit(solution)/shard_map/ppermute | solution.py:328
  59.6 1.9 %collective-permute-start.23 = (bf16[2,2,2,128,128]{4,3,2,1,0:T(8,128)(2,1)S(1)}, bf16[2,2,2,128,128]{4,3,2,1,0:T(8,128)(2,1)S(1)}, u32[]{:S(2)}, u32[]{:S(2)}) collective-permute-start(bf16[2,2,2,128,128]{4,3,2,1,0:T(8,128)(2,1)S(1)} %shard_map.84.rest_1_), channel_id=1, source_target_pairs={{0,1},{1,0},{2,3},{3,2},{4,5},{5,4},{6,7},{7,6},{8,9},{9,8},{10,11... | collective-permute-start | bytes 786440 | tf_op jit(solution)/shard_map/ppermute | solution.py:328
  60.3 1.5 %collective-permute-start.22 = (bf16[2,2,2,128,128]{4,3,2,1,0:T(8,128)(2,1)S(1)}, bf16[2,2,2,128,128]{4,3,2,1,0:T(8,128)(2,1)S(1)}, u32[]{:S(2)}, u32[]{:S(2)}) collective-permute-start(bf16[2,2,2,128,128]{4,3,2,1,0:T(8,128)(2,1)S(1)} %collective-permute-done.21.rest_2_), channel_id=1, source_target_pairs={{0,1},{1,0},{2,3},{3,2},{4,5},{5,4},{6,7},{7,6},{8,9},{9,8},{10,11... | collective-permute-start | bytes 786440 | tf_op jit(solution)/shard_map/ppermute | solution.py:328
  60.4 8.7 %collective-permute-start.20 = (bf16[2,2,2,128,128]{4,3,2,1,0:T(8,128)(2,1)S(1)}, bf16[2,2,2,128,128]{4,3,2,1,0:T(8,128)(2,1)S(1)}, u32[]{:S(2)}, u32[]{:S(2)}) collective-permute-start(bf16[2,2,2,128,128]{4,3,2,1,0:T(8,128)(2,1)S(1)} %shard_map.84.rest_1_), channel_id=1, source_target_pairs={{0,2},{1,3},{2,0},{3,1},{4,6},{5,7},{6,4},{7,5},{8,10},{9,11},{10,... | collective-permute-start | bytes 786440 | tf_op jit(solution)/shard_map/ppermute | solution.py:328
  69.1 1.5 %collective-permute-start.24 = (bf16[2,2,2,128,128]{4,3,2,1,0:T(8,128)(2,1)S(1)}, bf16[2,2,2,128,128]{4,3,2,1,0:T(8,128)(2,1)S(1)}, u32[]{:S(2)}, u32[]{:S(2)}) collective-permute-start(bf16[2,2,2,128,128]{4,3,2,1,0:T(8,128)(2,1)S(1)} %collective-permute-done.20.rest_0_), channel_id=1, source_target_pairs={{0,1},{1,0},{2,3},{3,2},{4,5},{5,4},{6,7},{7,6},{8,9},{9,8},{10,11... | collective-permute-start | bytes 786440 | tf_op jit(solution)/shard_map/ppermute | solution.py:328

commit v3 on v0

v3 whole, which is shorter than its diff:
```python
import functools

import jax
import jax.numpy as jnp
from jax import lax
from jax.experimental import pallas as pl
from jax.experimental.pallas import tpu as pltpu
from jax.sharding import PartitionSpec as P

F32 = jnp.float32
BF16 = jnp.bfloat16
SMEM = pl.BlockSpec(memory_space=pltpu.SMEM)
VMEM = pl.BlockSpec(memory_space=pltpu.VMEM)
ANY = pl.BlockSpec(memory_space=pl.ANY)
COST = pl.CostEstimate(flops=10000000000, bytes_accessed=1000000, transcendentals=0)
PARAMS = pltpu.CompilerParams(vmem_limit_bytes=16 << 20)


def turned(v):
    half = v.shape[-1] // 2
    return jnp.concatenate([-v[..., half:], v[..., :half]], axis=-1)


def turned_rows(v):
    half = v.shape[0] // 2
    return jnp.concatenate([-v[half:], v[:half]], axis=0)


def dot(a, b):
    return jnp.dot(a, b, preferred_element_type=F32)


def xor(a, b):
    return lax.bitwise_xor(a, jnp.int32(b))


def place(at_ref, planes, rel, base, core):
    turn = lax.bitwise_and(xor(at_ref[1], rel), jnp.int32(1))
    q = lax.bitwise_xor(xor(at_ref[0], base % planes), turn)
    return q, xor(at_ref[1], rel ^ core), xor(at_ref[2], base // planes)


def up_kernel(groups, at_ref, dir_ref, coef_hbm, mat_hbm, table_hbm, *rest):
    outs, (coef_ref, mat_ref, coef_sem, mat_sem) = rest[:-4], rest[-4:]
    children, planes, fam, nz, per = mat_hbm.shape[:5]

    coef_copy = pltpu.make_async_copy(coef_hbm, coef_ref, coef_sem)
    coef_copy.start()
    slots, flying = {}, []

    def start(group):
        copies = []
        for _, _, rel, bases in group:
            for base, core in [(base, core) for base in bases for core in range(2)]:
                key = (rel, core, base % planes)
                if key not in slots:
                    slots[key] = slot = len(slots)
                    q, j, _ = place(at_ref, planes, rel, base, core)
                    copies.append(pltpu.make_async_copy(mat_hbm.at[:, q, j], mat_ref.at[slot], mat_sem.at[slot]))
                    copies[-1].start()
        flying.append(copies)

    for group in groups[:2]:
        start(group)
    coef_copy.wait()
    for number, group in enumerate(groups):
        for copy in flying[number]:
            copy.wait()
        if number + 2 < len(groups):
            start(groups[number + 2])
        elif number + 2 == len(groups):
            table_copy = pltpu.make_async_copy(table_hbm.at[pl.ds(at_ref[2] * per, per)], outs[-1], coef_sem)
            table_copy.start()
        for out, offset, rel, bases in group:
            for n, core in [(n, core) for n in range(len(bases)) for core in range(2)]:
                q, j, z = place(at_ref, planes, rel, bases[n], core)
                slot = slots[rel, core, bases[n] % planes]
                for m in range(per):
                    left, right = [], []
                    for c in range(children):
                        v = coef_ref[c, dir_ref[c, ((q * fam + j) * nz + z) * per + m]]
                        left += [mat_ref[slot, c, z, m, 0], mat_ref[slot, c, z, m, 1]]
                        right += [v, turned(v)]
                    total = dot(jnp.concatenate(left, axis=1), jnp.concatenate(right, axis=0))
                    outs[out][offset + n, core, m] = total.astype(BF16)
    table_copy.wait()


def up(at, dirs, coef, mats, table, chunks, outs, groups):
    children, planes, fam, nz, per, _, rank, _ = mats.shape
    width = coef.shape[-1]
    where, shapes = {}, []
    for n, names in enumerate(outs):
        size = 0
        for c, rel in names:
            where[c, rel] = (n, size)
            size += len(chunks[c])
        shapes.append(jax.ShapeDtypeStruct((size, 2, per, rank, width), BF16))
    jobs = [[where[c, rel] + (rel, chunks[c]) for c, rel in group] for group in groups]
    slots = 2 * fam * len({base % planes for bases in chunks for base in bases})
    *found, table = pl.pallas_call(
        functools.partial(up_kernel, jobs),
        out_shape=shapes + [jax.ShapeDtypeStruct((per,) + table.shape[1:], BF16)],
        in_specs=[SMEM, SMEM, ANY, ANY, ANY],
        out_specs=[VMEM] * (len(outs) + 1),
        scratch_shapes=[
            pltpu.VMEM(coef.shape, BF16),
            pltpu.VMEM((slots, children, nz, per, 2, rank, rank), BF16),
            pltpu.SemaphoreType.DMA,
            pltpu.SemaphoreType.DMA((slots,)),
        ],
        compiler_params=PARAMS,
        cost_estimate=COST,
    )(at, dirs, *[pltpu.with_memory_space_constraint(x, pltpu.HBM) for x in (coef, mats, table)])
    return {name: (found[n], offset) for name, (n, offset) in where.items()}, found, table


def total_of(refs, offsets, count):
    total = None
    for ref, offset in zip(refs, offsets):
        term = ref[offset : offset + count].astype(F32)
        total = term if total is None else total + term
    return total.astype(BF16)


def add_kernel(offsets, *refs):
    refs[-1][...] = total_of(refs[:-1], offsets, refs[-1].shape[0])


def add(pieces, count):
    return pl.pallas_call(
        functools.partial(add_kernel, tuple(offset for _, offset in pieces)),
        out_shape=jax.ShapeDtypeStruct((count,) + pieces[0][0].shape[1:], BF16),
        in_specs=[VMEM] * len(pieces),
        out_specs=VMEM,
        compiler_params=PARAMS,
        cost_estimate=COST,
    )(*[array for array, _ in pieces])


def part_kernel(offsets, *refs):
    lists, outs = refs[:2], refs[2 + len(offsets) :]
    total = total_of(refs[2 : 2 + len(offsets)], offsets, len(outs))
    rows = total.shape[2] * total.shape[3]
    for n, out in enumerate(outs):
        for core in range(2):
            out[core, :rows] = total[n, core].reshape(rows, total.shape[4])
            out[core, rows:] = lists[core][...]


def part(pieces, count, lists):
    _, _, per, rank, width = pieces[0][0].shape
    return pl.pallas_call(
        functools.partial(part_kernel, tuple(offset for _, offset in pieces)),
        out_shape=[jax.ShapeDtypeStruct((2, per * rank + lists[0].shape[0], width), BF16)] * count,
        in_specs=[VMEM] * (2 + len(pieces)),
        out_specs=[VMEM] * count,
        compiler_params=PARAMS,
        cost_estimate=COST,
    )(*lists, *[array for array, _ in pieces])


def stack_kernel(core, *refs):
    for n, ref in enumerate(refs[:-1]):
        refs[-1][n] = ref[...] if core is None else ref[core]


def stack(arrays, core=None):
    shape = arrays[0].shape if core is None else arrays[0].shape[1:]
    return pl.pallas_call(
        functools.partial(stack_kernel, core),
        out_shape=jax.ShapeDtypeStruct((len(arrays),) + shape, arrays[0].dtype),
        in_specs=[VMEM] * len(arrays),
        out_specs=VMEM,
        compiler_params=PARAMS,
        cost_estimate=COST,
    )(*arrays)


def join_kernel(own_ref, other_ref, *outs):
    for n, out in enumerate(outs):
        out[0] = own_ref[n]
        out[1] = other_ref[n]


def join(own, other):
    return pl.pallas_call(
        join_kernel,
        out_shape=[jax.ShapeDtypeStruct((2,) + own.shape[1:], own.dtype)] * own.shape[0],
        in_specs=[VMEM] * 2,
        out_specs=[VMEM] * own.shape[0],
        compiler_params=PARAMS,
        cost_estimate=COST,
    )(own, other)


def couple_kernel(sizes, at_ref, table_ref, own_ref, *refs):
    planes, nz, most, held, chunks = sizes
    sources, (theirs_ref, mine_ref, wide, numbers, lists, sem) = refs[:-6], refs[-6:]
    me = lax.bitwise_and(at_ref[1], jnp.int32(1))
    per, _, _, rank, _ = table_ref.shape
    count = wide.shape[0] - 1
    held_by, pos = {}, 0
    for bases in chunks:
        for n, base in enumerate(bases):
            held_by[base] = (sources[pos + n].at[0], sources[pos + len(bases)].at[n])
        pos += len(bases) + 1
    gathered = sources[pos:]
    numbers[0] = own_ref[...].astype(F32).astype(jnp.int32)
    for z in range(1, nz):
        mine, theirs = (ref[per * rank :].astype(F32) for ref in held_by[z * planes])
        numbers[z] = jnp.where(me == 0, mine, theirs).astype(jnp.int32)
    copy = pltpu.make_async_copy(numbers, lists, sem)
    copy.start()
    parts = []
    if gathered:
        parts = [(t, gathered[0].at[t]) for t in range(gathered[0].shape[0])]
    else:
        for base, pair in held_by.items():
            for s, source in enumerate(pair):
                q = lax.bitwise_xor(xor(at_ref[0], base % planes), xor(me, s))
                parts.append((xor(at_ref[2], base // planes) * planes + q, source))
    for t, source in parts:
        for m in range(per):
            v = source[m * rank : (m + 1) * rank]
            wide[t, m, :rank] = v
            wide[t, m, rank:] = turned(v)
    wide[count] = jnp.zeros_like(wide[count])
    copy.wait()
    for row, s in ((theirs_ref, 1), (mine_ref, 0)):
        for n, base in enumerate(base for bases in chunks for base in bases):
            q, z = lax.bitwise_xor(xor(at_ref[0], base % planes), xor(me, s)), at_ref[2]
            for m in range(per):
                entry = (base // planes, q * held + z * per + m)
                active = lists[entry + (2 * most,)]
                total = None
                for k in range(most):
                    kind = lists[entry + (most + k,)]
                    source = jnp.where(k < active, lists[entry + (k,)], count)
                    both = jnp.concatenate([table_ref[m, kind, 0], table_ref[m, kind, 1]], axis=1)
                    term = dot(both, wide[source, m])
                    total = term if total is None else total + term
                row[n, m] = total.T.astype(BF16)


def couple(at, table, own, sources, sizes, total):
    per, _, _, rank, _ = table.shape
    width = sources[0].shape[-1]
    listed = (sizes[1],) + own.shape
    rows = sum(len(bases) for bases in sizes[-1])
    return pl.pallas_call(
        functools.partial(couple_kernel, sizes),
        out_shape=[jax.ShapeDtypeStruct((rows, per, width, rank), BF16)] * 2,
        in_specs=[SMEM] + [VMEM] * (2 + len(sources)),
        out_specs=[VMEM] * 2,
        scratch_shapes=[
            pltpu.VMEM((total + 1, per, 2 * rank, width), BF16),
            pltpu.VMEM(listed, jnp.int32),
            pltpu.SMEM(listed, jnp.int32),
            pltpu.SemaphoreType.DMA,
        ],
        compiler_params=PARAMS,
        cost_estimate=COST,
    )(at, table, own, *sources)


def down_kernel(jobs, last, at_ref, dir_ref, mat_ref, *rest):
    pieces = rest[: len(jobs)]
    if last:
        before, out_ref, sums = rest[len(jobs) :]
    else:
        (sums,) = rest[len(jobs) :]
    children, planes, fam, nz, per, _, rank, _ = mat_ref.shape
    sums[...] = jnp.zeros_like(sums)
    for piece, (rel, bases) in zip(pieces, jobs):
        for n, core in [(n, core) for n in range(len(bases)) for core in range(2)]:
            q, j, z = place(at_ref, planes, rel, bases[n], core)
            for m in range(per):
                e = ((q * fam + j) * nz + z) * per + m
                v = piece[n, core, m]
                x = jnp.concatenate([v, turned_rows(v)], axis=1)
                both = [mat_ref[c, q, j, z, m].reshape(2 * rank, rank) for c in range(children)]
                y = dot(x, jnp.concatenate(both, axis=1))
                for c in range(children):
                    sums[c, dir_ref[c, e]] += y[:, c * rank : (c + 1) * rank]
    if last:
        for c in range(children):
            for i in range(out_ref.shape[1]):
                out_ref[c, i] = (sums[c, i] + before[c, i]).T.astype(BF16)


def down(at, dirs, mats, jobs, pieces, groups, before=None):
    children, rank = mats.shape[0], mats.shape[-1]
    width = pieces[0].shape[-2]
    last = before is not None
    sums = (children, groups, width, rank)
    return pl.pallas_call(
        functools.partial(down_kernel, jobs, last),
        out_shape=jax.ShapeDtypeStruct((children, groups, rank, width), BF16) if last else jax.ShapeDtypeStruct(sums, F32),
        in_specs=[SMEM, SMEM] + [VMEM] * (1 + len(pieces) + (1 if last else 0)),
        out_specs=VMEM,
        scratch_shapes=[pltpu.VMEM(sums, F32)] if last else [],
        compiler_params=PARAMS,
        cost_estimate=COST,
    )(at, dirs, mats, *pieces, *([before] if last else []))


def body(nx, ny, child_coef, transfer, child_dir, couple_src, couple_kind, couple_count, couple_table):
    children, dirs, _, rank, _ = transfer.shape
    planes, held, most = couple_src.shape
    fam = ny // planes
    split = held % nx == 0
    nz = nx if split else 1
    per = held // nz
    partners = nz * planes
    at_y, at_x = lax.axis_index("gy"), lax.axis_index("gx")
    at = jnp.stack([at_y // fam, at_y % fam, at_x if split else jnp.zeros_like(at_x)]).astype(jnp.int32)
    mats = transfer.reshape(children, planes, fam, nz, per, 2, rank, rank)
    bases = tuple(range(partners - 2, -1, -2))
    half = len(bases) // 2
    chunks = tuple((base,) for base in bases[:half]) + (bases[half:],)

    def family(x, rel):
        return lax.ppermute(x, "gy", [(i, i ^ rel) for i in range(ny)])

    def partner(x, base):
        moves = [(r // planes) * ny + (r % planes) * fam for r in (base, base ^ 1)]
        axes, size = (("gx", "gy"), nx * ny) if split else ("gy", ny)
        return lax.ppermute(x, axes, [(i, i ^ moves[i & 1]) for i in range(size)])

    nearest = len(chunks) - 1
    order = range(len(chunks))
    top = fam - 1
    lead = [(c, top) for c in order[:-1]]
    rest = [(c, rel) for c in order for rel in range(1, fam, 2) if (c, rel) not in lead]
    keep = [(c, rel) for rel in range(fam - 2, -1, -2) for c in order]
    groups = [[(c, rel) for c in order] for rel in sorted(range(fam), key=lambda r: (-r, r))]
    sums, found, table = up(at, child_dir, child_coef, mats, couple_table, chunks, [lead, rest] + [[k] for k in keep], groups)
    got = {key: [sums[key]] for key in keep}
    for array, names in ((found[0], lead), (found[1], rest)):
        moved = family(array, 1)
        for c, rel in names:
            got[c, rel ^ 1].append((moved, sums[c, rel][1]))
    for bit in (1 << n for n in range(1, fam.bit_length() - 1)):
        for c in order:
            for rel in range(fam - 2, 0, -2):
                if rel & -rel == bit:
                    ready = add(got.pop((c, rel)), len(chunks[c]))
                    if bit == fam // 2:
                        ready, couple_src, couple_kind, couple_count = lax.optimization_barrier(
                            (ready, couple_src, couple_kind, couple_count)
                        )
                    moved = family(ready, bit)
                    got[c, rel ^ bit].append((moved, 0))
    lists = jnp.concatenate([couple_src, couple_kind, couple_count[..., None]], axis=-1).reshape(planes * held, -1)
    lists = jnp.pad(lists, ((0, -planes * held % 16), (0, rank - lists.shape[1]))).astype(BF16)
    both_lists = (lists, family(lists, 1))
    sources = []
    for c in order:
        arrived = [partner(x, base) for x, base in zip(part(got[c, 0], len(chunks[c]), both_lists), chunks[c])]
        sources += arrived + [family(stack(arrived, core=1), 1)]
    if not split:
        own = jnp.zeros((partners,) + sources[0].shape[1:], BF16)
        pos = 0
        for chunk in chunks:
            for n, base in enumerate(chunk):
                for s, value in enumerate((sources[pos + n][0], sources[pos + len(chunk)][n])):
                    spot = lax.bitwise_xor(at[0], jnp.int32(base ^ s)) ^ (at[1] & 1)
                    own = lax.dynamic_update_index_in_dim(own, value, spot, 0)
            pos += len(chunk) + 1
        sources.append(lax.all_gather(own, "gx", axis=0, tiled=True))
    theirs, mine = couple(at, table, lists, sources, (planes, nz, most, held, chunks), nx * planes)
    local = {base: partner(x, base) for base, x in zip(bases, join(mine, family(theirs, 1)))}

    groups = child_coef.shape[1]
    pieces = {(c, 0): stack([local[base] for base in chunks[c]]) for c in order}
    bits = [1 << n for n in range(fam.bit_length() - 2, -1, -1)]
    final = nearest - 1
    for c in [nearest] + list(order[:-1]):
        for bit in bits:
            for rel in sorted(r for g, r in pieces if g == c):
                if c != final or bit == fam // 2 or not rel & (fam // 2):
                    pieces[c, rel ^ bit] = family(pieces[c, rel], bit)
    last = [(final, rel) for rel in range(fam) if rel & (fam // 2)]
    soon = [key for key in pieces if key not in last]

    def work(keys):
        return tuple((rel, chunks[c]) for c, rel in keys)

    first = down(at, child_dir, mats, work(soon), [pieces[key] for key in soon], groups)
    pieces[last[0]], first = lax.optimization_barrier((pieces[last[0]], first))
    for bit in bits[1:]:
        for rel in sorted(r for g, r in pieces if g == final and r & (fam // 2)):
            pieces[final, rel ^ bit] = family(pieces[final, rel], bit)
    return down(at, child_dir, mats, work(last), [pieces[key] for key in last], groups, before=first)


def solution(mesh):
    return jax.shard_map(
        functools.partial(body, mesh.shape["gx"], mesh.shape["gy"]),
        mesh=mesh,
        in_specs=(
            P(("gx", "gy"), None, None, None),
            P(("gx", "gy"), None, None, None, None),
            P(("gx", "gy"), None),
            P("gx", "gy", None),
            P("gx", "gy", None),
            P("gx", "gy"),
            P("gy", None, None, None, None),
        ),
        out_specs=P(("gx", "gy"), None, None, None),
        check_vma=False,
    )
```

time: 247 us -> 67.5 us (0.27)
  blocking collectives: 54.1 us -> 0 us
  local copies, waits for them, and re-layouts: 53.7 us -> 1.62 us
  matrix products: 40.8 us -> 0 us
  other arithmetic: 34.8 us -> 0.17 us
  waiting for transfers between devices: 46.1 us -> 20.1 us
  starting transfers between devices: 3.82 us -> 29.4 us
  Pallas kernels: 0 us -> 15.7 us
  between operations: 13.5 us -> 0.21 us
    all_to_all x1 -> x0, blocking collectives: 54.1 us -> none  [body(): lax.all_to_all(upward.astype(jnp.bfloat16), 'gy', split_axis=1, concat_ax...]
    dot_general x7 -> x0, matrix products: 40.8 us -> none  [the longest x3 19.5 us: complex_apply(): jnp.einsum(pattern, real_part, vectors, preferred_element_type=jnp.float32)]
    gather x6 -> x0, local copies, waits for them, and re-layouts: 33.7 us -> none  [the longest x2 19.2 us: body(): matrices = couple_table[dir_local, couple_kind]]
    ppermute x0 -> x27, starting transfers between devices: none -> 29.4 us  [the longest x19 15.5 us: family(): return lax.ppermute(x, 'gy', [(i, i ^ rel) for i in range(ny)])]
    all_gather x1 -> x0, waiting for transfers between devices: 25.7 us -> none  [body(): everything = lax.all_gather(parent, 'gx', axis=0, tiled=True)]
    all_to_all x1 -> x0, waiting for transfers between devices: 20.3 us -> none  [body(): lax.all_to_all(copies, 'gy', split_axis=0, concat_axis=1, tiled=True)[0]]
    ppermute x0 -> x27, waiting for transfers between devices: none -> 20.1 us  [the longest x19 11.5 us: family(): return lax.ppermute(x, 'gy', [(i, i ^ rel) for i in range(ny)])]
    sub x2 -> x0, other arithmetic: 18 us -> none  [complex_apply(): real_term[..., :halfway] - imag_term[..., halfway:]]
  transfers between devices with their start and end apart: 2 -> 27, of which waited for: 2 -> 14; matrix products, arithmetic and copies ran while one was open for 10% -> 1% of each run, Pallas kernels for 0% -> 4%
where the time goes in v3:
time: 67.5 us; the launch traced here: 67.1 us
  starting transfers between devices  29.4 us (44%)
  waiting for transfers between devices  20.1 us (30%)
  Pallas kernels  15.7 us (23%)
  local copies, waits for them, and re-layouts  1.62 us (2%)
    ppermute x19, starting transfers between devices, family(): return lax.ppermute(x, 'gy', [(i, i ^ rel) for i in range(ny)])  15.5 us
    ppermute x8, starting transfers between devices, partner(): return lax.ppermute(x, axes, [(i, i ^ moves[i & 1]) for i in range(size)])  13.9 us
    ppermute x19, waiting for transfers between devices, family(): return lax.ppermute(x, 'gy', [(i, i ^ rel) for i in range(ny)])  11.5 us
    ppermute x8, waiting for transfers between devices, partner(): return lax.ppermute(x, axes, [(i, i ^ moves[i & 1]) for i in range(size)])  8.53 us
    pallas_call x1, Pallas kernels, up(): pl.pallas_call(functools.partial(up_kernel, jobs), out_shape=shapes + [ja...  6.38 us
    pallas_call x2, Pallas kernels, down(): pl.pallas_call(functools.partial(down_kernel, jobs, last), out_shape=jax....  4.74 us
    pallas_call x1, Pallas kernels, couple(): pl.pallas_call(functools.partial(couple_kernel, sizes), out_shape=[jax.Sh...  4.12 us
  transfers between devices with their start and end apart: 27, of which 14 were waited for; matrix products, arithmetic and copies ran while one was open for 1% of the time, Pallas kernels for 4%

profile of v3, /device:TPU:0, one launch (start us, length us, event | category | flops | bytes accessed | tf_op | source)
XLA Modules:
  0.0 67.1 jit_solution(4635748801083971248)
XLA Ops:
  0.1 0.7 %copy-done = s32[2,64]{1,0:T(2,128)S(1)} copy-done((s32[2,64]{1,0:T(2,128)S(1)}, s32[2,64]{1,0:T(2,128)}, u32[]{:S(2)}) %copy-start) | copy-done | bytes 536
  0.8 6.4 %shard_map.73 = (bf16[2,2,2,128,128]{4,3,2,1,0:T(8,128)(2,1)S(1)}, bf16[6,2,2,128,128]{4,3,2,1,0:T(8,128)(2,1)S(1)}, bf16[1,2,2,128,128]{4,3,2,1,0:T(8,128)(2,1)...) custom-call(s32[3]{0:T(128)S(1)} %pad_add_fusion.at_ref, ...), custom_call_target="tpu_custom_call" | custom-call | flops 10000000000 | bytes 1000000 | tf_op jit(solution)/shard_map/pallas_call | solution.py:101
  7.1 0.5 collective-permute-start.1
  7.7 0.1 collective-permute-start
  7.7 1.1 %collective-permute-done.1.refs_1_ = bf16[2,2,2,128,128]{4,3,2,1,0:T(8,128)(2,1)S(1)} collective-permute-done((bf16[2,2,2,128,128]{4,3,2,1,0:T(8,128)(2,1)S(1)}, bf16[2,2,2,128,128]{4,3,2,1,0:T(8,128)(2,1)S(1)}, u32[]{:S(2)}, u32[]{:S(2)}) %collective-permute-start.1) | collective-permute-done | bytes 262176 | tf_op jit(solution)/shard_map/ppermute | solution.py:324
  8.9 2.9 %collective-permute-start.6 = (bf16[1,2,2,128,128]{4,3,2,1,0:T(8,128)(2,1)S(1)}, bf16[1,2,2,128,128]{4,3,2,1,0:T(8,128)(2,1)S(1)}, u32[]{:S(2)}, u32[]{:S(2)}) collective-permute-start(bf16[1,2,2,128,128]{4,3,2,1,0:T(8,128)(2,1)S(1)} %shard_map.75), channel_id=1, source_target_pairs={{0,2},{1,3},{2,0},{3,1},{4,6},{5,7},{6,4},{7,5},{8,10},{9,11},{10,... | collective-permute-start | bytes 393224 | tf_op jit(solution)/shard_map/ppermute | solution.py:324
  11.9 0.6 copy-done.2
  12.5 0.1 copy.11
  12.7 0.1 copy.12
  12.8 0.1 concatenate.15
  12.8 0.1 fusion.4.refs_0_.own_ref
  13.0 1.1 %collective-permute-start.3 = (bf16[1,2,2,128,128]{4,3,2,1,0:T(8,128)(2,1)S(1)}, bf16[1,2,2,128,128]{4,3,2,1,0:T(8,128)(2,1)S(1)}, u32[]{:S(2)}, u32[]{:S(2)}) collective-permute-start(bf16[1,2,2,128,128]{4,3,2,1,0:T(8,128)(2,1)S(1)} %shard_map.76), channel_id=1, source_target_pairs={{0,2},{1,3},{2,0},{3,1},{4,6},{5,7},{6,4},{7,5},{8,10},{9,11},{10,... | collective-permute-start | bytes 393224 | tf_op jit(solution)/shard_map/ppermute | solution.py:324
  14.1 1.0 %collective-permute-start.9 = (bf16[2,2,2,128,128]{4,3,2,1,0:T(8,128)(2,1)S(1)}, bf16[2,2,2,128,128]{4,3,2,1,0:T(8,128)(2,1)S(1)}, u32[]{:S(2)}, u32[]{:S(2)}) collective-permute-start(bf16[2,2,2,128,128]{4,3,2,1,0:T(8,128)(2,1)S(1)} %shard_map.74), channel_id=1, source_target_pairs={{0,2},{1,3},{2,0},{3,1},{4,6},{5,7},{6,4},{7,5},{8,10},{9,11},{10,... | collective-permute-start | bytes 786440 | tf_op jit(solution)/shard_map/ppermute | solution.py:324
  15.0 0.6 collective-permute-done.6.refs_4_
  15.7 2.9 %collective-permute-start.7 = (bf16[2,272,128]{2,1,0:T(8,128)(2,1)S(1)}, bf16[2,272,128]{2,1,0:T(8,128)(2,1)S(1)}, u32[]{:S(2)}, u32[]{:S(2)}) collective-permute-start(bf16[2,272,128]{2,1,0:T(8,128)(2,1)S(1)} %shard_map.79), channel_id=1, source_target_pairs={{0,16},{1,21},{2,18},{3,23},{4,20},{5,17},{6,22},{7,19},{8,24},{9,... | collective-permute-start | bytes 417800 | tf_op jit(solution)/shard_map/ppermute | solution.py:329
  18.6 0.7 %collective-permute-done.3.refs_4_ = bf16[1,2,2,128,128]{4,3,2,1,0:T(8,128)(2,1)S(1)} collective-permute-done((bf16[1,2,2,128,128]{4,3,2,1,0:T(8,128)(2,1)S(1)}, bf16[1,2,2,128,128]{4,3,2,1,0:T(8,128)(2,1)S(1)}, u32[]{:S(2)}, u32[]{:S(2)}) %collective-permute-start.3) | collective-permute-done | bytes 131104 | tf_op jit(solution)/shard_map/ppermute | solution.py:324
  19.4 3.7 %collective-permute-start.4 = (bf16[2,272,128]{2,1,0:T(8,128)(2,1)S(1)}, bf16[2,272,128]{2,1,0:T(8,128)(2,1)S(1)}, u32[]{:S(2)}, u32[]{:S(2)}) collective-permute-start(bf16[2,272,128]{2,1,0:T(8,128)(2,1)S(1)} %shard_map.77), channel_id=1, source_target_pairs={{0,24},{1,29},{2,26},{3,31},{4,28},{5,25},{6,30},{7,27},{8,16},{9,... | collective-permute-start | bytes 417800 | tf_op jit(solution)/shard_map/ppermute | solution.py:329
  23.0 1.4 %collective-permute-done.9.refs_4_ = bf16[2,2,2,128,128]{4,3,2,1,0:T(8,128)(2,1)S(1)} collective-permute-done((bf16[2,2,2,128,128]{4,3,2,1,0:T(8,128)(2,1)S(1)}, bf16[2,2,2,128,128]{4,3,2,1,0:T(8,128)(2,1)S(1)}, u32[]{:S(2)}, u32[]{:S(2)}) %collective-permute-start.9) | collective-permute-done | bytes 262176 | tf_op jit(solution)/shard_map/ppermute | solution.py:324
  24.5 0.1 shard_map.81
  24.6 1.6 %collective-permute-start.10 = (bf16[2,272,128]{2,1,0:T(8,128)(2,1)S(1)}, bf16[2,272,128]{2,1,0:T(8,128)(2,1)S(1)}, u32[]{:S(2)}, u32[]{:S(2)}) collective-permute-start(bf16[2,272,128]{2,1,0:T(8,128)(2,1)S(1)} %get-tuple-element.57), channel_id=1, source_target_pairs={{0,8},{1,13},{2,10},{3,15},{4,12},{5,9},{6,14},{7,11},{8,0},{9,5},... | collective-permute-start | bytes 417800 | tf_op jit(solution)/shard_map/ppermute | solution.py:329
  26.2 0.7 collective-permute-start.11
  26.9 2.2 %collective-permute-done.7.refs_0_.refs_2_ = bf16[2,272,128]{2,1,0:T(8,128)(2,1)S(1)} collective-permute-done((bf16[2,272,128]{2,1,0:T(8,128)(2,1)S(1)}, bf16[2,272,128]{2,1,0:T(8,128)(2,1)S(1)}, u32[]{:S(2)}, u32[]{:S(2)}) %collective-permute-start.7) | collective-permute-done | bytes 139296 | tf_op jit(solution)/shard_map/ppermute | solution.py:329
  29.1 2.6 %collective-permute-done.10.refs_0_.refs_4_ = bf16[2,272,128]{2,1,0:T(8,128)(2,1)S(1)} collective-permute-done((bf16[2,272,128]{2,1,0:T(8,128)(2,1)S(1)}, bf16[2,272,128]{2,1,0:T(8,128)(2,1)S(1)}, u32[]{:S(2)}, u32[]{:S(2)}) %collective-permute-start.10) | collective-permute-done | bytes 139296 | tf_op jit(solution)/shard_map/ppermute | solution.py:329
  31.7 0.7 %collective-permute-start.12 = (bf16[2,272,128]{2,1,0:T(8,128)(2,1)S(1)}, bf16[2,272,128]{2,1,0:T(8,128)(2,1)S(1)}, u32[]{:S(2)}, u32[]{:S(2)}) collective-permute-start(bf16[2,272,128]{2,1,0:T(8,128)(2,1)S(1)} %shard_map.82), channel_id=1, source_target_pairs={{0,1},{1,0},{2,3},{3,2},{4,5},{5,4},{6,7},{7,6},{8,9},{9,8},{10,11... | collective-permute-start | bytes 417800 | tf_op jit(solution)/shard_map/ppermute | solution.py:324
  32.5 0.1 collective-permute-start.5
  32.6 1.2 %collective-permute-done.5.refs_1_ = bf16[1,272,128]{2,1,0:T(8,128)(2,1)S(1)} collective-permute-done((bf16[1,272,128]{2,1,0:T(8,128)(2,1)S(1)}, bf16[1,272,128]{2,1,0:T(8,128)(2,1)S(1)}, u32[]{:S(2)}, u32[]{:S(2)}) %collective-permute-start.5) | collective-permute-done | bytes 69664 | tf_op jit(solution)/shard_map/ppermute | solution.py:324
  33.8 4.1 %shard_map.83 = (bf16[4,2,128,128]{3,2,1,0:T(8,128)(2,1)S(1)}, bf16[4,2,128,128]{3,2,1,0:T(8,128)(2,1)S(1)}) custom-call(s32[3]{0:T(128)S(1)} %pad_add_fusion.at_ref, bf16[2,8,2,128,128]{4,3,2,1,0:T(8,128)(2,1)S(1)} %get-tuple-element.36.table_ref, bf16[16,128]{1,0:T(8,128)(2,1)S(1)} %fusion.4.refs_0_.own_ref, ...), custom_call_target="tpu_custom_call" | custom-call | flops 10000000000 | bytes 1000000 | tf_op jit(solution)/shard_map/pallas_call | solution.py:251
  37.9 0.2 collective-permute-start.13
  38.1 1.4 %collective-permute-done.13.other_ref = bf16[4,2,128,128]{3,2,1,0:T(8,128)(2,1)S(1)} collective-permute-done((bf16[4,2,128,128]{3,2,1,0:T(8,128)(2,1)S(1)}, bf16[4,2,128,128]{3,2,1,0:T(8,128)(2,1)S(1)}, u32[]{:S(2)}, u32[]{:S(2)}) %collective-permute-start.13) | collective-permute-done | bytes 262176 | tf_op jit(solution)/shard_map/ppermute | solution.py:324
  39.6 0.8 %collective-permute-start.17 = (bf16[2,2,128,128]{3,2,1,0:T(8,128)(2,1)S(1)}, bf16[2,2,128,128]{3,2,1,0:T(8,128)(2,1)S(1)}, u32[]{:S(2)}, u32[]{:S(2)}) collective-permute-start(bf16[2,2,128,128]{3,2,1,0:T(8,128)(2,1)S(1)} %get-tuple-element.63), channel_id=1, source_target_pairs={{0,8},{1,13},{2,10},{3,15},{4,12},{5,9},{6,14},{7,11},{8,0},{9,5},... | collective-permute-start | bytes 393224 | tf_op jit(solution)/shard_map/ppermute | solution.py:329
  40.3 0.7 collective-permute-start.18
  41.0 3.6 %collective-permute-start.16 = (bf16[2,2,128,128]{3,2,1,0:T(8,128)(2,1)S(1)}, bf16[2,2,128,128]{3,2,1,0:T(8,128)(2,1)S(1)}, u32[]{:S(2)}, u32[]{:S(2)}) collective-permute-start(bf16[2,2,128,128]{3,2,1,0:T(8,128)(2,1)S(1)} %get-tuple-element.62), channel_id=1, source_target_pairs={{0,24},{1,29},{2,26},{3,31},{4,28},{5,25},{6,30},{7,27},{8,16},{9,... | collective-permute-start | bytes 393224 | tf_op jit(solution)/shard_map/ppermute | solution.py:329
  44.6 1.3 %collective-permute-done.17.refs_0_ = bf16[2,2,128,128]{3,2,1,0:T(8,128)(2,1)S(1)} collective-permute-done((bf16[2,2,128,128]{3,2,1,0:T(8,128)(2,1)S(1)}, bf16[2,2,128,128]{3,2,1,0:T(8,128)(2,1)S(1)}, u32[]{:S(2)}, u32[]{:S(2)}) %collective-permute-start.17) | collective-permute-done | bytes 131104 | tf_op jit(solution)/shard_map/ppermute | solution.py:329
  45.9 1.6 %collective-permute-start.19 = (bf16[2,2,2,128,128]{4,3,2,1,0:T(8,128)(2,1)S(1)}, bf16[2,2,2,128,128]{4,3,2,1,0:T(8,128)(2,1)S(1)}, u32[]{:S(2)}, u32[]{:S(2)}) collective-permute-start(bf16[2,2,2,128,128]{4,3,2,1,0:T(8,128)(2,1)S(1)} %shard_map.87.rest_2_), channel_id=1, source_target_pairs={{0,2},{1,3},{2,0},{3,1},{4,6},{5,7},{6,4},{7,5},{8,10},{9,11},{10,... | collective-permute-start | bytes 786440 | tf_op jit(solution)/shard_map/ppermute | solution.py:324
  47.5 1.2 %collective-permute-start.20 = (bf16[2,2,2,128,128]{4,3,2,1,0:T(8,128)(2,1)S(1)}, bf16[2,2,2,128,128]{4,3,2,1,0:T(8,128)(2,1)S(1)}, u32[]{:S(2)}, u32[]{:S(2)}) collective-permute-start(bf16[2,2,2,128,128]{4,3,2,1,0:T(8,128)(2,1)S(1)} %shard_map.87.rest_2_), channel_id=1, source_target_pairs={{0,1},{1,0},{2,3},{3,2},{4,5},{5,4},{6,7},{7,6},{8,9},{9,8},{10,11... | collective-permute-start | bytes 786440 | tf_op jit(solution)/shard_map/ppermute | solution.py:324
  48.7 1.4 %collective-permute-done.16.refs_0_ = bf16[2,2,128,128]{3,2,1,0:T(8,128)(2,1)S(1)} collective-permute-done((bf16[2,2,128,128]{3,2,1,0:T(8,128)(2,1)S(1)}, bf16[2,2,128,128]{3,2,1,0:T(8,128)(2,1)S(1)}, u32[]{:S(2)}, u32[]{:S(2)}) %collective-permute-start.16) | collective-permute-done | bytes 131104 | tf_op jit(solution)/shard_map/ppermute | solution.py:329
  50.2 1.6 %collective-permute-start.22 = (bf16[1,2,2,128,128]{4,3,2,1,0:T(8,128)(2,1)S(1)}, bf16[1,2,2,128,128]{4,3,2,1,0:T(8,128)(2,1)S(1)}, u32[]{:S(2)}, u32[]{:S(2)}) collective-permute-start(bf16[1,2,2,128,128]{4,3,2,1,0:T(8,128)(2,1)S(1)} %shard_map.86.rest_0_), channel_id=1, source_target_pairs={{0,2},{1,3},{2,0},{3,1},{4,6},{5,7},{6,4},{7,5},{8,10},{9,11},{10,... | collective-permute-start | bytes 393224 | tf_op jit(solution)/shard_map/ppermute | solution.py:324
  51.7 1.0 %collective-permute-start.23 = (bf16[1,2,2,128,128]{4,3,2,1,0:T(8,128)(2,1)S(1)}, bf16[1,2,2,128,128]{4,3,2,1,0:T(8,128)(2,1)S(1)}, u32[]{:S(2)}, u32[]{:S(2)}) collective-permute-start(bf16[1,2,2,128,128]{4,3,2,1,0:T(8,128)(2,1)S(1)} %shard_map.86.rest_0_), channel_id=1, source_target_pairs={{0,1},{1,0},{2,3},{3,2},{4,5},{5,4},{6,7},{7,6},{8,9},{9,8},{10,11... | collective-permute-start | bytes 393224 | tf_op jit(solution)/shard_map/ppermute | solution.py:324
  52.7 2.0 %collective-permute-done.19.rest_3_ = bf16[2,2,2,128,128]{4,3,2,1,0:T(8,128)(2,1)S(1)} collective-permute-done((bf16[2,2,2,128,128]{4,3,2,1,0:T(8,128)(2,1)S(1)}, bf16[2,2,2,128,128]{4,3,2,1,0:T(8,128)(2,1)S(1)}, u32[]{:S(2)}, u32[]{:S(2)}) %collective-permute-start.19) | collective-permute-done | bytes 262176 | tf_op jit(solution)/shard_map/ppermute | solution.py:324
  54.7 1.0 %collective-permute-start.21 = (bf16[2,2,2,128,128]{4,3,2,1,0:T(8,128)(2,1)S(1)}, bf16[2,2,2,128,128]{4,3,2,1,0:T(8,128)(2,1)S(1)}, u32[]{:S(2)}, u32[]{:S(2)}) collective-permute-start(bf16[2,2,2,128,128]{4,3,2,1,0:T(8,128)(2,1)S(1)} %collective-permute-done.19.rest_3_), channel_id=1, source_target_pairs={{0,1},{1,0},{2,3},{3,2},{4,5},{5,4},{6,7},{7,6},{8,9},{9,8},{10,11... | collective-permute-start | bytes 786440 | tf_op jit(solution)/shard_map/ppermute | solution.py:324
  55.7 1.0 %collective-permute-done.14.refs_0_ = bf16[2,2,128,128]{3,2,1,0:T(8,128)(2,1)S(1)} collective-permute-done((bf16[2,2,128,128]{3,2,1,0:T(8,128)(2,1)S(1)}, bf16[2,2,128,128]{3,2,1,0:T(8,128)(2,1)S(1)}, u32[]{:S(2)}, u32[]{:S(2)}) %collective-permute-start.14) | collective-permute-done | bytes 131104 | tf_op jit(solution)/shard_map/ppermute | solution.py:329
  56.8 0.7 %collective-permute-start.25 = (bf16[1,2,2,128,128]{4,3,2,1,0:T(8,128)(2,1)S(1)}, bf16[1,2,2,128,128]{4,3,2,1,0:T(8,128)(2,1)S(1)}, u32[]{:S(2)}, u32[]{:S(2)}) collective-permute-start(bf16[1,2,2,128,128]{4,3,2,1,0:T(8,128)(2,1)S(1)} %shard_map.85.rest_1_), channel_id=1, source_target_pairs={{0,1},{1,0},{2,3},{3,2},{4,5},{5,4},{6,7},{7,6},{8,9},{9,8},{10,11... | collective-permute-start | bytes 393224 | tf_op jit(solution)/shard_map/ppermute | solution.py:324
  57.5 0.3 collective-permute-start.24
  57.8 1.5 %collective-permute-start.15 = (bf16[1,2,2,128,128]{4,3,2,1,0:T(8,128)(2,1)S(1)}, bf16[1,2,2,128,128]{4,3,2,1,0:T(8,128)(2,1)S(1)}, u32[]{:S(2)}, u32[]{:S(2)}) collective-permute-start(bf16[1,2,2,128,128]{4,3,2,1,0:T(8,128)(2,1)S(1)} %shard_map.85.rest_1_), channel_id=1, source_target_pairs={{0,2},{1,3},{2,0},{3,1},{4,6},{5,7},{6,4},{7,5},{8,10},{9,11},{10,... | collective-permute-start | bytes 393224 | tf_op jit(solution)/shard_map/ppermute | solution.py:324
  59.4 2.4 %shard_map.88.rest_2_ = f32[2,16,128,128]{3,2,1,0:T(8,128)S(1)} custom-call(s32[3]{0:T(128)S(1)} %pad_add_fusion.at_ref, s32[2,64]{1,0:T(2,128)S(1)} %copy-done.1, bf16[2,2,4,4,2,2,128,128]{7,6,5,4,3,2,1,0:T(8,128)(2,1)S(1)} %bitcast.9, bf16[1,2,2,128,128]{4,3,2,1,0:T(8,128)(2,1)S(1)} %shard_map.86.rest_0_, ...), custom_call_target="tpu_custom_call" | custom-call | flops 10000000000 | bytes 1000000 | tf_op jit(solution)/shard_map/pallas_call | solution.py:297
  61.8 1.7 %collective-permute-done.15.rest_0_ = bf16[1,2,2,128,128]{4,3,2,1,0:T(8,128)(2,1)S(1)} collective-permute-done((bf16[1,2,2,128,128]{4,3,2,1,0:T(8,128)(2,1)S(1)}, bf16[1,2,2,128,128]{4,3,2,1,0:T(8,128)(2,1)S(1)}, u32[]{:S(2)}, u32[]{:S(2)}) %collective-permute-start.15) | collective-permute-done | bytes 131104 | tf_op jit(solution)/shard_map/ppermute | solution.py:324
  63.4 1.3 %collective-permute-done.26.rest_1_ = bf16[1,2,2,128,128]{4,3,2,1,0:T(8,128)(2,1)S(1)} collective-permute-done((bf16[1,2,2,128,128]{4,3,2,1,0:T(8,128)(2,1)S(1)}, bf16[1,2,2,128,128]{4,3,2,1,0:T(8,128)(2,1)S(1)}, u32[]{:S(2)}, u32[]{:S(2)}) %collective-permute-start.26) | collective-permute-done | bytes 131104 | tf_op jit(solution)/shard_map/ppermute | solution.py:324
  64.8 2.3 %shard_map.89 = bf16[2,16,128,128]{3,2,1,0:T(8,128)(2,1)} custom-call(s32[3]{0:T(128)S(1)} %pad_add_fusion.at_ref, s32[2,64]{1,0:T(2,128)S(1)} %copy-done.1, bf16[2,2,4,4,2,2,128,128]{7,6,5,4,3,2,1,0:T(8,128)(2,1)S(1)} %bitcast.10, bf16[1,2,2,128,128]{4,3,2,1,0:T(8,128)(2,1)S(1)} %collective-permute-done.15.rest_0_, ...), custom_call_target="tpu_custom_call" | custom-call | flops 10000000000 | bytes 1000000 | tf_op jit(solution)/shard_map/pallas_call | solution.py:297
  (46 shorter events, 0.5 us)
Async XLA Ops:
  0.1 0.7 %copy-start = (s32[2,64]{1,0:T(2,128)S(1)}, s32[2,64]{1,0:T(2,128)}, u32[]{:S(2)}) copy-start(s32[2,64]{1,0:T(2,128)} %dir_ref.5) | copy-start | bytes 1540
  7.1 1.7 %collective-permute-start.1 = (bf16[2,2,2,128,128]{4,3,2,1,0:T(8,128)(2,1)S(1)}, bf16[2,2,2,128,128]{4,3,2,1,0:T(8,128)(2,1)S(1)}, u32[]{:S(2)}, u32[]{:S(2)}) collective-permute-start(bf16[2,2,2,128,128]{4,3,2,1,0:T(8,128)(2,1)S(1)} %get-tuple-element.40), channel_id=1, source_target_pairs={{0,1},{1,0},{2,3},{3,2},{4,5},{5,4},{6,7},{7,6},{8,9},{9,8},{10,11... | collective-permute-start | bytes 786440 | tf_op jit(solution)/shard_map/ppermute | solution.py:324
  7.7 4.2 %collective-permute-start = (bf16[6,2,2,128,128]{4,3,2,1,0:T(8,128)(2,1)S(1)}, bf16[6,2,2,128,128]{4,3,2,1,0:T(8,128)(2,1)S(1)}, u32[]{:S(2)}, u32[]{:S(2)}) collective-permute-start(bf16[6,2,2,128,128]{4,3,2,1,0:T(8,128)(2,1)S(1)} %get-tuple-element.38), channel_id=1, source_target_pairs={{0,1},{1,0},{2,3},{3,2},{4,5},{5,4},{6,7},{7,6},{8,9},{9,8},{10,11... | collective-permute-start | bytes 2359304 | tf_op jit(solution)/shard_map/ppermute | solution.py:324
  8.9 6.7 %collective-permute-start.6 = (bf16[1,2,2,128,128]{4,3,2,1,0:T(8,128)(2,1)S(1)}, bf16[1,2,2,128,128]{4,3,2,1,0:T(8,128)(2,1)S(1)}, u32[]{:S(2)}, u32[]{:S(2)}) collective-permute-start(bf16[1,2,2,128,128]{4,3,2,1,0:T(8,128)(2,1)S(1)} %shard_map.75), channel_id=1, source_target_pairs={{0,2},{1,3},{2,0},{3,1},{4,6},{5,7},{6,4},{7,5},{8,10},{9,11},{10,... | collective-permute-start | bytes 393224 | tf_op jit(solution)/shard_map/ppermute | solution.py:324
  11.8 0.7 %copy-start.2 = (s32[2,8,7]{1,0,2:T(2,128)S(1)}, s32[2,8,7]{1,0,2:T(2,128)}, u32[]{:S(2)}) copy-start(s32[2,8,7]{1,0,2:T(2,128)} %param.10) | copy-start | bytes 1348
  11.8 0.8 %copy-start.3 = (s32[2,8,7]{1,0,2:T(2,128)S(1)}, s32[2,8,7]{1,0,2:T(2,128)}, u32[]{:S(2)}) copy-start(s32[2,8,7]{1,0,2:T(2,128)} %param.11) | copy-start | bytes 1348
  11.8 0.9 %copy-start.4 = (s32[2,8]{1,0:T(2,128)S(1)}, s32[2,8]{1,0:T(2,128)}, u32[]{:S(2)}) copy-start(s32[2,8]{1,0:T(2,128)} %param.12) | copy-start | bytes 196
  12.9 2.7 %collective-permute-start.2 = (bf16[16,128]{1,0:T(8,128)(2,1)S(1)}, bf16[16,128]{1,0:T(8,128)(2,1)S(1)}, u32[]{:S(2)}, u32[]{:S(2)}) collective-permute-start(bf16[16,128]{1,0:T(8,128)(2,1)S(1)} %fusion.4.refs_0_.own_ref), channel_id=1, source_target_pairs={{0,1},{1,0},{2,3},{3,2},{4,5},{5,4},{6,7},{7,6},{8,9},{9,8},{10,11... | collective-permute-start | bytes 12296 | tf_op jit(solution)/shard_map/ppermute | solution.py:324
  13.0 6.4 %collective-permute-start.3 = (bf16[1,2,2,128,128]{4,3,2,1,0:T(8,128)(2,1)S(1)}, bf16[1,2,2,128,128]{4,3,2,1,0:T(8,128)(2,1)S(1)}, u32[]{:S(2)}, u32[]{:S(2)}) collective-permute-start(bf16[1,2,2,128,128]{4,3,2,1,0:T(8,128)(2,1)S(1)} %shard_map.76), channel_id=1, source_target_pairs={{0,2},{1,3},{2,0},{3,1},{4,6},{5,7},{6,4},{7,5},{8,10},{9,11},{10,... | collective-permute-start | bytes 393224 | tf_op jit(solution)/shard_map/ppermute | solution.py:324
  14.1 10.4 %collective-permute-start.9 = (bf16[2,2,2,128,128]{4,3,2,1,0:T(8,128)(2,1)S(1)}, bf16[2,2,2,128,128]{4,3,2,1,0:T(8,128)(2,1)S(1)}, u32[]{:S(2)}, u32[]{:S(2)}) collective-permute-start(bf16[2,2,2,128,128]{4,3,2,1,0:T(8,128)(2,1)S(1)} %shard_map.74), channel_id=1, source_target_pairs={{0,2},{1,3},{2,0},{3,1},{4,6},{5,7},{6,4},{7,5},{8,10},{9,11},{10,... | collective-permute-start | bytes 786440 | tf_op jit(solution)/shard_map/ppermute | solution.py:324
  15.7 13.4 %collective-permute-start.7 = (bf16[2,272,128]{2,1,0:T(8,128)(2,1)S(1)}, bf16[2,272,128]{2,1,0:T(8,128)(2,1)S(1)}, u32[]{:S(2)}, u32[]{:S(2)}) collective-permute-start(bf16[2,272,128]{2,1,0:T(8,128)(2,1)S(1)} %shard_map.79), channel_id=1, source_target_pairs={{0,16},{1,21},{2,18},{3,23},{4,20},{5,17},{6,22},{7,19},{8,24},{9,... | collective-permute-start | bytes 417800 | tf_op jit(solution)/shard_map/ppermute | solution.py:329
  19.4 13.1 %collective-permute-start.4 = (bf16[2,272,128]{2,1,0:T(8,128)(2,1)S(1)}, bf16[2,272,128]{2,1,0:T(8,128)(2,1)S(1)}, u32[]{:S(2)}, u32[]{:S(2)}) collective-permute-start(bf16[2,272,128]{2,1,0:T(8,128)(2,1)S(1)} %shard_map.77), channel_id=1, source_target_pairs={{0,24},{1,29},{2,26},{3,31},{4,28},{5,25},{6,30},{7,27},{8,16},{9,... | collective-permute-start | bytes 417800 | tf_op jit(solution)/shard_map/ppermute | solution.py:329
  24.6 7.1 %collective-permute-start.10 = (bf16[2,272,128]{2,1,0:T(8,128)(2,1)S(1)}, bf16[2,272,128]{2,1,0:T(8,128)(2,1)S(1)}, u32[]{:S(2)}, u32[]{:S(2)}) collective-permute-start(bf16[2,272,128]{2,1,0:T(8,128)(2,1)S(1)} %get-tuple-element.57), channel_id=1, source_target_pairs={{0,8},{1,13},{2,10},{3,15},{4,12},{5,9},{6,14},{7,11},{8,0},{9,5},... | collective-permute-start | bytes 417800 | tf_op jit(solution)/shard_map/ppermute | solution.py:329
  26.2 5.5 %collective-permute-start.11 = (bf16[2,272,128]{2,1,0:T(8,128)(2,1)S(1)}, bf16[2,272,128]{2,1,0:T(8,128)(2,1)S(1)}, u32[]{:S(2)}, u32[]{:S(2)}) collective-permute-start(bf16[2,272,128]{2,1,0:T(8,128)(2,1)S(1)} %get-tuple-element.58), channel_id=1, source_target_pairs={{0,0},{1,5},{2,2},{3,7},{4,4},{5,1},{6,6},{7,3},{8,8},{9,13},{10,1... | collective-permute-start | bytes 417800 | tf_op jit(solution)/shard_map/ppermute | solution.py:329
  29.1 3.5 %collective-permute-start.8 = (bf16[1,272,128]{2,1,0:T(8,128)(2,1)S(1)}, bf16[1,272,128]{2,1,0:T(8,128)(2,1)S(1)}, u32[]{:S(2)}, u32[]{:S(2)}) collective-permute-start(bf16[1,272,128]{2,1,0:T(8,128)(2,1)S(1)} %shard_map.80), channel_id=1, source_target_pairs={{0,1},{1,0},{2,3},{3,2},{4,5},{5,4},{6,7},{7,6},{8,9},{9,8},{10,11... | collective-permute-start | bytes 208904 | tf_op jit(solution)/shard_map/ppermute | solution.py:324
  31.7 2.1 %collective-permute-start.12 = (bf16[2,272,128]{2,1,0:T(8,128)(2,1)S(1)}, bf16[2,272,128]{2,1,0:T(8,128)(2,1)S(1)}, u32[]{:S(2)}, u32[]{:S(2)}) collective-permute-start(bf16[2,272,128]{2,1,0:T(8,128)(2,1)S(1)} %shard_map.82), channel_id=1, source_target_pairs={{0,1},{1,0},{2,3},{3,2},{4,5},{5,4},{6,7},{7,6},{8,9},{9,8},{10,11... | collective-permute-start | bytes 417800 | tf_op jit(solution)/shard_map/ppermute | solution.py:324
  32.5 1.3 %collective-permute-start.5 = (bf16[1,272,128]{2,1,0:T(8,128)(2,1)S(1)}, bf16[1,272,128]{2,1,0:T(8,128)(2,1)S(1)}, u32[]{:S(2)}, u32[]{:S(2)}) collective-permute-start(bf16[1,272,128]{2,1,0:T(8,128)(2,1)S(1)} %shard_map.78), channel_id=1, source_target_pairs={{0,1},{1,0},{2,3},{3,2},{4,5},{5,4},{6,7},{7,6},{8,9},{9,8},{10,11... | collective-permute-start | bytes 208904 | tf_op jit(solution)/shard_map/ppermute | solution.py:324
  37.9 1.6 %collective-permute-start.13 = (bf16[4,2,128,128]{3,2,1,0:T(8,128)(2,1)S(1)}, bf16[4,2,128,128]{3,2,1,0:T(8,128)(2,1)S(1)}, u32[]{:S(2)}, u32[]{:S(2)}) collective-permute-start(bf16[4,2,128,128]{3,2,1,0:T(8,128)(2,1)S(1)} %get-tuple-element.60), channel_id=1, source_target_pairs={{0,1},{1,0},{2,3},{3,2},{4,5},{5,4},{6,7},{7,6},{8,9},{9,8},{10,11... | collective-permute-start | bytes 786440 | tf_op jit(solution)/shard_map/ppermute | solution.py:324
  39.6 6.3 %collective-permute-start.17 = (bf16[2,2,128,128]{3,2,1,0:T(8,128)(2,1)S(1)}, bf16[2,2,128,128]{3,2,1,0:T(8,128)(2,1)S(1)}, u32[]{:S(2)}, u32[]{:S(2)}) collective-permute-start(bf16[2,2,128,128]{3,2,1,0:T(8,128)(2,1)S(1)} %get-tuple-element.63), channel_id=1, source_target_pairs={{0,8},{1,13},{2,10},{3,15},{4,12},{5,9},{6,14},{7,11},{8,0},{9,5},... | collective-permute-start | bytes 393224 | tf_op jit(solution)/shard_map/ppermute | solution.py:329
  40.3 5.6 %collective-permute-start.18 = (bf16[2,2,128,128]{3,2,1,0:T(8,128)(2,1)S(1)}, bf16[2,2,128,128]{3,2,1,0:T(8,128)(2,1)S(1)}, u32[]{:S(2)}, u32[]{:S(2)}) collective-permute-start(bf16[2,2,128,128]{3,2,1,0:T(8,128)(2,1)S(1)} %get-tuple-element.64), channel_id=1, source_target_pairs={{0,0},{1,5},{2,2},{3,7},{4,4},{5,1},{6,6},{7,3},{8,8},{9,13},{10,1... | collective-permute-start | bytes 393224 | tf_op jit(solution)/shard_map/ppermute | solution.py:329
  41.0 9.1 %collective-permute-start.16 = (bf16[2,2,128,128]{3,2,1,0:T(8,128)(2,1)S(1)}, bf16[2,2,128,128]{3,2,1,0:T(8,128)(2,1)S(1)}, u32[]{:S(2)}, u32[]{:S(2)}) collective-permute-start(bf16[2,2,128,128]{3,2,1,0:T(8,128)(2,1)S(1)} %get-tuple-element.62), channel_id=1, source_target_pairs={{0,24},{1,29},{2,26},{3,31},{4,28},{5,25},{6,30},{7,27},{8,16},{9,... | collective-permute-start | bytes 393224 | tf_op jit(solution)/shard_map/ppermute | solution.py:329
  44.6 12.2 %collective-permute-start.14 = (bf16[2,2,128,128]{3,2,1,0:T(8,128)(2,1)S(1)}, bf16[2,2,128,128]{3,2,1,0:T(8,128)(2,1)S(1)}, u32[]{:S(2)}, u32[]{:S(2)}) collective-permute-start(bf16[2,2,128,128]{3,2,1,0:T(8,128)(2,1)S(1)} %get-tuple-element.61), channel_id=1, source_target_pairs={{0,16},{1,21},{2,18},{3,23},{4,20},{5,17},{6,22},{7,19},{8,24},{9,... | collective-permute-start | bytes 393224 | tf_op jit(solution)/shard_map/ppermute | solution.py:329
  45.9 8.8 %collective-permute-start.19 = (bf16[2,2,2,128,128]{4,3,2,1,0:T(8,128)(2,1)S(1)}, bf16[2,2,2,128,128]{4,3,2,1,0:T(8,128)(2,1)S(1)}, u32[]{:S(2)}, u32[]{:S(2)}) collective-permute-start(bf16[2,2,2,128,128]{4,3,2,1,0:T(8,128)(2,1)S(1)} %shard_map.87.rest_2_), channel_id=1, source_target_pairs={{0,2},{1,3},{2,0},{3,1},{4,6},{5,7},{6,4},{7,5},{8,10},{9,11},{10,... | collective-permute-start | bytes 786440 | tf_op jit(solution)/shard_map/ppermute | solution.py:324
  47.5 11.8 %collective-permute-start.20 = (bf16[2,2,2,128,128]{4,3,2,1,0:T(8,128)(2,1)S(1)}, bf16[2,2,2,128,128]{4,3,2,1,0:T(8,128)(2,1)S(1)}, u32[]{:S(2)}, u32[]{:S(2)}) collective-permute-start(bf16[2,2,2,128,128]{4,3,2,1,0:T(8,128)(2,1)S(1)} %shard_map.87.rest_2_), channel_id=1, source_target_pairs={{0,1},{1,0},{2,3},{3,2},{4,5},{5,4},{6,7},{7,6},{8,9},{9,8},{10,11... | collective-permute-start | bytes 786440 | tf_op jit(solution)/shard_map/ppermute | solution.py:324
  50.1 9.2 %slice-start = ((s8[8388608]{0:T(1024)(128)(4,1)}), s8[4194304]{0:T(1024)(128)(4,1)S(1)}, s32[]{:S(2)}) async-start(s8[8388608]{0:T(1024)(128)(4,1)} %bitcast.7), calls=%async_computation | async-start | bytes 8388608
  50.1 9.2 %slice-start.1 = ((s8[8388608]{0:T(1024)(128)(4,1)}), s8[4194304]{0:T(1024)(128)(4,1)S(1)}, s32[]{:S(2)}) async-start(s8[8388608]{0:T(1024)(128)(4,1)} %bitcast.7), calls=%async_computation.1 | async-start | bytes 8388608
  50.2 9.2 %copy-start.1 = (s32[2,64]{1,0:T(2,128)S(1)}, s32[2,64]{1,0:T(2,128)}, u32[]{:S(2)}) copy-start(s32[2,64]{1,0:T(2,128)} %dir_ref.5) | copy-start | bytes 1540
  50.2 7.4 %collective-permute-start.22 = (bf16[1,2,2,128,128]{4,3,2,1,0:T(8,128)(2,1)S(1)}, bf16[1,2,2,128,128]{4,3,2,1,0:T(8,128)(2,1)S(1)}, u32[]{:S(2)}, u32[]{:S(2)}) collective-permute-start(bf16[1,2,2,128,128]{4,3,2,1,0:T(8,128)(2,1)S(1)} %shard_map.86.rest_0_), channel_id=1, source_target_pairs={{0,2},{1,3},{2,0},{3,1},{4,6},{5,7},{6,4},{7,5},{8,10},{9,11},{10,... | collective-permute-start | bytes 393224 | tf_op jit(solution)/shard_map/ppermute | solution.py:324
  51.7 6.1 %collective-permute-start.23 = (bf16[1,2,2,128,128]{4,3,2,1,0:T(8,128)(2,1)S(1)}, bf16[1,2,2,128,128]{4,3,2,1,0:T(8,128)(2,1)S(1)}, u32[]{:S(2)}, u32[]{:S(2)}) collective-permute-start(bf16[1,2,2,128,128]{4,3,2,1,0:T(8,128)(2,1)S(1)} %shard_map.86.rest_0_), channel_id=1, source_target_pairs={{0,1},{1,0},{2,3},{3,2},{4,5},{5,4},{6,7},{7,6},{8,9},{9,8},{10,11... | collective-permute-start | bytes 393224 | tf_op jit(solution)/shard_map/ppermute | solution.py:324
  54.7 4.6 %collective-permute-start.21 = (bf16[2,2,2,128,128]{4,3,2,1,0:T(8,128)(2,1)S(1)}, bf16[2,2,2,128,128]{4,3,2,1,0:T(8,128)(2,1)S(1)}, u32[]{:S(2)}, u32[]{:S(2)}) collective-permute-start(bf16[2,2,2,128,128]{4,3,2,1,0:T(8,128)(2,1)S(1)} %collective-permute-done.19.rest_3_), channel_id=1, source_target_pairs={{0,1},{1,0},{2,3},{3,2},{4,5},{5,4},{6,7},{7,6},{8,9},{9,8},{10,11... | collective-permute-start | bytes 786440 | tf_op jit(solution)/shard_map/ppermute | solution.py:324
  56.8 2.5 %collective-permute-start.25 = (bf16[1,2,2,128,128]{4,3,2,1,0:T(8,128)(2,1)S(1)}, bf16[1,2,2,128,128]{4,3,2,1,0:T(8,128)(2,1)S(1)}, u32[]{:S(2)}, u32[]{:S(2)}) collective-permute-start(bf16[1,2,2,128,128]{4,3,2,1,0:T(8,128)(2,1)S(1)} %shard_map.85.rest_1_), channel_id=1, source_target_pairs={{0,1},{1,0},{2,3},{3,2},{4,5},{5,4},{6,7},{7,6},{8,9},{9,8},{10,11... | collective-permute-start | bytes 393224 | tf_op jit(solution)/shard_map/ppermute | solution.py:324
  57.5 1.8 %collective-permute-start.24 = (bf16[1,2,2,128,128]{4,3,2,1,0:T(8,128)(2,1)S(1)}, bf16[1,2,2,128,128]{4,3,2,1,0:T(8,128)(2,1)S(1)}, u32[]{:S(2)}, u32[]{:S(2)}) collective-permute-start(bf16[1,2,2,128,128]{4,3,2,1,0:T(8,128)(2,1)S(1)} %collective-permute-done.22.rest_6_), channel_id=1, source_target_pairs={{0,1},{1,0},{2,3},{3,2},{4,5},{5,4},{6,7},{7,6},{8,9},{9,8},{10,11... | collective-permute-start | bytes 393224 | tf_op jit(solution)/shard_map/ppermute | solution.py:324
  57.8 5.6 %collective-permute-start.15 = (bf16[1,2,2,128,128]{4,3,2,1,0:T(8,128)(2,1)S(1)}, bf16[1,2,2,128,128]{4,3,2,1,0:T(8,128)(2,1)S(1)}, u32[]{:S(2)}, u32[]{:S(2)}) collective-permute-start(bf16[1,2,2,128,128]{4,3,2,1,0:T(8,128)(2,1)S(1)} %shard_map.85.rest_1_), channel_id=1, source_target_pairs={{0,2},{1,3},{2,0},{3,1},{4,6},{5,7},{6,4},{7,5},{8,10},{9,11},{10,... | collective-permute-start | bytes 393224 | tf_op jit(solution)/shard_map/ppermute | solution.py:324
  63.4 1.3 %collective-permute-start.26 = (bf16[1,2,2,128,128]{4,3,2,1,0:T(8,128)(2,1)S(1)}, bf16[1,2,2,128,128]{4,3,2,1,0:T(8,128)(2,1)S(1)}, u32[]{:S(2)}, u32[]{:S(2)}) collective-permute-start(bf16[1,2,2,128,128]{4,3,2,1,0:T(8,128)(2,1)S(1)} %collective-permute-done.15.rest_0_), channel_id=1, source_target_pairs={{0,1},{1,0},{2,3},{3,2},{4,5},{5,4},{6,7},{7,6},{8,9},{9,8},{10,11... | collective-permute-start | bytes 393224 | tf_op jit(solution)/shard_map/ppermute | solution.py:324

commit v4 on v3

--- a/solution.py
+++ b/solution.py
@@ -40,12 +40,14 @@
     return q, xor(at_ref[1], rel ^ core), xor(at_ref[2], base // planes)
 
 
-def up_kernel(groups, at_ref, dir_ref, coef_hbm, mat_hbm, table_hbm, *rest):
-    outs, (coef_ref, mat_ref, coef_sem, mat_sem) = rest[:-4], rest[-4:]
+def up_kernel(groups, at_ref, dir_hbm, coef_hbm, mat_hbm, table_hbm, *rest):
+    outs, (dir_ref, coef_ref, mat_ref, dir_sem, coef_sem, mat_sem) = rest[:-6], rest[-6:]
     children, planes, fam, nz, per = mat_hbm.shape[:5]
 
     coef_copy = pltpu.make_async_copy(coef_hbm, coef_ref, coef_sem)
     coef_copy.start()
+    dir_copy = pltpu.make_async_copy(dir_hbm, dir_ref, dir_sem)
+    dir_copy.start()
     slots, flying = {}, []
 
     def start(group):
@@ -63,6 +65,7 @@
     for group in groups[:2]:
         start(group)
     coef_copy.wait()
+    dir_copy.wait()
     for number, group in enumerate(groups):
         for copy in flying[number]:
             copy.wait()
@@ -101,17 +104,19 @@
     *found, table = pl.pallas_call(
         functools.partial(up_kernel, jobs),
         out_shape=shapes + [jax.ShapeDtypeStruct((per,) + table.shape[1:], BF16)],
-        in_specs=[SMEM, SMEM, ANY, ANY, ANY],
+        in_specs=[SMEM, ANY, ANY, ANY, ANY],
         out_specs=[VMEM] * (len(outs) + 1),
         scratch_shapes=[
+            pltpu.SMEM(dirs.shape, jnp.int32),
             pltpu.VMEM(coef.shape, BF16),
             pltpu.VMEM((slots, children, nz, per, 2, rank, rank), BF16),
             pltpu.SemaphoreType.DMA,
+            pltpu.SemaphoreType.DMA,
             pltpu.SemaphoreType.DMA((slots,)),
         ],
         compiler_params=PARAMS,
         cost_estimate=COST,
-    )(at, dirs, *[pltpu.with_memory_space_constraint(x, pltpu.HBM) for x in (coef, mats, table)])
+    )(at, *[pltpu.with_memory_space_constraint(x, pltpu.HBM) for x in (dirs, coef, mats, table)])
     return {name: (found[n], offset) for name, (n, offset) in where.items()}, found, table
 
 
@@ -195,16 +200,16 @@
 
 
 def couple_kernel(sizes, at_ref, table_ref, own_ref, *refs):
-    planes, nz, most, held, chunks = sizes
+    planes, nz, most, held, chunks, bases = sizes
     sources, (theirs_ref, mine_ref, wide, numbers, lists, sem) = refs[:-6], refs[-6:]
     me = lax.bitwise_and(at_ref[1], jnp.int32(1))
     per, _, _, rank, _ = table_ref.shape
     count = wide.shape[0] - 1
     held_by, pos = {}, 0
-    for bases in chunks:
-        for n, base in enumerate(bases):
-            held_by[base] = (sources[pos + n].at[0], sources[pos + len(bases)].at[n])
-        pos += len(bases) + 1
+    for chunk in chunks:
+        for n, base in enumerate(chunk):
+            held_by[base] = (sources[pos + n].at[0], sources[pos + len(chunk)].at[n])
+        pos += len(chunk) + 1
     gathered = sources[pos:]
     numbers[0] = own_ref[...].astype(F32).astype(jnp.int32)
     for z in range(1, nz):
@@ -228,7 +233,7 @@
     wide[count] = jnp.zeros_like(wide[count])
     copy.wait()
     for row, s in ((theirs_ref, 1), (mine_ref, 0)):
-        for n, base in enumerate(base for bases in chunks for base in bases):
+        for n, base in enumerate(bases):
             q, z = lax.bitwise_xor(xor(at_ref[0], base % planes), xor(me, s)), at_ref[2]
             for m in range(per):
                 entry = (base // planes, q * held + z * per + m)
@@ -247,7 +252,7 @@
     per, _, _, rank, _ = table.shape
     width = sources[0].shape[-1]
     listed = (sizes[1],) + own.shape
-    rows = sum(len(bases) for bases in sizes[-1])
+    rows = len(sizes[-1])
     return pl.pallas_call(
         functools.partial(couple_kernel, sizes),
         out_shape=[jax.ShapeDtypeStruct((rows, per, width, rank), BF16)] * 2,
@@ -267,7 +272,7 @@
 def down_kernel(jobs, last, at_ref, dir_ref, mat_ref, *rest):
     pieces = rest[: len(jobs)]
     if last:
-        before, out_ref, sums = rest[len(jobs) :]
+        before, out_ref, sums, staged, sems = rest[len(jobs) :]
     else:
         (sums,) = rest[len(jobs) :]
     children, planes, fam, nz, per, _, rank, _ = mat_ref.shape
@@ -284,9 +289,14 @@
                 for c in range(children):
                     sums[c, dir_ref[c, e]] += y[:, c * rank : (c + 1) * rank]
     if last:
+        copies = []
         for c in range(children):
-            for i in range(out_ref.shape[1]):
-                out_ref[c, i] = (sums[c, i] + before[c, i]).T.astype(BF16)
+            for i in range(staged.shape[1]):
+                staged[c, i] = (sums[c, i] + before[c, i]).T.astype(BF16)
+            copies.append(pltpu.make_async_copy(staged.at[c], out_ref.at[c], sems.at[c]))
+            copies[-1].start()
+        for copy in copies:
+            copy.wait()
 
 
 def down(at, dirs, mats, jobs, pieces, groups, before=None):
@@ -298,8 +308,14 @@
         functools.partial(down_kernel, jobs, last),
         out_shape=jax.ShapeDtypeStruct((children, groups, rank, width), BF16) if last else jax.ShapeDtypeStruct(sums, F32),
         in_specs=[SMEM, SMEM] + [VMEM] * (1 + len(pieces) + (1 if last else 0)),
-        out_specs=VMEM,
-        scratch_shapes=[pltpu.VMEM(sums, F32)] if last else [],
+        out_specs=ANY if last else VMEM,
+        scratch_shapes=[
+            pltpu.VMEM(sums, F32),
+            pltpu.VMEM((children, groups, rank, width), BF16),
+            pltpu.SemaphoreType.DMA((children,)),
+        ]
+        if last
+        else [],
         compiler_params=PARAMS,
         cost_estimate=COST,
     )(at, dirs, mats, *pieces, *([before] if last else []))
@@ -318,7 +334,7 @@
     mats = transfer.reshape(children, planes, fam, nz, per, 2, rank, rank)
     bases = tuple(range(partners - 2, -1, -2))
     half = len(bases) // 2
-    chunks = tuple((base,) for base in bases[:half]) + (bases[half:],)
+    chunks = tuple((base,) for pair in zip(bases[:half], bases[half:]) for base in pair)
 
     def family(x, rel):
         return lax.ppermute(x, "gy", [(i, i ^ rel) for i in range(ny)])
@@ -369,10 +385,13 @@
                     own = lax.dynamic_update_index_in_dim(own, value, spot, 0)
             pos += len(chunk) + 1
         sources.append(lax.all_gather(own, "gx", axis=0, tiled=True))
-    theirs, mine = couple(at, table, lists, sources, (planes, nz, most, held, chunks), nx * planes)
+    theirs, mine = couple(at, table, lists, sources, (planes, nz, most, held, chunks, bases), nx * planes)
     local = {base: partner(x, base) for base, x in zip(bases, join(mine, family(theirs, 1)))}
 
     groups = child_coef.shape[1]
+    chunks = tuple((base,) for base in bases[:half]) + (bases[half:],)
+    order = range(len(chunks))
+    nearest = len(chunks) - 1
     pieces = {(c, 0): stack([local[base] for base in chunks[c]]) for c in order}
     bits = [1 << n for n in range(fam.bit_length() - 2, -1, -1)]
     final = nearest - 1

time: 67.5 us -> 65.9 us (0.976)
  waiting for transfers between devices: 20.1 us -> 15.8 us
  starting transfers between devices: 29.4 us -> 32.9 us
    ppermute x19 -> x21, starting transfers between devices: 15.5 us -> 18.5 us  [family(): return lax.ppermute(x, 'gy', [(i, i ^ rel) for i in range(ny)])]
    ppermute x19 -> x21, waiting for transfers between devices: 11.5 us -> 8.67 us  [family(): return lax.ppermute(x, 'gy', [(i, i ^ rel) for i in range(ny)])]
    ppermute x8, waiting for transfers between devices: 8.53 us -> 7.12 us  [partner(): return lax.ppermute(x, axes, [(i, i ^ moves[i & 1]) for i in range(size)])]
  transfers between devices with their start and end apart: 27 -> 29, of which waited for: 14 -> 11; matrix products, arithmetic and copies ran while one was open for 1% -> 1% of each run, Pallas kernels for 4% -> 4%
where the time goes in v4:
time: 65.9 us; the launch traced here: 65.7 us
  starting transfers between devices  32.9 us (50%)
  waiting for transfers between devices  15.8 us (24%)
  Pallas kernels  15.6 us (24%)
  local copies, waits for them, and re-layouts  0.97 us (1%)
    ppermute x21, starting transfers between devices, family(): return lax.ppermute(x, 'gy', [(i, i ^ rel) for i in range(ny)])  18.5 us
    ppermute x8, starting transfers between devices, partner(): return lax.ppermute(x, axes, [(i, i ^ moves[i & 1]) for i in range(size)])  14.4 us
    ppermute x21, waiting for transfers between devices, family(): return lax.ppermute(x, 'gy', [(i, i ^ rel) for i in range(ny)])  8.67 us
    ppermute x8, waiting for transfers between devices, partner(): return lax.ppermute(x, axes, [(i, i ^ moves[i & 1]) for i in range(size)])  7.12 us
    pallas_call x1, Pallas kernels, up(): pl.pallas_call(functools.partial(up_kernel, jobs), out_shape=shapes + [ja...  6.39 us
    pallas_call x2, Pallas kernels, down(): pl.pallas_call(functools.partial(down_kernel, jobs, last), out_shape=jax....  4.6 us
    pallas_call x1, Pallas kernels, couple(): pl.pallas_call(functools.partial(couple_kernel, sizes), out_shape=[jax.Sh...  4.11 us
  transfers between devices with their start and end apart: 29, of which 11 were waited for; matrix products, arithmetic and copies ran while one was open for 1% of the time, Pallas kernels for 4%

profile of v4, /device:TPU:0, one launch (start us, length us, event | category | flops | bytes accessed | tf_op | source)
XLA Modules:
  0.0 65.7 jit_solution(1741910783043952589)
XLA Ops:
  0.0 0.1 pad_add_fusion.at_ref
  0.1 6.4 %shard_map.73 = (bf16[3,2,2,128,128]{4,3,2,1,0:T(8,128)(2,1)S(1)}, bf16[5,2,2,128,128]{4,3,2,1,0:T(8,128)(2,1)S(1)}, bf16[1,2,2,128,128]{4,3,2,1,0:T(8,128)(2,1)...) custom-call(s32[3]{0:T(128)S(1)} %pad_add_fusion.at_ref, ...), custom_call_target="tpu_custom_call" | custom-call | flops 10000000000 | bytes 1000000 | tf_op jit(solution)/shard_map/pallas_call | solution.py:104
  6.5 0.5 collective-permute-start.1
  7.0 0.1 collective-permute-start
  7.1 1.3 %collective-permute-done.1.refs_1_ = bf16[3,2,2,128,128]{4,3,2,1,0:T(8,128)(2,1)S(1)} collective-permute-done((bf16[3,2,2,128,128]{4,3,2,1,0:T(8,128)(2,1)S(1)}, bf16[3,2,2,128,128]{4,3,2,1,0:T(8,128)(2,1)S(1)}, u32[]{:S(2)}, u32[]{:S(2)}) %collective-permute-start.1) | collective-permute-done | bytes 393248 | tf_op jit(solution)/shard_map/ppermute | solution.py:340
  8.5 2.9 %collective-permute-start.9 = (bf16[1,2,2,128,128]{4,3,2,1,0:T(8,128)(2,1)S(1)}, bf16[1,2,2,128,128]{4,3,2,1,0:T(8,128)(2,1)S(1)}, u32[]{:S(2)}, u32[]{:S(2)}) collective-permute-start(bf16[1,2,2,128,128]{4,3,2,1,0:T(8,128)(2,1)S(1)} %shard_map.75), channel_id=1, source_target_pairs={{0,2},{1,3},{2,0},{3,1},{4,6},{5,7},{6,4},{7,5},{8,10},{9,11},{10,... | collective-permute-start | bytes 393224 | tf_op jit(solution)/shard_map/ppermute | solution.py:340
  11.4 0.6 copy-done.1
  12.1 0.1 copy.11
  12.2 0.1 copy.12
  12.3 0.1 concatenate.15
  12.4 0.1 fusion.4.refs_0_.own_ref
  12.5 0.9 %collective-permute-start.6 = (bf16[1,2,2,128,128]{4,3,2,1,0:T(8,128)(2,1)S(1)}, bf16[1,2,2,128,128]{4,3,2,1,0:T(8,128)(2,1)S(1)}, u32[]{:S(2)}, u32[]{:S(2)}) collective-permute-start(bf16[1,2,2,128,128]{4,3,2,1,0:T(8,128)(2,1)S(1)} %shard_map.76), channel_id=1, source_target_pairs={{0,2},{1,3},{2,0},{3,1},{4,6},{5,7},{6,4},{7,5},{8,10},{9,11},{10,... | collective-permute-start | bytes 393224 | tf_op jit(solution)/shard_map/ppermute | solution.py:340
  13.4 1.2 %collective-permute-start.3 = (bf16[1,2,2,128,128]{4,3,2,1,0:T(8,128)(2,1)S(1)}, bf16[1,2,2,128,128]{4,3,2,1,0:T(8,128)(2,1)S(1)}, u32[]{:S(2)}, u32[]{:S(2)}) collective-permute-start(bf16[1,2,2,128,128]{4,3,2,1,0:T(8,128)(2,1)S(1)} %shard_map.77), channel_id=1, source_target_pairs={{0,2},{1,3},{2,0},{3,1},{4,6},{5,7},{6,4},{7,5},{8,10},{9,11},{10,... | collective-permute-start | bytes 393224 | tf_op jit(solution)/shard_map/ppermute | solution.py:340
  14.6 0.8 %collective-permute-start.12 = (bf16[1,2,2,128,128]{4,3,2,1,0:T(8,128)(2,1)S(1)}, bf16[1,2,2,128,128]{4,3,2,1,0:T(8,128)(2,1)S(1)}, u32[]{:S(2)}, u32[]{:S(2)}) collective-permute-start(bf16[1,2,2,128,128]{4,3,2,1,0:T(8,128)(2,1)S(1)} %shard_map.74), channel_id=1, source_target_pairs={{0,2},{1,3},{2,0},{3,1},{4,6},{5,7},{6,4},{7,5},{8,10},{9,11},{10,... | collective-permute-start | bytes 393224 | tf_op jit(solution)/shard_map/ppermute | solution.py:340
  15.5 2.7 %collective-permute-start.10 = (bf16[2,272,128]{2,1,0:T(8,128)(2,1)S(1)}, bf16[2,272,128]{2,1,0:T(8,128)(2,1)S(1)}, u32[]{:S(2)}, u32[]{:S(2)}) collective-permute-start(bf16[2,272,128]{2,1,0:T(8,128)(2,1)S(1)} %shard_map.82), channel_id=1, source_target_pairs={{0,16},{1,21},{2,18},{3,23},{4,20},{5,17},{6,22},{7,19},{8,24},{9,... | collective-permute-start | bytes 417800 | tf_op jit(solution)/shard_map/ppermute | solution.py:345
  18.1 0.7 %collective-permute-done.6.refs_4_ = bf16[1,2,2,128,128]{4,3,2,1,0:T(8,128)(2,1)S(1)} collective-permute-done((bf16[1,2,2,128,128]{4,3,2,1,0:T(8,128)(2,1)S(1)}, bf16[1,2,2,128,128]{4,3,2,1,0:T(8,128)(2,1)S(1)}, u32[]{:S(2)}, u32[]{:S(2)}) %collective-permute-start.6) | collective-permute-done | bytes 131104 | tf_op jit(solution)/shard_map/ppermute | solution.py:340
  18.9 0.1 shard_map.80
  18.9 1.6 %collective-permute-start.7 = (bf16[2,272,128]{2,1,0:T(8,128)(2,1)S(1)}, bf16[2,272,128]{2,1,0:T(8,128)(2,1)S(1)}, u32[]{:S(2)}, u32[]{:S(2)}) collective-permute-start(bf16[2,272,128]{2,1,0:T(8,128)(2,1)S(1)} %shard_map.80), channel_id=1, source_target_pairs={{0,8},{1,13},{2,10},{3,15},{4,12},{5,9},{6,14},{7,11},{8,0},{9,5},... | collective-permute-start | bytes 417800 | tf_op jit(solution)/shard_map/ppermute | solution.py:345
  20.6 1.1 %collective-permute-done.3.refs_4_ = bf16[1,2,2,128,128]{4,3,2,1,0:T(8,128)(2,1)S(1)} collective-permute-done((bf16[1,2,2,128,128]{4,3,2,1,0:T(8,128)(2,1)S(1)}, bf16[1,2,2,128,128]{4,3,2,1,0:T(8,128)(2,1)S(1)}, u32[]{:S(2)}, u32[]{:S(2)}) %collective-permute-start.3) | collective-permute-done | bytes 131104 | tf_op jit(solution)/shard_map/ppermute | solution.py:340
  21.7 3.7 %collective-permute-start.4 = (bf16[2,272,128]{2,1,0:T(8,128)(2,1)S(1)}, bf16[2,272,128]{2,1,0:T(8,128)(2,1)S(1)}, u32[]{:S(2)}, u32[]{:S(2)}) collective-permute-start(bf16[2,272,128]{2,1,0:T(8,128)(2,1)S(1)} %shard_map.78), channel_id=1, source_target_pairs={{0,24},{1,29},{2,26},{3,31},{4,28},{5,25},{6,30},{7,27},{8,16},{9,... | collective-permute-start | bytes 417800 | tf_op jit(solution)/shard_map/ppermute | solution.py:345
  25.4 0.1 shard_map.84
  25.5 0.7 %collective-permute-start.13 = (bf16[2,272,128]{2,1,0:T(8,128)(2,1)S(1)}, bf16[2,272,128]{2,1,0:T(8,128)(2,1)S(1)}, u32[]{:S(2)}, u32[]{:S(2)}) collective-permute-start(bf16[2,272,128]{2,1,0:T(8,128)(2,1)S(1)} %shard_map.84), channel_id=1, source_target_pairs={{0,0},{1,5},{2,2},{3,7},{4,4},{5,1},{6,6},{7,3},{8,8},{9,13},{10,1... | collective-permute-start | bytes 417800 | tf_op jit(solution)/shard_map/ppermute | solution.py:345
  26.2 1.4 %collective-permute-start.11 = (bf16[1,272,128]{2,1,0:T(8,128)(2,1)S(1)}, bf16[1,272,128]{2,1,0:T(8,128)(2,1)S(1)}, u32[]{:S(2)}, u32[]{:S(2)}) collective-permute-start(bf16[1,272,128]{2,1,0:T(8,128)(2,1)S(1)} %shard_map.83), channel_id=1, source_target_pairs={{0,1},{1,0},{2,3},{3,2},{4,5},{5,4},{6,7},{7,6},{8,9},{9,8},{10,11... | collective-permute-start | bytes 208904 | tf_op jit(solution)/shard_map/ppermute | solution.py:340
  27.6 0.1 collective-permute-start.8
  27.7 2.2 %collective-permute-done.4.refs_0_ = bf16[2,272,128]{2,1,0:T(8,128)(2,1)S(1)} collective-permute-done((bf16[2,272,128]{2,1,0:T(8,128)(2,1)S(1)}, bf16[2,272,128]{2,1,0:T(8,128)(2,1)S(1)}, u32[]{:S(2)}, u32[]{:S(2)}) %collective-permute-start.4) | collective-permute-done | bytes 139296 | tf_op jit(solution)/shard_map/ppermute | solution.py:345
  29.9 1.3 %collective-permute-start.14 = (bf16[1,272,128]{2,1,0:T(8,128)(2,1)S(1)}, bf16[1,272,128]{2,1,0:T(8,128)(2,1)S(1)}, u32[]{:S(2)}, u32[]{:S(2)}) collective-permute-start(bf16[1,272,128]{2,1,0:T(8,128)(2,1)S(1)} %shard_map.85), channel_id=1, source_target_pairs={{0,1},{1,0},{2,3},{3,2},{4,5},{5,4},{6,7},{7,6},{8,9},{9,8},{10,11... | collective-permute-start | bytes 208904 | tf_op jit(solution)/shard_map/ppermute | solution.py:340
  31.2 0.9 %collective-permute-done.14.refs_7_ = bf16[1,272,128]{2,1,0:T(8,128)(2,1)S(1)} collective-permute-done((bf16[1,272,128]{2,1,0:T(8,128)(2,1)S(1)}, bf16[1,272,128]{2,1,0:T(8,128)(2,1)S(1)}, u32[]{:S(2)}, u32[]{:S(2)}) %collective-permute-start.14) | collective-permute-done | bytes 69664 | tf_op jit(solution)/shard_map/ppermute | solution.py:340
  32.1 4.1 %shard_map.86 = (bf16[4,2,128,128]{3,2,1,0:T(8,128)(2,1)S(1)}, bf16[4,2,128,128]{3,2,1,0:T(8,128)(2,1)S(1)}) custom-call(s32[3]{0:T(128)S(1)} %pad_add_fusion.at_ref, bf16[2,8,2,128,128]{4,3,2,1,0:T(8,128)(2,1)S(1)} %get-tuple-element.40.table_ref, bf16[16,128]{1,0:T(8,128)(2,1)S(1)} %fusion.4.refs_0_.own_ref, ...), custom_call_target="tpu_custom_call" | custom-call | flops 10000000000 | bytes 1000000 | tf_op jit(solution)/shard_map/pallas_call | solution.py:256
  36.2 0.4 collective-permute-start.15
  36.6 1.2 %collective-permute-done.15.other_ref = bf16[4,2,128,128]{3,2,1,0:T(8,128)(2,1)S(1)} collective-permute-done((bf16[4,2,128,128]{3,2,1,0:T(8,128)(2,1)S(1)}, bf16[4,2,128,128]{3,2,1,0:T(8,128)(2,1)S(1)}, u32[]{:S(2)}, u32[]{:S(2)}) %collective-permute-start.15) | collective-permute-done | bytes 262176 | tf_op jit(solution)/shard_map/ppermute | solution.py:340
  37.8 1.7 %collective-permute-start.19 = (bf16[2,2,128,128]{3,2,1,0:T(8,128)(2,1)S(1)}, bf16[2,2,128,128]{3,2,1,0:T(8,128)(2,1)S(1)}, u32[]{:S(2)}, u32[]{:S(2)}) collective-permute-start(bf16[2,2,128,128]{3,2,1,0:T(8,128)(2,1)S(1)} %get-tuple-element.71), channel_id=1, source_target_pairs={{0,8},{1,13},{2,10},{3,15},{4,12},{5,9},{6,14},{7,11},{8,0},{9,5},... | collective-permute-start | bytes 393224 | tf_op jit(solution)/shard_map/ppermute | solution.py:345
  39.5 0.7 %collective-permute-start.20 = (bf16[2,2,128,128]{3,2,1,0:T(8,128)(2,1)S(1)}, bf16[2,2,128,128]{3,2,1,0:T(8,128)(2,1)S(1)}, u32[]{:S(2)}, u32[]{:S(2)}) collective-permute-start(bf16[2,2,128,128]{3,2,1,0:T(8,128)(2,1)S(1)} %get-tuple-element.72), channel_id=1, source_target_pairs={{0,0},{1,5},{2,2},{3,7},{4,4},{5,1},{6,6},{7,3},{8,8},{9,13},{10,1... | collective-permute-start | bytes 393224 | tf_op jit(solution)/shard_map/ppermute | solution.py:345
  40.2 3.4 %collective-permute-start.18 = (bf16[2,2,128,128]{3,2,1,0:T(8,128)(2,1)S(1)}, bf16[2,2,128,128]{3,2,1,0:T(8,128)(2,1)S(1)}, u32[]{:S(2)}, u32[]{:S(2)}) collective-permute-start(bf16[2,2,128,128]{3,2,1,0:T(8,128)(2,1)S(1)} %get-tuple-element.70), channel_id=1, source_target_pairs={{0,24},{1,29},{2,26},{3,31},{4,28},{5,25},{6,30},{7,27},{8,16},{9,... | collective-permute-start | bytes 393224 | tf_op jit(solution)/shard_map/ppermute | solution.py:345
  43.6 0.3 collective-permute-done.19.refs_0_
  43.9 1.2 %collective-permute-start.21 = (bf16[2,2,2,128,128]{4,3,2,1,0:T(8,128)(2,1)S(1)}, bf16[2,2,2,128,128]{4,3,2,1,0:T(8,128)(2,1)S(1)}, u32[]{:S(2)}, u32[]{:S(2)}) collective-permute-start(bf16[2,2,2,128,128]{4,3,2,1,0:T(8,128)(2,1)S(1)} %shard_map.90.rest_2_), channel_id=1, source_target_pairs={{0,2},{1,3},{2,0},{3,1},{4,6},{5,7},{6,4},{7,5},{8,10},{9,11},{10,... | collective-permute-start | bytes 786440 | tf_op jit(solution)/shard_map/ppermute | solution.py:340
  45.2 2.1 %collective-permute-start.22 = (bf16[2,2,2,128,128]{4,3,2,1,0:T(8,128)(2,1)S(1)}, bf16[2,2,2,128,128]{4,3,2,1,0:T(8,128)(2,1)S(1)}, u32[]{:S(2)}, u32[]{:S(2)}) collective-permute-start(bf16[2,2,2,128,128]{4,3,2,1,0:T(8,128)(2,1)S(1)} %shard_map.90.rest_2_), channel_id=1, source_target_pairs={{0,1},{1,0},{2,3},{3,2},{4,5},{5,4},{6,7},{7,6},{8,9},{9,8},{10,11... | collective-permute-start | bytes 786440 | tf_op jit(solution)/shard_map/ppermute | solution.py:340
  47.2 2.4 %collective-permute-done.18.refs_0_ = bf16[2,2,128,128]{3,2,1,0:T(8,128)(2,1)S(1)} collective-permute-done((bf16[2,2,128,128]{3,2,1,0:T(8,128)(2,1)S(1)}, bf16[2,2,128,128]{3,2,1,0:T(8,128)(2,1)S(1)}, u32[]{:S(2)}, u32[]{:S(2)}) %collective-permute-start.18) | collective-permute-done | bytes 131104 | tf_op jit(solution)/shard_map/ppermute | solution.py:345
  49.7 1.3 %collective-permute-start.24 = (bf16[1,2,2,128,128]{4,3,2,1,0:T(8,128)(2,1)S(1)}, bf16[1,2,2,128,128]{4,3,2,1,0:T(8,128)(2,1)S(1)}, u32[]{:S(2)}, u32[]{:S(2)}) collective-permute-start(bf16[1,2,2,128,128]{4,3,2,1,0:T(8,128)(2,1)S(1)} %shard_map.89.rest_0_), channel_id=1, source_target_pairs={{0,2},{1,3},{2,0},{3,1},{4,6},{5,7},{6,4},{7,5},{8,10},{9,11},{10,... | collective-permute-start | bytes 393224 | tf_op jit(solution)/shard_map/ppermute | solution.py:340
  51.0 0.9 %collective-permute-start.25 = (bf16[1,2,2,128,128]{4,3,2,1,0:T(8,128)(2,1)S(1)}, bf16[1,2,2,128,128]{4,3,2,1,0:T(8,128)(2,1)S(1)}, u32[]{:S(2)}, u32[]{:S(2)}) collective-permute-start(bf16[1,2,2,128,128]{4,3,2,1,0:T(8,128)(2,1)S(1)} %shard_map.89.rest_0_), channel_id=1, source_target_pairs={{0,1},{1,0},{2,3},{3,2},{4,5},{5,4},{6,7},{7,6},{8,9},{9,8},{10,11... | collective-permute-start | bytes 393224 | tf_op jit(solution)/shard_map/ppermute | solution.py:340
  51.9 1.4 %collective-permute-start.23 = (bf16[2,2,2,128,128]{4,3,2,1,0:T(8,128)(2,1)S(1)}, bf16[2,2,2,128,128]{4,3,2,1,0:T(8,128)(2,1)S(1)}, u32[]{:S(2)}, u32[]{:S(2)}) collective-permute-start(bf16[2,2,2,128,128]{4,3,2,1,0:T(8,128)(2,1)S(1)} %collective-permute-done.21.rest_3_), channel_id=1, source_target_pairs={{0,1},{1,0},{2,3},{3,2},{4,5},{5,4},{6,7},{7,6},{8,9},{9,8},{10,11... | collective-permute-start | bytes 786440 | tf_op jit(solution)/shard_map/ppermute | solution.py:340
  53.3 2.2 %collective-permute-done.16.refs_0_ = bf16[2,2,128,128]{3,2,1,0:T(8,128)(2,1)S(1)} collective-permute-done((bf16[2,2,128,128]{3,2,1,0:T(8,128)(2,1)S(1)}, bf16[2,2,128,128]{3,2,1,0:T(8,128)(2,1)S(1)}, u32[]{:S(2)}, u32[]{:S(2)}) %collective-permute-start.16) | collective-permute-done | bytes 131104 | tf_op jit(solution)/shard_map/ppermute | solution.py:345
  55.5 0.6 collective-permute-start.27
  56.2 0.1 collective-permute-start.26
  56.2 1.3 %collective-permute-start.17 = (bf16[1,2,2,128,128]{4,3,2,1,0:T(8,128)(2,1)S(1)}, bf16[1,2,2,128,128]{4,3,2,1,0:T(8,128)(2,1)S(1)}, u32[]{:S(2)}, u32[]{:S(2)}) collective-permute-start(bf16[1,2,2,128,128]{4,3,2,1,0:T(8,128)(2,1)S(1)} %shard_map.88.rest_1_), channel_id=1, source_target_pairs={{0,2},{1,3},{2,0},{3,1},{4,6},{5,7},{6,4},{7,5},{8,10},{9,11},{10,... | collective-permute-start | bytes 393224 | tf_op jit(solution)/shard_map/ppermute | solution.py:340
  57.6 2.4 %shard_map.91.rest_2_ = f32[2,16,128,128]{3,2,1,0:T(8,128)S(1)} custom-call(s32[3]{0:T(128)S(1)} %pad_add_fusion.at_ref, s32[2,64]{1,0:T(2,128)S(1)} %copy-done, bf16[2,2,4,4,2,2,128,128]{7,6,5,4,3,2,1,0:T(8,128)(2,1)S(1)} %bitcast.9, bf16[1,2,2,128,128]{4,3,2,1,0:T(8,128)(2,1)S(1)} %shard_map.89.rest_0_, ...), custom_call_target="tpu_custom_call" | custom-call | flops 10000000000 | bytes 1000000 | tf_op jit(solution)/shard_map/pallas_call | solution.py:307
  60.0 2.1 %collective-permute-done.17.rest_0_ = bf16[1,2,2,128,128]{4,3,2,1,0:T(8,128)(2,1)S(1)} collective-permute-done((bf16[1,2,2,128,128]{4,3,2,1,0:T(8,128)(2,1)S(1)}, bf16[1,2,2,128,128]{4,3,2,1,0:T(8,128)(2,1)S(1)}, u32[]{:S(2)}, u32[]{:S(2)}) %collective-permute-start.17) | collective-permute-done | bytes 131104 | tf_op jit(solution)/shard_map/ppermute | solution.py:340
  62.1 1.3 %collective-permute-done.28.rest_1_ = bf16[1,2,2,128,128]{4,3,2,1,0:T(8,128)(2,1)S(1)} collective-permute-done((bf16[1,2,2,128,128]{4,3,2,1,0:T(8,128)(2,1)S(1)}, bf16[1,2,2,128,128]{4,3,2,1,0:T(8,128)(2,1)S(1)}, u32[]{:S(2)}, u32[]{:S(2)}) %collective-permute-start.28) | collective-permute-done | bytes 131104 | tf_op jit(solution)/shard_map/ppermute | solution.py:340
  63.4 2.2 %shard_map.92 = bf16[2,16,128,128]{3,2,1,0:T(8,128)(2,1)} custom-call(s32[3]{0:T(128)S(1)} %pad_add_fusion.at_ref, s32[2,64]{1,0:T(2,128)S(1)} %copy-done, bf16[2,2,4,4,2,2,128,128]{7,6,5,4,3,2,1,0:T(8,128)(2,1)S(1)} %bitcast.10, bf16[1,2,2,128,128]{4,3,2,1,0:T(8,128)(2,1)S(1)} %collective-permute-done.17.rest_0_, ...), custom_call_target="tpu_custom_call" | custom-call | flops 10000000000 | bytes 1000000 | tf_op jit(solution)/shard_map/pallas_call | solution.py:307
  (51 shorter events, 0.4 us)
Async XLA Ops:
  6.5 1.9 %collective-permute-start.1 = (bf16[3,2,2,128,128]{4,3,2,1,0:T(8,128)(2,1)S(1)}, bf16[3,2,2,128,128]{4,3,2,1,0:T(8,128)(2,1)S(1)}, u32[]{:S(2)}, u32[]{:S(2)}) collective-permute-start(bf16[3,2,2,128,128]{4,3,2,1,0:T(8,128)(2,1)S(1)} %get-tuple-element.44), channel_id=1, source_target_pairs={{0,1},{1,0},{2,3},{3,2},{4,5},{5,4},{6,7},{7,6},{8,9},{9,8},{10,11... | collective-permute-start | bytes 1179656 | tf_op jit(solution)/shard_map/ppermute | solution.py:340
  7.0 4.4 %collective-permute-start = (bf16[5,2,2,128,128]{4,3,2,1,0:T(8,128)(2,1)S(1)}, bf16[5,2,2,128,128]{4,3,2,1,0:T(8,128)(2,1)S(1)}, u32[]{:S(2)}, u32[]{:S(2)}) collective-permute-start(bf16[5,2,2,128,128]{4,3,2,1,0:T(8,128)(2,1)S(1)} %get-tuple-element.42), channel_id=1, source_target_pairs={{0,1},{1,0},{2,3},{3,2},{4,5},{5,4},{6,7},{7,6},{8,9},{9,8},{10,11... | collective-permute-start | bytes 1966088 | tf_op jit(solution)/shard_map/ppermute | solution.py:340
  8.5 7.0 %collective-permute-start.9 = (bf16[1,2,2,128,128]{4,3,2,1,0:T(8,128)(2,1)S(1)}, bf16[1,2,2,128,128]{4,3,2,1,0:T(8,128)(2,1)S(1)}, u32[]{:S(2)}, u32[]{:S(2)}) collective-permute-start(bf16[1,2,2,128,128]{4,3,2,1,0:T(8,128)(2,1)S(1)} %shard_map.75), channel_id=1, source_target_pairs={{0,2},{1,3},{2,0},{3,1},{4,6},{5,7},{6,4},{7,5},{8,10},{9,11},{10,... | collective-permute-start | bytes 393224 | tf_op jit(solution)/shard_map/ppermute | solution.py:340
  11.4 0.7 %copy-start.1 = (s32[2,8,7]{1,0,2:T(2,128)S(1)}, s32[2,8,7]{1,0,2:T(2,128)}, u32[]{:S(2)}) copy-start(s32[2,8,7]{1,0,2:T(2,128)} %param.10) | copy-start | bytes 1348
  11.4 0.8 %copy-start.2 = (s32[2,8,7]{1,0,2:T(2,128)S(1)}, s32[2,8,7]{1,0,2:T(2,128)}, u32[]{:S(2)}) copy-start(s32[2,8,7]{1,0,2:T(2,128)} %param.11) | copy-start | bytes 1348
  11.4 0.9 %copy-start.3 = (s32[2,8]{1,0:T(2,128)S(1)}, s32[2,8]{1,0:T(2,128)}, u32[]{:S(2)}) copy-start(s32[2,8]{1,0:T(2,128)} %param.12) | copy-start | bytes 196
  12.5 2.9 %collective-permute-start.2 = (bf16[16,128]{1,0:T(8,128)(2,1)S(1)}, bf16[16,128]{1,0:T(8,128)(2,1)S(1)}, u32[]{:S(2)}, u32[]{:S(2)}) collective-permute-start(bf16[16,128]{1,0:T(8,128)(2,1)S(1)} %fusion.4.refs_0_.own_ref), channel_id=1, source_target_pairs={{0,1},{1,0},{2,3},{3,2},{4,5},{5,4},{6,7},{7,6},{8,9},{9,8},{10,11... | collective-permute-start | bytes 12296 | tf_op jit(solution)/shard_map/ppermute | solution.py:340
  12.5 6.4 %collective-permute-start.6 = (bf16[1,2,2,128,128]{4,3,2,1,0:T(8,128)(2,1)S(1)}, bf16[1,2,2,128,128]{4,3,2,1,0:T(8,128)(2,1)S(1)}, u32[]{:S(2)}, u32[]{:S(2)}) collective-permute-start(bf16[1,2,2,128,128]{4,3,2,1,0:T(8,128)(2,1)S(1)} %shard_map.76), channel_id=1, source_target_pairs={{0,2},{1,3},{2,0},{3,1},{4,6},{5,7},{6,4},{7,5},{8,10},{9,11},{10,... | collective-permute-start | bytes 393224 | tf_op jit(solution)/shard_map/ppermute | solution.py:340
  13.4 8.3 %collective-permute-start.3 = (bf16[1,2,2,128,128]{4,3,2,1,0:T(8,128)(2,1)S(1)}, bf16[1,2,2,128,128]{4,3,2,1,0:T(8,128)(2,1)S(1)}, u32[]{:S(2)}, u32[]{:S(2)}) collective-permute-start(bf16[1,2,2,128,128]{4,3,2,1,0:T(8,128)(2,1)S(1)} %shard_map.77), channel_id=1, source_target_pairs={{0,2},{1,3},{2,0},{3,1},{4,6},{5,7},{6,4},{7,5},{8,10},{9,11},{10,... | collective-permute-start | bytes 393224 | tf_op jit(solution)/shard_map/ppermute | solution.py:340
  14.6 10.8 %collective-permute-start.12 = (bf16[1,2,2,128,128]{4,3,2,1,0:T(8,128)(2,1)S(1)}, bf16[1,2,2,128,128]{4,3,2,1,0:T(8,128)(2,1)S(1)}, u32[]{:S(2)}, u32[]{:S(2)}) collective-permute-start(bf16[1,2,2,128,128]{4,3,2,1,0:T(8,128)(2,1)S(1)} %shard_map.74), channel_id=1, source_target_pairs={{0,2},{1,3},{2,0},{3,1},{4,6},{5,7},{6,4},{7,5},{8,10},{9,11},{10,... | collective-permute-start | bytes 393224 | tf_op jit(solution)/shard_map/ppermute | solution.py:340
  15.5 10.7 %collective-permute-start.10 = (bf16[2,272,128]{2,1,0:T(8,128)(2,1)S(1)}, bf16[2,272,128]{2,1,0:T(8,128)(2,1)S(1)}, u32[]{:S(2)}, u32[]{:S(2)}) collective-permute-start(bf16[2,272,128]{2,1,0:T(8,128)(2,1)S(1)} %shard_map.82), channel_id=1, source_target_pairs={{0,16},{1,21},{2,18},{3,23},{4,20},{5,17},{6,22},{7,19},{8,24},{9,... | collective-permute-start | bytes 417800 | tf_op jit(solution)/shard_map/ppermute | solution.py:345
  18.9 8.7 %collective-permute-start.7 = (bf16[2,272,128]{2,1,0:T(8,128)(2,1)S(1)}, bf16[2,272,128]{2,1,0:T(8,128)(2,1)S(1)}, u32[]{:S(2)}, u32[]{:S(2)}) collective-permute-start(bf16[2,272,128]{2,1,0:T(8,128)(2,1)S(1)} %shard_map.80), channel_id=1, source_target_pairs={{0,8},{1,13},{2,10},{3,15},{4,12},{5,9},{6,14},{7,11},{8,0},{9,5},... | collective-permute-start | bytes 417800 | tf_op jit(solution)/shard_map/ppermute | solution.py:345
  21.7 8.1 %collective-permute-start.4 = (bf16[2,272,128]{2,1,0:T(8,128)(2,1)S(1)}, bf16[2,272,128]{2,1,0:T(8,128)(2,1)S(1)}, u32[]{:S(2)}, u32[]{:S(2)}) collective-permute-start(bf16[2,272,128]{2,1,0:T(8,128)(2,1)S(1)} %shard_map.78), channel_id=1, source_target_pairs={{0,24},{1,29},{2,26},{3,31},{4,28},{5,25},{6,30},{7,27},{8,16},{9,... | collective-permute-start | bytes 417800 | tf_op jit(solution)/shard_map/ppermute | solution.py:345
  25.5 4.4 %collective-permute-start.13 = (bf16[2,272,128]{2,1,0:T(8,128)(2,1)S(1)}, bf16[2,272,128]{2,1,0:T(8,128)(2,1)S(1)}, u32[]{:S(2)}, u32[]{:S(2)}) collective-permute-start(bf16[2,272,128]{2,1,0:T(8,128)(2,1)S(1)} %shard_map.84), channel_id=1, source_target_pairs={{0,0},{1,5},{2,2},{3,7},{4,4},{5,1},{6,6},{7,3},{8,8},{9,13},{10,1... | collective-permute-start | bytes 417800 | tf_op jit(solution)/shard_map/ppermute | solution.py:345
  26.2 5.0 %collective-permute-start.11 = (bf16[1,272,128]{2,1,0:T(8,128)(2,1)S(1)}, bf16[1,272,128]{2,1,0:T(8,128)(2,1)S(1)}, u32[]{:S(2)}, u32[]{:S(2)}) collective-permute-start(bf16[1,272,128]{2,1,0:T(8,128)(2,1)S(1)} %shard_map.83), channel_id=1, source_target_pairs={{0,1},{1,0},{2,3},{3,2},{4,5},{5,4},{6,7},{7,6},{8,9},{9,8},{10,11... | collective-permute-start | bytes 208904 | tf_op jit(solution)/shard_map/ppermute | solution.py:340
  27.6 3.6 %collective-permute-start.8 = (bf16[1,272,128]{2,1,0:T(8,128)(2,1)S(1)}, bf16[1,272,128]{2,1,0:T(8,128)(2,1)S(1)}, u32[]{:S(2)}, u32[]{:S(2)}) collective-permute-start(bf16[1,272,128]{2,1,0:T(8,128)(2,1)S(1)} %shard_map.81), channel_id=1, source_target_pairs={{0,1},{1,0},{2,3},{3,2},{4,5},{5,4},{6,7},{7,6},{8,9},{9,8},{10,11... | collective-permute-start | bytes 208904 | tf_op jit(solution)/shard_map/ppermute | solution.py:340
  29.9 1.3 %collective-permute-start.5 = (bf16[1,272,128]{2,1,0:T(8,128)(2,1)S(1)}, bf16[1,272,128]{2,1,0:T(8,128)(2,1)S(1)}, u32[]{:S(2)}, u32[]{:S(2)}) collective-permute-start(bf16[1,272,128]{2,1,0:T(8,128)(2,1)S(1)} %shard_map.79), channel_id=1, source_target_pairs={{0,1},{1,0},{2,3},{3,2},{4,5},{5,4},{6,7},{7,6},{8,9},{9,8},{10,11... | collective-permute-start | bytes 208904 | tf_op jit(solution)/shard_map/ppermute | solution.py:340
  29.9 2.2 %collective-permute-start.14 = (bf16[1,272,128]{2,1,0:T(8,128)(2,1)S(1)}, bf16[1,272,128]{2,1,0:T(8,128)(2,1)S(1)}, u32[]{:S(2)}, u32[]{:S(2)}) collective-permute-start(bf16[1,272,128]{2,1,0:T(8,128)(2,1)S(1)} %shard_map.85), channel_id=1, source_target_pairs={{0,1},{1,0},{2,3},{3,2},{4,5},{5,4},{6,7},{7,6},{8,9},{9,8},{10,11... | collective-permute-start | bytes 208904 | tf_op jit(solution)/shard_map/ppermute | solution.py:340
  36.2 1.6 %collective-permute-start.15 = (bf16[4,2,128,128]{3,2,1,0:T(8,128)(2,1)S(1)}, bf16[4,2,128,128]{3,2,1,0:T(8,128)(2,1)S(1)}, u32[]{:S(2)}, u32[]{:S(2)}) collective-permute-start(bf16[4,2,128,128]{3,2,1,0:T(8,128)(2,1)S(1)} %get-tuple-element.68), channel_id=1, source_target_pairs={{0,1},{1,0},{2,3},{3,2},{4,5},{5,4},{6,7},{7,6},{8,9},{9,8},{10,11... | collective-permute-start | bytes 786440 | tf_op jit(solution)/shard_map/ppermute | solution.py:340
  37.8 6.1 %collective-permute-start.19 = (bf16[2,2,128,128]{3,2,1,0:T(8,128)(2,1)S(1)}, bf16[2,2,128,128]{3,2,1,0:T(8,128)(2,1)S(1)}, u32[]{:S(2)}, u32[]{:S(2)}) collective-permute-start(bf16[2,2,128,128]{3,2,1,0:T(8,128)(2,1)S(1)} %get-tuple-element.71), channel_id=1, source_target_pairs={{0,8},{1,13},{2,10},{3,15},{4,12},{5,9},{6,14},{7,11},{8,0},{9,5},... | collective-permute-start | bytes 393224 | tf_op jit(solution)/shard_map/ppermute | solution.py:345
  39.5 4.4 %collective-permute-start.20 = (bf16[2,2,128,128]{3,2,1,0:T(8,128)(2,1)S(1)}, bf16[2,2,128,128]{3,2,1,0:T(8,128)(2,1)S(1)}, u32[]{:S(2)}, u32[]{:S(2)}) collective-permute-start(bf16[2,2,128,128]{3,2,1,0:T(8,128)(2,1)S(1)} %get-tuple-element.72), channel_id=1, source_target_pairs={{0,0},{1,5},{2,2},{3,7},{4,4},{5,1},{6,6},{7,3},{8,8},{9,13},{10,1... | collective-permute-start | bytes 393224 | tf_op jit(solution)/shard_map/ppermute | solution.py:345
  40.2 9.5 %collective-permute-start.18 = (bf16[2,2,128,128]{3,2,1,0:T(8,128)(2,1)S(1)}, bf16[2,2,128,128]{3,2,1,0:T(8,128)(2,1)S(1)}, u32[]{:S(2)}, u32[]{:S(2)}) collective-permute-start(bf16[2,2,128,128]{3,2,1,0:T(8,128)(2,1)S(1)} %get-tuple-element.70), channel_id=1, source_target_pairs={{0,24},{1,29},{2,26},{3,31},{4,28},{5,25},{6,30},{7,27},{8,16},{9,... | collective-permute-start | bytes 393224 | tf_op jit(solution)/shard_map/ppermute | solution.py:345
  43.6 11.9 %collective-permute-start.16 = (bf16[2,2,128,128]{3,2,1,0:T(8,128)(2,1)S(1)}, bf16[2,2,128,128]{3,2,1,0:T(8,128)(2,1)S(1)}, u32[]{:S(2)}, u32[]{:S(2)}) collective-permute-start(bf16[2,2,128,128]{3,2,1,0:T(8,128)(2,1)S(1)} %get-tuple-element.69), channel_id=1, source_target_pairs={{0,16},{1,21},{2,18},{3,23},{4,20},{5,17},{6,22},{7,19},{8,24},{9,... | collective-permute-start | bytes 393224 | tf_op jit(solution)/shard_map/ppermute | solution.py:345
  43.9 8.0 %collective-permute-start.21 = (bf16[2,2,2,128,128]{4,3,2,1,0:T(8,128)(2,1)S(1)}, bf16[2,2,2,128,128]{4,3,2,1,0:T(8,128)(2,1)S(1)}, u32[]{:S(2)}, u32[]{:S(2)}) collective-permute-start(bf16[2,2,2,128,128]{4,3,2,1,0:T(8,128)(2,1)S(1)} %shard_map.90.rest_2_), channel_id=1, source_target_pairs={{0,2},{1,3},{2,0},{3,1},{4,6},{5,7},{6,4},{7,5},{8,10},{9,11},{10,... | collective-permute-start | bytes 786440 | tf_op jit(solution)/shard_map/ppermute | solution.py:340
  45.2 12.4 %collective-permute-start.22 = (bf16[2,2,2,128,128]{4,3,2,1,0:T(8,128)(2,1)S(1)}, bf16[2,2,2,128,128]{4,3,2,1,0:T(8,128)(2,1)S(1)}, u32[]{:S(2)}, u32[]{:S(2)}) collective-permute-start(bf16[2,2,2,128,128]{4,3,2,1,0:T(8,128)(2,1)S(1)} %shard_map.90.rest_2_), channel_id=1, source_target_pairs={{0,1},{1,0},{2,3},{3,2},{4,5},{5,4},{6,7},{7,6},{8,9},{9,8},{10,11... | collective-permute-start | bytes 786440 | tf_op jit(solution)/shard_map/ppermute | solution.py:340
  49.6 7.9 %slice-start = ((s8[8388608]{0:T(1024)(128)(4,1)}), s8[4194304]{0:T(1024)(128)(4,1)S(1)}, s32[]{:S(2)}) async-start(s8[8388608]{0:T(1024)(128)(4,1)} %bitcast.7), calls=%async_computation | async-start | bytes 8388608
  49.7 7.9 %slice-start.1 = ((s8[8388608]{0:T(1024)(128)(4,1)}), s8[4194304]{0:T(1024)(128)(4,1)S(1)}, s32[]{:S(2)}) async-start(s8[8388608]{0:T(1024)(128)(4,1)} %bitcast.7), calls=%async_computation.1 | async-start | bytes 8388608
  49.7 7.9 %copy-start = (s32[2,64]{1,0:T(2,128)S(1)}, s32[2,64]{1,0:T(2,128)}, u32[]{:S(2)}) copy-start(s32[2,64]{1,0:T(2,128)} %dir_ref.3) | copy-start | bytes 1540
  49.7 6.5 %collective-permute-start.24 = (bf16[1,2,2,128,128]{4,3,2,1,0:T(8,128)(2,1)S(1)}, bf16[1,2,2,128,128]{4,3,2,1,0:T(8,128)(2,1)S(1)}, u32[]{:S(2)}, u32[]{:S(2)}) collective-permute-start(bf16[1,2,2,128,128]{4,3,2,1,0:T(8,128)(2,1)S(1)} %shard_map.89.rest_0_), channel_id=1, source_target_pairs={{0,2},{1,3},{2,0},{3,1},{4,6},{5,7},{6,4},{7,5},{8,10},{9,11},{10,... | collective-permute-start | bytes 393224 | tf_op jit(solution)/shard_map/ppermute | solution.py:340
  51.0 5.3 %collective-permute-start.25 = (bf16[1,2,2,128,128]{4,3,2,1,0:T(8,128)(2,1)S(1)}, bf16[1,2,2,128,128]{4,3,2,1,0:T(8,128)(2,1)S(1)}, u32[]{:S(2)}, u32[]{:S(2)}) collective-permute-start(bf16[1,2,2,128,128]{4,3,2,1,0:T(8,128)(2,1)S(1)} %shard_map.89.rest_0_), channel_id=1, source_target_pairs={{0,1},{1,0},{2,3},{3,2},{4,5},{5,4},{6,7},{7,6},{8,9},{9,8},{10,11... | collective-permute-start | bytes 393224 | tf_op jit(solution)/shard_map/ppermute | solution.py:340
  51.9 5.6 %collective-permute-start.23 = (bf16[2,2,2,128,128]{4,3,2,1,0:T(8,128)(2,1)S(1)}, bf16[2,2,2,128,128]{4,3,2,1,0:T(8,128)(2,1)S(1)}, u32[]{:S(2)}, u32[]{:S(2)}) collective-permute-start(bf16[2,2,2,128,128]{4,3,2,1,0:T(8,128)(2,1)S(1)} %collective-permute-done.21.rest_3_), channel_id=1, source_target_pairs={{0,1},{1,0},{2,3},{3,2},{4,5},{5,4},{6,7},{7,6},{8,9},{9,8},{10,11... | collective-permute-start | bytes 786440 | tf_op jit(solution)/shard_map/ppermute | solution.py:340
  55.5 2.0 %collective-permute-start.27 = (bf16[1,2,2,128,128]{4,3,2,1,0:T(8,128)(2,1)S(1)}, bf16[1,2,2,128,128]{4,3,2,1,0:T(8,128)(2,1)S(1)}, u32[]{:S(2)}, u32[]{:S(2)}) collective-permute-start(bf16[1,2,2,128,128]{4,3,2,1,0:T(8,128)(2,1)S(1)} %shard_map.88.rest_1_), channel_id=1, source_target_pairs={{0,1},{1,0},{2,3},{3,2},{4,5},{5,4},{6,7},{7,6},{8,9},{9,8},{10,11... | collective-permute-start | bytes 393224 | tf_op jit(solution)/shard_map/ppermute | solution.py:340
  56.2 1.4 %collective-permute-start.26 = (bf16[1,2,2,128,128]{4,3,2,1,0:T(8,128)(2,1)S(1)}, bf16[1,2,2,128,128]{4,3,2,1,0:T(8,128)(2,1)S(1)}, u32[]{:S(2)}, u32[]{:S(2)}) collective-permute-start(bf16[1,2,2,128,128]{4,3,2,1,0:T(8,128)(2,1)S(1)} %collective-permute-done.24.rest_6_), channel_id=1, source_target_pairs={{0,1},{1,0},{2,3},{3,2},{4,5},{5,4},{6,7},{7,6},{8,9},{9,8},{10,11... | collective-permute-start | bytes 393224 | tf_op jit(solution)/shard_map/ppermute | solution.py:340
  56.2 5.8 %collective-permute-start.17 = (bf16[1,2,2,128,128]{4,3,2,1,0:T(8,128)(2,1)S(1)}, bf16[1,2,2,128,128]{4,3,2,1,0:T(8,128)(2,1)S(1)}, u32[]{:S(2)}, u32[]{:S(2)}) collective-permute-start(bf16[1,2,2,128,128]{4,3,2,1,0:T(8,128)(2,1)S(1)} %shard_map.88.rest_1_), channel_id=1, source_target_pairs={{0,2},{1,3},{2,0},{3,1},{4,6},{5,7},{6,4},{7,5},{8,10},{9,11},{10,... | collective-permute-start | bytes 393224 | tf_op jit(solution)/shard_map/ppermute | solution.py:340
  62.1 1.3 %collective-permute-start.28 = (bf16[1,2,2,128,128]{4,3,2,1,0:T(8,128)(2,1)S(1)}, bf16[1,2,2,128,128]{4,3,2,1,0:T(8,128)(2,1)S(1)}, u32[]{:S(2)}, u32[]{:S(2)}) collective-permute-start(bf16[1,2,2,128,128]{4,3,2,1,0:T(8,128)(2,1)S(1)} %collective-permute-done.17.rest_0_), channel_id=1, source_target_pairs={{0,1},{1,0},{2,3},{3,2},{4,5},{5,4},{6,7},{7,6},{8,9},{9,8},{10,11... | collective-permute-start | bytes 393224 | tf_op jit(solution)/shard_map/ppermute | solution.py:340

commit v5 on v4

--- a/solution.py
+++ b/solution.py
@@ -211,10 +211,16 @@
             held_by[base] = (sources[pos + n].at[0], sources[pos + len(chunk)].at[n])
         pos += len(chunk) + 1
     gathered = sources[pos:]
-    numbers[0] = own_ref[...].astype(F32).astype(jnp.int32)
-    for z in range(1, nz):
-        mine, theirs = (ref[per * rank :].astype(F32) for ref in held_by[z * planes])
-        numbers[z] = jnp.where(me == 0, mine, theirs).astype(jnp.int32)
+    for z in range(nz):
+        if z == 0:
+            tile = own_ref[...].astype(F32)
+        else:
+            mine, theirs = (ref[per * rank :].astype(F32) for ref in held_by[z * planes])
+            tile = jnp.where(me == 0, mine, theirs)
+        row_of = lax.broadcasted_iota(jnp.int32, tile.shape, 0)
+        for q in range(planes):
+            row = jnp.where(row_of == at_ref[2] * planes + q, tile, 0.0)
+            numbers[pl.ds(z * planes + q, 1)] = jnp.sum(row, axis=0, keepdims=True).astype(jnp.int32)
     copy = pltpu.make_async_copy(numbers, lists, sem)
     copy.start()
     parts = []
@@ -234,14 +240,14 @@
     copy.wait()
     for row, s in ((theirs_ref, 1), (mine_ref, 0)):
         for n, base in enumerate(bases):
-            q, z = lax.bitwise_xor(xor(at_ref[0], base % planes), xor(me, s)), at_ref[2]
+            q = lax.bitwise_xor(xor(at_ref[0], base % planes), xor(me, s))
             for m in range(per):
-                entry = (base // planes, q * held + z * per + m)
-                active = lists[entry + (2 * most,)]
+                line, column = base // planes * planes + q, m * (2 * most + 1)
+                active = lists[line, column + 2 * most]
                 total = None
                 for k in range(most):
-                    kind = lists[entry + (most + k,)]
-                    source = jnp.where(k < active, lists[entry + (k,)], count)
+                    kind = lists[line, column + most + k]
+                    source = jnp.where(k < active, lists[line, column + k], count)
                     both = jnp.concatenate([table_ref[m, kind, 0], table_ref[m, kind, 1]], axis=1)
                     term = dot(both, wide[source, m])
                     total = term if total is None else total + term
@@ -251,7 +257,7 @@
 def couple(at, table, own, sources, sizes, total):
     per, _, _, rank, _ = table.shape
     width = sources[0].shape[-1]
-    listed = (sizes[1],) + own.shape
+    listed = (sizes[0] * sizes[1], own.shape[1])
     rows = len(sizes[-1])
     return pl.pallas_call(
         functools.partial(couple_kernel, sizes),
@@ -368,8 +374,9 @@
                         )
                     moved = family(ready, bit)
                     got[c, rel ^ bit].append((moved, 0))
-    lists = jnp.concatenate([couple_src, couple_kind, couple_count[..., None]], axis=-1).reshape(planes * held, -1)
-    lists = jnp.pad(lists, ((0, -planes * held % 16), (0, rank - lists.shape[1]))).astype(BF16)
+    lists = jnp.concatenate([couple_src, couple_kind, couple_count[..., None]], axis=-1)
+    lists = lists.reshape(planes, nz, -1).transpose(1, 0, 2).reshape(partners, -1)
+    lists = jnp.pad(lists, ((0, -partners % 16), (0, rank - lists.shape[1]))).astype(BF16)
     both_lists = (lists, family(lists, 1))
     sources = []
     for c in order:

time: 65.9 us -> 65.4 us (level)
  transfers between devices with their start and end apart: 29 -> 29, of which waited for: 11 -> 12; matrix products, arithmetic and copies ran while one was open for 1% -> 0% of each run, Pallas kernels for 4% -> 4%
where the time goes in v5:
time: 65.4 us; the launch traced here: 65.1 us
  starting transfers between devices  33 us (50%)
  waiting for transfers between devices  15.8 us (24%)
  Pallas kernels  15.1 us (23%)
  local copies, waits for them, and re-layouts  0.89 us (1%)
    ppermute x21, starting transfers between devices, family(): return lax.ppermute(x, 'gy', [(i, i ^ rel) for i in range(ny)])  18.5 us
    ppermute x8, starting transfers between devices, partner(): return lax.ppermute(x, axes, [(i, i ^ moves[i & 1]) for i in range(size)])  14.5 us
    ppermute x21, waiting for transfers between devices, family(): return lax.ppermute(x, 'gy', [(i, i ^ rel) for i in range(ny)])  8.74 us
    ppermute x8, waiting for transfers between devices, partner(): return lax.ppermute(x, axes, [(i, i ^ moves[i & 1]) for i in range(size)])  7.07 us
    pallas_call x1, Pallas kernels, up(): pl.pallas_call(functools.partial(up_kernel, jobs), out_shape=shapes + [ja...  6.39 us
    pallas_call x2, Pallas kernels, down(): pl.pallas_call(functools.partial(down_kernel, jobs, last), out_shape=jax....  4.61 us
    pallas_call x1, Pallas kernels, couple(): pl.pallas_call(functools.partial(couple_kernel, sizes), out_shape=[jax.Sh...  3.63 us
  transfers between devices with their start and end apart: 29, of which 12 were waited for; matrix products, arithmetic and copies ran while one was open for 0% of the time, Pallas kernels for 4%

profile of v5, /device:TPU:0, one launch (start us, length us, event | category | flops | bytes accessed | tf_op | source)
XLA Modules:
  0.0 65.1 jit_solution(844361135458040909)
XLA Ops:
  0.0 0.1 pad_add_fusion.at_ref
  0.1 6.4 %shard_map.73 = (bf16[3,2,2,128,128]{4,3,2,1,0:T(8,128)(2,1)S(1)}, bf16[5,2,2,128,128]{4,3,2,1,0:T(8,128)(2,1)S(1)}, bf16[1,2,2,128,128]{4,3,2,1,0:T(8,128)(2,1)...) custom-call(s32[3]{0:T(128)S(1)} %pad_add_fusion.at_ref, ...), custom_call_target="tpu_custom_call" | custom-call | flops 10000000000 | bytes 1000000 | tf_op jit(solution)/shard_map/pallas_call | solution.py:104
  6.5 0.5 collective-permute-start.1
  7.0 0.1 collective-permute-start
  7.1 1.3 %collective-permute-done.1.refs_1_ = bf16[3,2,2,128,128]{4,3,2,1,0:T(8,128)(2,1)S(1)} collective-permute-done((bf16[3,2,2,128,128]{4,3,2,1,0:T(8,128)(2,1)S(1)}, bf16[3,2,2,128,128]{4,3,2,1,0:T(8,128)(2,1)S(1)}, u32[]{:S(2)}, u32[]{:S(2)}) %collective-permute-start.1) | collective-permute-done | bytes 393248 | tf_op jit(solution)/shard_map/ppermute | solution.py:346
  8.5 2.9 %collective-permute-start.9 = (bf16[1,2,2,128,128]{4,3,2,1,0:T(8,128)(2,1)S(1)}, bf16[1,2,2,128,128]{4,3,2,1,0:T(8,128)(2,1)S(1)}, u32[]{:S(2)}, u32[]{:S(2)}) collective-permute-start(bf16[1,2,2,128,128]{4,3,2,1,0:T(8,128)(2,1)S(1)} %shard_map.75), channel_id=1, source_target_pairs={{0,2},{1,3},{2,0},{3,1},{4,6},{5,7},{6,4},{7,5},{8,10},{9,11},{10,... | collective-permute-start | bytes 393224 | tf_op jit(solution)/shard_map/ppermute | solution.py:346
  11.4 0.6 copy-done.3
  12.2 0.1 copy.8
  12.3 0.1 reshape.12
  12.4 0.1 collective-permute-start.2
  12.4 0.9 %collective-permute-start.6 = (bf16[1,2,2,128,128]{4,3,2,1,0:T(8,128)(2,1)S(1)}, bf16[1,2,2,128,128]{4,3,2,1,0:T(8,128)(2,1)S(1)}, u32[]{:S(2)}, u32[]{:S(2)}) collective-permute-start(bf16[1,2,2,128,128]{4,3,2,1,0:T(8,128)(2,1)S(1)} %shard_map.76), channel_id=1, source_target_pairs={{0,2},{1,3},{2,0},{3,1},{4,6},{5,7},{6,4},{7,5},{8,10},{9,11},{10,... | collective-permute-start | bytes 393224 | tf_op jit(solution)/shard_map/ppermute | solution.py:346
  13.3 1.2 %collective-permute-start.3 = (bf16[1,2,2,128,128]{4,3,2,1,0:T(8,128)(2,1)S(1)}, bf16[1,2,2,128,128]{4,3,2,1,0:T(8,128)(2,1)S(1)}, u32[]{:S(2)}, u32[]{:S(2)}) collective-permute-start(bf16[1,2,2,128,128]{4,3,2,1,0:T(8,128)(2,1)S(1)} %shard_map.77), channel_id=1, source_target_pairs={{0,2},{1,3},{2,0},{3,1},{4,6},{5,7},{6,4},{7,5},{8,10},{9,11},{10,... | collective-permute-start | bytes 393224 | tf_op jit(solution)/shard_map/ppermute | solution.py:346
  14.5 0.8 %collective-permute-start.12 = (bf16[1,2,2,128,128]{4,3,2,1,0:T(8,128)(2,1)S(1)}, bf16[1,2,2,128,128]{4,3,2,1,0:T(8,128)(2,1)S(1)}, u32[]{:S(2)}, u32[]{:S(2)}) collective-permute-start(bf16[1,2,2,128,128]{4,3,2,1,0:T(8,128)(2,1)S(1)} %shard_map.74), channel_id=1, source_target_pairs={{0,2},{1,3},{2,0},{3,1},{4,6},{5,7},{6,4},{7,5},{8,10},{9,11},{10,... | collective-permute-start | bytes 393224 | tf_op jit(solution)/shard_map/ppermute | solution.py:346
  15.4 2.7 %collective-permute-start.10 = (bf16[2,272,128]{2,1,0:T(8,128)(2,1)S(1)}, bf16[2,272,128]{2,1,0:T(8,128)(2,1)S(1)}, u32[]{:S(2)}, u32[]{:S(2)}) collective-permute-start(bf16[2,272,128]{2,1,0:T(8,128)(2,1)S(1)} %shard_map.82), channel_id=1, source_target_pairs={{0,16},{1,21},{2,18},{3,23},{4,20},{5,17},{6,22},{7,19},{8,24},{9,... | collective-permute-start | bytes 417800 | tf_op jit(solution)/shard_map/ppermute | solution.py:351
  18.1 0.6 collective-permute-done.6.refs_4_
  18.8 0.1 shard_map.80
  18.9 1.6 %collective-permute-start.7 = (bf16[2,272,128]{2,1,0:T(8,128)(2,1)S(1)}, bf16[2,272,128]{2,1,0:T(8,128)(2,1)S(1)}, u32[]{:S(2)}, u32[]{:S(2)}) collective-permute-start(bf16[2,272,128]{2,1,0:T(8,128)(2,1)S(1)} %shard_map.80), channel_id=1, source_target_pairs={{0,8},{1,13},{2,10},{3,15},{4,12},{5,9},{6,14},{7,11},{8,0},{9,5},... | collective-permute-start | bytes 417800 | tf_op jit(solution)/shard_map/ppermute | solution.py:351
  20.5 1.1 %collective-permute-done.3.refs_4_ = bf16[1,2,2,128,128]{4,3,2,1,0:T(8,128)(2,1)S(1)} collective-permute-done((bf16[1,2,2,128,128]{4,3,2,1,0:T(8,128)(2,1)S(1)}, bf16[1,2,2,128,128]{4,3,2,1,0:T(8,128)(2,1)S(1)}, u32[]{:S(2)}, u32[]{:S(2)}) %collective-permute-start.3) | collective-permute-done | bytes 131104 | tf_op jit(solution)/shard_map/ppermute | solution.py:346
  21.7 3.7 %collective-permute-start.4 = (bf16[2,272,128]{2,1,0:T(8,128)(2,1)S(1)}, bf16[2,272,128]{2,1,0:T(8,128)(2,1)S(1)}, u32[]{:S(2)}, u32[]{:S(2)}) collective-permute-start(bf16[2,272,128]{2,1,0:T(8,128)(2,1)S(1)} %shard_map.78), channel_id=1, source_target_pairs={{0,24},{1,29},{2,26},{3,31},{4,28},{5,25},{6,30},{7,27},{8,16},{9,... | collective-permute-start | bytes 417800 | tf_op jit(solution)/shard_map/ppermute | solution.py:351
  25.3 0.1 shard_map.84
  25.4 0.7 %collective-permute-start.13 = (bf16[2,272,128]{2,1,0:T(8,128)(2,1)S(1)}, bf16[2,272,128]{2,1,0:T(8,128)(2,1)S(1)}, u32[]{:S(2)}, u32[]{:S(2)}) collective-permute-start(bf16[2,272,128]{2,1,0:T(8,128)(2,1)S(1)} %shard_map.84), channel_id=1, source_target_pairs={{0,0},{1,5},{2,2},{3,7},{4,4},{5,1},{6,6},{7,3},{8,8},{9,13},{10,1... | collective-permute-start | bytes 417800 | tf_op jit(solution)/shard_map/ppermute | solution.py:351
  26.1 1.4 %collective-permute-start.11 = (bf16[1,272,128]{2,1,0:T(8,128)(2,1)S(1)}, bf16[1,272,128]{2,1,0:T(8,128)(2,1)S(1)}, u32[]{:S(2)}, u32[]{:S(2)}) collective-permute-start(bf16[1,272,128]{2,1,0:T(8,128)(2,1)S(1)} %shard_map.83), channel_id=1, source_target_pairs={{0,1},{1,0},{2,3},{3,2},{4,5},{5,4},{6,7},{7,6},{8,9},{9,8},{10,11... | collective-permute-start | bytes 208904 | tf_op jit(solution)/shard_map/ppermute | solution.py:346
  27.5 0.1 collective-permute-start.8
  27.6 2.2 %collective-permute-done.4.refs_0_ = bf16[2,272,128]{2,1,0:T(8,128)(2,1)S(1)} collective-permute-done((bf16[2,272,128]{2,1,0:T(8,128)(2,1)S(1)}, bf16[2,272,128]{2,1,0:T(8,128)(2,1)S(1)}, u32[]{:S(2)}, u32[]{:S(2)}) %collective-permute-start.4) | collective-permute-done | bytes 139296 | tf_op jit(solution)/shard_map/ppermute | solution.py:351
  29.8 1.3 %collective-permute-start.14 = (bf16[1,272,128]{2,1,0:T(8,128)(2,1)S(1)}, bf16[1,272,128]{2,1,0:T(8,128)(2,1)S(1)}, u32[]{:S(2)}, u32[]{:S(2)}) collective-permute-start(bf16[1,272,128]{2,1,0:T(8,128)(2,1)S(1)} %shard_map.85), channel_id=1, source_target_pairs={{0,1},{1,0},{2,3},{3,2},{4,5},{5,4},{6,7},{7,6},{8,9},{9,8},{10,11... | collective-permute-start | bytes 208904 | tf_op jit(solution)/shard_map/ppermute | solution.py:346
  31.1 0.9 %collective-permute-done.14.refs_7_ = bf16[1,272,128]{2,1,0:T(8,128)(2,1)S(1)} collective-permute-done((bf16[1,272,128]{2,1,0:T(8,128)(2,1)S(1)}, bf16[1,272,128]{2,1,0:T(8,128)(2,1)S(1)}, u32[]{:S(2)}, u32[]{:S(2)}) %collective-permute-start.14) | collective-permute-done | bytes 69664 | tf_op jit(solution)/shard_map/ppermute | solution.py:346
  32.0 3.6 %shard_map.86 = (bf16[4,2,128,128]{3,2,1,0:T(8,128)(2,1)S(1)}, bf16[4,2,128,128]{3,2,1,0:T(8,128)(2,1)S(1)}) custom-call(s32[3]{0:T(128)S(1)} %pad_add_fusion.at_ref, bf16[2,8,2,128,128]{4,3,2,1,0:T(8,128)(2,1)S(1)} %get-tuple-element.40.table_ref, bf16[16,128]{1,0:T(8,128)(2,1)S(1)} %pad.5.refs_0_.own_ref, ...), custom_call_target="tpu_custom_call" | custom-call | flops 10000000000 | bytes 1000000 | tf_op jit(solution)/shard_map/pallas_call | solution.py:262
  35.6 0.4 collective-permute-start.15
  36.0 1.2 %collective-permute-done.15.other_ref = bf16[4,2,128,128]{3,2,1,0:T(8,128)(2,1)S(1)} collective-permute-done((bf16[4,2,128,128]{3,2,1,0:T(8,128)(2,1)S(1)}, bf16[4,2,128,128]{3,2,1,0:T(8,128)(2,1)S(1)}, u32[]{:S(2)}, u32[]{:S(2)}) %collective-permute-start.15) | collective-permute-done | bytes 262176 | tf_op jit(solution)/shard_map/ppermute | solution.py:346
  37.3 1.7 %collective-permute-start.19 = (bf16[2,2,128,128]{3,2,1,0:T(8,128)(2,1)S(1)}, bf16[2,2,128,128]{3,2,1,0:T(8,128)(2,1)S(1)}, u32[]{:S(2)}, u32[]{:S(2)}) collective-permute-start(bf16[2,2,128,128]{3,2,1,0:T(8,128)(2,1)S(1)} %get-tuple-element.71), channel_id=1, source_target_pairs={{0,8},{1,13},{2,10},{3,15},{4,12},{5,9},{6,14},{7,11},{8,0},{9,5},... | collective-permute-start | bytes 393224 | tf_op jit(solution)/shard_map/ppermute | solution.py:351
  39.0 0.7 %collective-permute-start.20 = (bf16[2,2,128,128]{3,2,1,0:T(8,128)(2,1)S(1)}, bf16[2,2,128,128]{3,2,1,0:T(8,128)(2,1)S(1)}, u32[]{:S(2)}, u32[]{:S(2)}) collective-permute-start(bf16[2,2,128,128]{3,2,1,0:T(8,128)(2,1)S(1)} %get-tuple-element.72), channel_id=1, source_target_pairs={{0,0},{1,5},{2,2},{3,7},{4,4},{5,1},{6,6},{7,3},{8,8},{9,13},{10,1... | collective-permute-start | bytes 393224 | tf_op jit(solution)/shard_map/ppermute | solution.py:351
  39.6 3.4 %collective-permute-start.18 = (bf16[2,2,128,128]{3,2,1,0:T(8,128)(2,1)S(1)}, bf16[2,2,128,128]{3,2,1,0:T(8,128)(2,1)S(1)}, u32[]{:S(2)}, u32[]{:S(2)}) collective-permute-start(bf16[2,2,128,128]{3,2,1,0:T(8,128)(2,1)S(1)} %get-tuple-element.70), channel_id=1, source_target_pairs={{0,24},{1,29},{2,26},{3,31},{4,28},{5,25},{6,30},{7,27},{8,16},{9,... | collective-permute-start | bytes 393224 | tf_op jit(solution)/shard_map/ppermute | solution.py:351
  43.1 0.3 collective-permute-done.19.refs_0_
  43.4 1.2 %collective-permute-start.21 = (bf16[2,2,2,128,128]{4,3,2,1,0:T(8,128)(2,1)S(1)}, bf16[2,2,2,128,128]{4,3,2,1,0:T(8,128)(2,1)S(1)}, u32[]{:S(2)}, u32[]{:S(2)}) collective-permute-start(bf16[2,2,2,128,128]{4,3,2,1,0:T(8,128)(2,1)S(1)} %shard_map.90.rest_2_), channel_id=1, source_target_pairs={{0,2},{1,3},{2,0},{3,1},{4,6},{5,7},{6,4},{7,5},{8,10},{9,11},{10,... | collective-permute-start | bytes 786440 | tf_op jit(solution)/shard_map/ppermute | solution.py:346
  44.5 2.2 %collective-permute-start.22 = (bf16[2,2,2,128,128]{4,3,2,1,0:T(8,128)(2,1)S(1)}, bf16[2,2,2,128,128]{4,3,2,1,0:T(8,128)(2,1)S(1)}, u32[]{:S(2)}, u32[]{:S(2)}) collective-permute-start(bf16[2,2,2,128,128]{4,3,2,1,0:T(8,128)(2,1)S(1)} %shard_map.90.rest_2_), channel_id=1, source_target_pairs={{0,1},{1,0},{2,3},{3,2},{4,5},{5,4},{6,7},{7,6},{8,9},{9,8},{10,11... | collective-permute-start | bytes 786440 | tf_op jit(solution)/shard_map/ppermute | solution.py:346
  46.7 2.4 %collective-permute-done.18.refs_0_ = bf16[2,2,128,128]{3,2,1,0:T(8,128)(2,1)S(1)} collective-permute-done((bf16[2,2,128,128]{3,2,1,0:T(8,128)(2,1)S(1)}, bf16[2,2,128,128]{3,2,1,0:T(8,128)(2,1)S(1)}, u32[]{:S(2)}, u32[]{:S(2)}) %collective-permute-start.18) | collective-permute-done | bytes 131104 | tf_op jit(solution)/shard_map/ppermute | solution.py:351
  49.2 1.3 %collective-permute-start.24 = (bf16[1,2,2,128,128]{4,3,2,1,0:T(8,128)(2,1)S(1)}, bf16[1,2,2,128,128]{4,3,2,1,0:T(8,128)(2,1)S(1)}, u32[]{:S(2)}, u32[]{:S(2)}) collective-permute-start(bf16[1,2,2,128,128]{4,3,2,1,0:T(8,128)(2,1)S(1)} %shard_map.89.rest_0_), channel_id=1, source_target_pairs={{0,2},{1,3},{2,0},{3,1},{4,6},{5,7},{6,4},{7,5},{8,10},{9,11},{10,... | collective-permute-start | bytes 393224 | tf_op jit(solution)/shard_map/ppermute | solution.py:346
  50.5 0.9 %collective-permute-start.25 = (bf16[1,2,2,128,128]{4,3,2,1,0:T(8,128)(2,1)S(1)}, bf16[1,2,2,128,128]{4,3,2,1,0:T(8,128)(2,1)S(1)}, u32[]{:S(2)}, u32[]{:S(2)}) collective-permute-start(bf16[1,2,2,128,128]{4,3,2,1,0:T(8,128)(2,1)S(1)} %shard_map.89.rest_0_), channel_id=1, source_target_pairs={{0,1},{1,0},{2,3},{3,2},{4,5},{5,4},{6,7},{7,6},{8,9},{9,8},{10,11... | collective-permute-start | bytes 393224 | tf_op jit(solution)/shard_map/ppermute | solution.py:346
  51.5 1.3 %collective-permute-start.23 = (bf16[2,2,2,128,128]{4,3,2,1,0:T(8,128)(2,1)S(1)}, bf16[2,2,2,128,128]{4,3,2,1,0:T(8,128)(2,1)S(1)}, u32[]{:S(2)}, u32[]{:S(2)}) collective-permute-start(bf16[2,2,2,128,128]{4,3,2,1,0:T(8,128)(2,1)S(1)} %collective-permute-done.21.rest_3_), channel_id=1, source_target_pairs={{0,1},{1,0},{2,3},{3,2},{4,5},{5,4},{6,7},{7,6},{8,9},{9,8},{10,11... | collective-permute-start | bytes 786440 | tf_op jit(solution)/shard_map/ppermute | solution.py:346
  52.7 2.2 %collective-permute-done.16.refs_0_ = bf16[2,2,128,128]{3,2,1,0:T(8,128)(2,1)S(1)} collective-permute-done((bf16[2,2,128,128]{3,2,1,0:T(8,128)(2,1)S(1)}, bf16[2,2,128,128]{3,2,1,0:T(8,128)(2,1)S(1)}, u32[]{:S(2)}, u32[]{:S(2)}) %collective-permute-start.16) | collective-permute-done | bytes 131104 | tf_op jit(solution)/shard_map/ppermute | solution.py:351
  55.0 0.7 %collective-permute-start.27 = (bf16[1,2,2,128,128]{4,3,2,1,0:T(8,128)(2,1)S(1)}, bf16[1,2,2,128,128]{4,3,2,1,0:T(8,128)(2,1)S(1)}, u32[]{:S(2)}, u32[]{:S(2)}) collective-permute-start(bf16[1,2,2,128,128]{4,3,2,1,0:T(8,128)(2,1)S(1)} %shard_map.88.rest_1_), channel_id=1, source_target_pairs={{0,1},{1,0},{2,3},{3,2},{4,5},{5,4},{6,7},{7,6},{8,9},{9,8},{10,11... | collective-permute-start | bytes 393224 | tf_op jit(solution)/shard_map/ppermute | solution.py:346
  55.6 0.1 collective-permute-start.26
  55.7 1.1 %collective-permute-start.17 = (bf16[1,2,2,128,128]{4,3,2,1,0:T(8,128)(2,1)S(1)}, bf16[1,2,2,128,128]{4,3,2,1,0:T(8,128)(2,1)S(1)}, u32[]{:S(2)}, u32[]{:S(2)}) collective-permute-start(bf16[1,2,2,128,128]{4,3,2,1,0:T(8,128)(2,1)S(1)} %shard_map.88.rest_1_), channel_id=1, source_target_pairs={{0,2},{1,3},{2,0},{3,1},{4,6},{5,7},{6,4},{7,5},{8,10},{9,11},{10,... | collective-permute-start | bytes 393224 | tf_op jit(solution)/shard_map/ppermute | solution.py:346
  56.9 0.1 collective-permute-done.26.rest_8_
  57.0 2.4 %shard_map.91.rest_2_ = f32[2,16,128,128]{3,2,1,0:T(8,128)S(1)} custom-call(s32[3]{0:T(128)S(1)} %pad_add_fusion.at_ref, s32[2,64]{1,0:T(2,128)S(1)} %copy-done, bf16[2,2,4,4,2,2,128,128]{7,6,5,4,3,2,1,0:T(8,128)(2,1)S(1)} %bitcast.11, bf16[1,2,2,128,128]{4,3,2,1,0:T(8,128)(2,1)S(1)} %shard_map.89.rest_0_, ...), custom_call_target="tpu_custom_call" | custom-call | flops 10000000000 | bytes 1000000 | tf_op jit(solution)/shard_map/pallas_call | solution.py:313
  59.4 2.1 %collective-permute-done.17.rest_0_ = bf16[1,2,2,128,128]{4,3,2,1,0:T(8,128)(2,1)S(1)} collective-permute-done((bf16[1,2,2,128,128]{4,3,2,1,0:T(8,128)(2,1)S(1)}, bf16[1,2,2,128,128]{4,3,2,1,0:T(8,128)(2,1)S(1)}, u32[]{:S(2)}, u32[]{:S(2)}) %collective-permute-start.17) | collective-permute-done | bytes 131104 | tf_op jit(solution)/shard_map/ppermute | solution.py:346
  61.6 1.3 %collective-permute-done.28.rest_1_ = bf16[1,2,2,128,128]{4,3,2,1,0:T(8,128)(2,1)S(1)} collective-permute-done((bf16[1,2,2,128,128]{4,3,2,1,0:T(8,128)(2,1)S(1)}, bf16[1,2,2,128,128]{4,3,2,1,0:T(8,128)(2,1)S(1)}, u32[]{:S(2)}, u32[]{:S(2)}) %collective-permute-start.28) | collective-permute-done | bytes 131104 | tf_op jit(solution)/shard_map/ppermute | solution.py:346
  62.9 2.2 %shard_map.92 = bf16[2,16,128,128]{3,2,1,0:T(8,128)(2,1)} custom-call(s32[3]{0:T(128)S(1)} %pad_add_fusion.at_ref, s32[2,64]{1,0:T(2,128)S(1)} %copy-done, bf16[2,2,4,4,2,2,128,128]{7,6,5,4,3,2,1,0:T(8,128)(2,1)S(1)} %bitcast.12, bf16[1,2,2,128,128]{4,3,2,1,0:T(8,128)(2,1)S(1)} %collective-permute-done.17.rest_0_, ...), custom_call_target="tpu_custom_call" | custom-call | flops 10000000000 | bytes 1000000 | tf_op jit(solution)/shard_map/pallas_call | solution.py:313
  (52 shorter events, 0.5 us)
Async XLA Ops:
  6.5 1.9 %collective-permute-start.1 = (bf16[3,2,2,128,128]{4,3,2,1,0:T(8,128)(2,1)S(1)}, bf16[3,2,2,128,128]{4,3,2,1,0:T(8,128)(2,1)S(1)}, u32[]{:S(2)}, u32[]{:S(2)}) collective-permute-start(bf16[3,2,2,128,128]{4,3,2,1,0:T(8,128)(2,1)S(1)} %get-tuple-element.44), channel_id=1, source_target_pairs={{0,1},{1,0},{2,3},{3,2},{4,5},{5,4},{6,7},{7,6},{8,9},{9,8},{10,11... | collective-permute-start | bytes 1179656 | tf_op jit(solution)/shard_map/ppermute | solution.py:346
  7.0 4.4 %collective-permute-start = (bf16[5,2,2,128,128]{4,3,2,1,0:T(8,128)(2,1)S(1)}, bf16[5,2,2,128,128]{4,3,2,1,0:T(8,128)(2,1)S(1)}, u32[]{:S(2)}, u32[]{:S(2)}) collective-permute-start(bf16[5,2,2,128,128]{4,3,2,1,0:T(8,128)(2,1)S(1)} %get-tuple-element.42), channel_id=1, source_target_pairs={{0,1},{1,0},{2,3},{3,2},{4,5},{5,4},{6,7},{7,6},{8,9},{9,8},{10,11... | collective-permute-start | bytes 1966088 | tf_op jit(solution)/shard_map/ppermute | solution.py:346
  8.5 6.9 %collective-permute-start.9 = (bf16[1,2,2,128,128]{4,3,2,1,0:T(8,128)(2,1)S(1)}, bf16[1,2,2,128,128]{4,3,2,1,0:T(8,128)(2,1)S(1)}, u32[]{:S(2)}, u32[]{:S(2)}) collective-permute-start(bf16[1,2,2,128,128]{4,3,2,1,0:T(8,128)(2,1)S(1)} %shard_map.75), channel_id=1, source_target_pairs={{0,2},{1,3},{2,0},{3,1},{4,6},{5,7},{6,4},{7,5},{8,10},{9,11},{10,... | collective-permute-start | bytes 393224 | tf_op jit(solution)/shard_map/ppermute | solution.py:346
  11.4 0.7 %copy-start.3 = (s32[2,8]{1,0:T(2,128)S(1)}, s32[2,8]{1,0:T(2,128)}, u32[]{:S(2)}) copy-start(s32[2,8]{1,0:T(2,128)} %param.12) | copy-start | bytes 196
  11.4 0.7 %copy-start.1 = (s32[2,8,7]{1,0,2:T(2,128)S(1)}, s32[2,8,7]{1,0,2:T(2,128)}, u32[]{:S(2)}) copy-start(s32[2,8,7]{1,0,2:T(2,128)} %param.10) | copy-start | bytes 1348
  11.4 0.7 %copy-start.2 = (s32[2,8,7]{1,0,2:T(2,128)S(1)}, s32[2,8,7]{1,0,2:T(2,128)}, u32[]{:S(2)}) copy-start(s32[2,8,7]{1,0,2:T(2,128)} %param.11) | copy-start | bytes 1348
  12.4 3.0 %collective-permute-start.2 = (bf16[16,128]{1,0:T(8,128)(2,1)S(1)}, bf16[16,128]{1,0:T(8,128)(2,1)S(1)}, u32[]{:S(2)}, u32[]{:S(2)}) collective-permute-start(bf16[16,128]{1,0:T(8,128)(2,1)S(1)} %pad.5.refs_0_.own_ref), channel_id=1, source_target_pairs={{0,1},{1,0},{2,3},{3,2},{4,5},{5,4},{6,7},{7,6},{8,9},{9,8},{10,11... | collective-permute-start | bytes 12296 | tf_op jit(solution)/shard_map/ppermute | solution.py:346
  12.4 6.4 %collective-permute-start.6 = (bf16[1,2,2,128,128]{4,3,2,1,0:T(8,128)(2,1)S(1)}, bf16[1,2,2,128,128]{4,3,2,1,0:T(8,128)(2,1)S(1)}, u32[]{:S(2)}, u32[]{:S(2)}) collective-permute-start(bf16[1,2,2,128,128]{4,3,2,1,0:T(8,128)(2,1)S(1)} %shard_map.76), channel_id=1, source_target_pairs={{0,2},{1,3},{2,0},{3,1},{4,6},{5,7},{6,4},{7,5},{8,10},{9,11},{10,... | collective-permute-start | bytes 393224 | tf_op jit(solution)/shard_map/ppermute | solution.py:346
  13.3 8.3 %collective-permute-start.3 = (bf16[1,2,2,128,128]{4,3,2,1,0:T(8,128)(2,1)S(1)}, bf16[1,2,2,128,128]{4,3,2,1,0:T(8,128)(2,1)S(1)}, u32[]{:S(2)}, u32[]{:S(2)}) collective-permute-start(bf16[1,2,2,128,128]{4,3,2,1,0:T(8,128)(2,1)S(1)} %shard_map.77), channel_id=1, source_target_pairs={{0,2},{1,3},{2,0},{3,1},{4,6},{5,7},{6,4},{7,5},{8,10},{9,11},{10,... | collective-permute-start | bytes 393224 | tf_op jit(solution)/shard_map/ppermute | solution.py:346
  14.5 10.8 %collective-permute-start.12 = (bf16[1,2,2,128,128]{4,3,2,1,0:T(8,128)(2,1)S(1)}, bf16[1,2,2,128,128]{4,3,2,1,0:T(8,128)(2,1)S(1)}, u32[]{:S(2)}, u32[]{:S(2)}) collective-permute-start(bf16[1,2,2,128,128]{4,3,2,1,0:T(8,128)(2,1)S(1)} %shard_map.74), channel_id=1, source_target_pairs={{0,2},{1,3},{2,0},{3,1},{4,6},{5,7},{6,4},{7,5},{8,10},{9,11},{10,... | collective-permute-start | bytes 393224 | tf_op jit(solution)/shard_map/ppermute | solution.py:346
  15.4 10.7 %collective-permute-start.10 = (bf16[2,272,128]{2,1,0:T(8,128)(2,1)S(1)}, bf16[2,272,128]{2,1,0:T(8,128)(2,1)S(1)}, u32[]{:S(2)}, u32[]{:S(2)}) collective-permute-start(bf16[2,272,128]{2,1,0:T(8,128)(2,1)S(1)} %shard_map.82), channel_id=1, source_target_pairs={{0,16},{1,21},{2,18},{3,23},{4,20},{5,17},{6,22},{7,19},{8,24},{9,... | collective-permute-start | bytes 417800 | tf_op jit(solution)/shard_map/ppermute | solution.py:351
  18.9 8.7 %collective-permute-start.7 = (bf16[2,272,128]{2,1,0:T(8,128)(2,1)S(1)}, bf16[2,272,128]{2,1,0:T(8,128)(2,1)S(1)}, u32[]{:S(2)}, u32[]{:S(2)}) collective-permute-start(bf16[2,272,128]{2,1,0:T(8,128)(2,1)S(1)} %shard_map.80), channel_id=1, source_target_pairs={{0,8},{1,13},{2,10},{3,15},{4,12},{5,9},{6,14},{7,11},{8,0},{9,5},... | collective-permute-start | bytes 417800 | tf_op jit(solution)/shard_map/ppermute | solution.py:351
  21.7 8.1 %collective-permute-start.4 = (bf16[2,272,128]{2,1,0:T(8,128)(2,1)S(1)}, bf16[2,272,128]{2,1,0:T(8,128)(2,1)S(1)}, u32[]{:S(2)}, u32[]{:S(2)}) collective-permute-start(bf16[2,272,128]{2,1,0:T(8,128)(2,1)S(1)} %shard_map.78), channel_id=1, source_target_pairs={{0,24},{1,29},{2,26},{3,31},{4,28},{5,25},{6,30},{7,27},{8,16},{9,... | collective-permute-start | bytes 417800 | tf_op jit(solution)/shard_map/ppermute | solution.py:351
  25.4 4.4 %collective-permute-start.13 = (bf16[2,272,128]{2,1,0:T(8,128)(2,1)S(1)}, bf16[2,272,128]{2,1,0:T(8,128)(2,1)S(1)}, u32[]{:S(2)}, u32[]{:S(2)}) collective-permute-start(bf16[2,272,128]{2,1,0:T(8,128)(2,1)S(1)} %shard_map.84), channel_id=1, source_target_pairs={{0,0},{1,5},{2,2},{3,7},{4,4},{5,1},{6,6},{7,3},{8,8},{9,13},{10,1... | collective-permute-start | bytes 417800 | tf_op jit(solution)/shard_map/ppermute | solution.py:351
  26.1 5.0 %collective-permute-start.11 = (bf16[1,272,128]{2,1,0:T(8,128)(2,1)S(1)}, bf16[1,272,128]{2,1,0:T(8,128)(2,1)S(1)}, u32[]{:S(2)}, u32[]{:S(2)}) collective-permute-start(bf16[1,272,128]{2,1,0:T(8,128)(2,1)S(1)} %shard_map.83), channel_id=1, source_target_pairs={{0,1},{1,0},{2,3},{3,2},{4,5},{5,4},{6,7},{7,6},{8,9},{9,8},{10,11... | collective-permute-start | bytes 208904 | tf_op jit(solution)/shard_map/ppermute | solution.py:346
  27.5 3.6 %collective-permute-start.8 = (bf16[1,272,128]{2,1,0:T(8,128)(2,1)S(1)}, bf16[1,272,128]{2,1,0:T(8,128)(2,1)S(1)}, u32[]{:S(2)}, u32[]{:S(2)}) collective-permute-start(bf16[1,272,128]{2,1,0:T(8,128)(2,1)S(1)} %shard_map.81), channel_id=1, source_target_pairs={{0,1},{1,0},{2,3},{3,2},{4,5},{5,4},{6,7},{7,6},{8,9},{9,8},{10,11... | collective-permute-start | bytes 208904 | tf_op jit(solution)/shard_map/ppermute | solution.py:346
  29.8 1.3 %collective-permute-start.5 = (bf16[1,272,128]{2,1,0:T(8,128)(2,1)S(1)}, bf16[1,272,128]{2,1,0:T(8,128)(2,1)S(1)}, u32[]{:S(2)}, u32[]{:S(2)}) collective-permute-start(bf16[1,272,128]{2,1,0:T(8,128)(2,1)S(1)} %shard_map.79), channel_id=1, source_target_pairs={{0,1},{1,0},{2,3},{3,2},{4,5},{5,4},{6,7},{7,6},{8,9},{9,8},{10,11... | collective-permute-start | bytes 208904 | tf_op jit(solution)/shard_map/ppermute | solution.py:346
  29.8 2.2 %collective-permute-start.14 = (bf16[1,272,128]{2,1,0:T(8,128)(2,1)S(1)}, bf16[1,272,128]{2,1,0:T(8,128)(2,1)S(1)}, u32[]{:S(2)}, u32[]{:S(2)}) collective-permute-start(bf16[1,272,128]{2,1,0:T(8,128)(2,1)S(1)} %shard_map.85), channel_id=1, source_target_pairs={{0,1},{1,0},{2,3},{3,2},{4,5},{5,4},{6,7},{7,6},{8,9},{9,8},{10,11... | collective-permute-start | bytes 208904 | tf_op jit(solution)/shard_map/ppermute | solution.py:346
  35.6 1.6 %collective-permute-start.15 = (bf16[4,2,128,128]{3,2,1,0:T(8,128)(2,1)S(1)}, bf16[4,2,128,128]{3,2,1,0:T(8,128)(2,1)S(1)}, u32[]{:S(2)}, u32[]{:S(2)}) collective-permute-start(bf16[4,2,128,128]{3,2,1,0:T(8,128)(2,1)S(1)} %get-tuple-element.68), channel_id=1, source_target_pairs={{0,1},{1,0},{2,3},{3,2},{4,5},{5,4},{6,7},{7,6},{8,9},{9,8},{10,11... | collective-permute-start | bytes 786440 | tf_op jit(solution)/shard_map/ppermute | solution.py:346
  37.3 6.1 %collective-permute-start.19 = (bf16[2,2,128,128]{3,2,1,0:T(8,128)(2,1)S(1)}, bf16[2,2,128,128]{3,2,1,0:T(8,128)(2,1)S(1)}, u32[]{:S(2)}, u32[]{:S(2)}) collective-permute-start(bf16[2,2,128,128]{3,2,1,0:T(8,128)(2,1)S(1)} %get-tuple-element.71), channel_id=1, source_target_pairs={{0,8},{1,13},{2,10},{3,15},{4,12},{5,9},{6,14},{7,11},{8,0},{9,5},... | collective-permute-start | bytes 393224 | tf_op jit(solution)/shard_map/ppermute | solution.py:351
  39.0 4.4 %collective-permute-start.20 = (bf16[2,2,128,128]{3,2,1,0:T(8,128)(2,1)S(1)}, bf16[2,2,128,128]{3,2,1,0:T(8,128)(2,1)S(1)}, u32[]{:S(2)}, u32[]{:S(2)}) collective-permute-start(bf16[2,2,128,128]{3,2,1,0:T(8,128)(2,1)S(1)} %get-tuple-element.72), channel_id=1, source_target_pairs={{0,0},{1,5},{2,2},{3,7},{4,4},{5,1},{6,6},{7,3},{8,8},{9,13},{10,1... | collective-permute-start | bytes 393224 | tf_op jit(solution)/shard_map/ppermute | solution.py:351
  39.6 9.5 %collective-permute-start.18 = (bf16[2,2,128,128]{3,2,1,0:T(8,128)(2,1)S(1)}, bf16[2,2,128,128]{3,2,1,0:T(8,128)(2,1)S(1)}, u32[]{:S(2)}, u32[]{:S(2)}) collective-permute-start(bf16[2,2,128,128]{3,2,1,0:T(8,128)(2,1)S(1)} %get-tuple-element.70), channel_id=1, source_target_pairs={{0,24},{1,29},{2,26},{3,31},{4,28},{5,25},{6,30},{7,27},{8,16},{9,... | collective-permute-start | bytes 393224 | tf_op jit(solution)/shard_map/ppermute | solution.py:351
  43.1 11.9 %collective-permute-start.16 = (bf16[2,2,128,128]{3,2,1,0:T(8,128)(2,1)S(1)}, bf16[2,2,128,128]{3,2,1,0:T(8,128)(2,1)S(1)}, u32[]{:S(2)}, u32[]{:S(2)}) collective-permute-start(bf16[2,2,128,128]{3,2,1,0:T(8,128)(2,1)S(1)} %get-tuple-element.69), channel_id=1, source_target_pairs={{0,16},{1,21},{2,18},{3,23},{4,20},{5,17},{6,22},{7,19},{8,24},{9,... | collective-permute-start | bytes 393224 | tf_op jit(solution)/shard_map/ppermute | solution.py:351
  43.4 8.1 %collective-permute-start.21 = (bf16[2,2,2,128,128]{4,3,2,1,0:T(8,128)(2,1)S(1)}, bf16[2,2,2,128,128]{4,3,2,1,0:T(8,128)(2,1)S(1)}, u32[]{:S(2)}, u32[]{:S(2)}) collective-permute-start(bf16[2,2,2,128,128]{4,3,2,1,0:T(8,128)(2,1)S(1)} %shard_map.90.rest_2_), channel_id=1, source_target_pairs={{0,2},{1,3},{2,0},{3,1},{4,6},{5,7},{6,4},{7,5},{8,10},{9,11},{10,... | collective-permute-start | bytes 786440 | tf_op jit(solution)/shard_map/ppermute | solution.py:346
  44.5 12.4 %collective-permute-start.22 = (bf16[2,2,2,128,128]{4,3,2,1,0:T(8,128)(2,1)S(1)}, bf16[2,2,2,128,128]{4,3,2,1,0:T(8,128)(2,1)S(1)}, u32[]{:S(2)}, u32[]{:S(2)}) collective-permute-start(bf16[2,2,2,128,128]{4,3,2,1,0:T(8,128)(2,1)S(1)} %shard_map.90.rest_2_), channel_id=1, source_target_pairs={{0,1},{1,0},{2,3},{3,2},{4,5},{5,4},{6,7},{7,6},{8,9},{9,8},{10,11... | collective-permute-start | bytes 786440 | tf_op jit(solution)/shard_map/ppermute | solution.py:346
  49.1 7.9 %slice-start = ((s8[8388608]{0:T(1024)(128)(4,1)}), s8[4194304]{0:T(1024)(128)(4,1)S(1)}, s32[]{:S(2)}) async-start(s8[8388608]{0:T(1024)(128)(4,1)} %bitcast.9), calls=%async_computation | async-start | bytes 8388608
  49.1 7.9 %slice-start.1 = ((s8[8388608]{0:T(1024)(128)(4,1)}), s8[4194304]{0:T(1024)(128)(4,1)S(1)}, s32[]{:S(2)}) async-start(s8[8388608]{0:T(1024)(128)(4,1)} %bitcast.9), calls=%async_computation.1 | async-start | bytes 8388608
  49.1 7.9 %copy-start = (s32[2,64]{1,0:T(2,128)S(1)}, s32[2,64]{1,0:T(2,128)}, u32[]{:S(2)}) copy-start(s32[2,64]{1,0:T(2,128)} %dir_ref.3) | copy-start | bytes 1540
  49.2 6.5 %collective-permute-start.24 = (bf16[1,2,2,128,128]{4,3,2,1,0:T(8,128)(2,1)S(1)}, bf16[1,2,2,128,128]{4,3,2,1,0:T(8,128)(2,1)S(1)}, u32[]{:S(2)}, u32[]{:S(2)}) collective-permute-start(bf16[1,2,2,128,128]{4,3,2,1,0:T(8,128)(2,1)S(1)} %shard_map.89.rest_0_), channel_id=1, source_target_pairs={{0,2},{1,3},{2,0},{3,1},{4,6},{5,7},{6,4},{7,5},{8,10},{9,11},{10,... | collective-permute-start | bytes 393224 | tf_op jit(solution)/shard_map/ppermute | solution.py:346
  50.5 5.2 %collective-permute-start.25 = (bf16[1,2,2,128,128]{4,3,2,1,0:T(8,128)(2,1)S(1)}, bf16[1,2,2,128,128]{4,3,2,1,0:T(8,128)(2,1)S(1)}, u32[]{:S(2)}, u32[]{:S(2)}) collective-permute-start(bf16[1,2,2,128,128]{4,3,2,1,0:T(8,128)(2,1)S(1)} %shard_map.89.rest_0_), channel_id=1, source_target_pairs={{0,1},{1,0},{2,3},{3,2},{4,5},{5,4},{6,7},{7,6},{8,9},{9,8},{10,11... | collective-permute-start | bytes 393224 | tf_op jit(solution)/shard_map/ppermute | solution.py:346
  51.5 5.5 %collective-permute-start.23 = (bf16[2,2,2,128,128]{4,3,2,1,0:T(8,128)(2,1)S(1)}, bf16[2,2,2,128,128]{4,3,2,1,0:T(8,128)(2,1)S(1)}, u32[]{:S(2)}, u32[]{:S(2)}) collective-permute-start(bf16[2,2,2,128,128]{4,3,2,1,0:T(8,128)(2,1)S(1)} %collective-permute-done.21.rest_3_), channel_id=1, source_target_pairs={{0,1},{1,0},{2,3},{3,2},{4,5},{5,4},{6,7},{7,6},{8,9},{9,8},{10,11... | collective-permute-start | bytes 786440 | tf_op jit(solution)/shard_map/ppermute | solution.py:346
  55.0 1.9 %collective-permute-start.27 = (bf16[1,2,2,128,128]{4,3,2,1,0:T(8,128)(2,1)S(1)}, bf16[1,2,2,128,128]{4,3,2,1,0:T(8,128)(2,1)S(1)}, u32[]{:S(2)}, u32[]{:S(2)}) collective-permute-start(bf16[1,2,2,128,128]{4,3,2,1,0:T(8,128)(2,1)S(1)} %shard_map.88.rest_1_), channel_id=1, source_target_pairs={{0,1},{1,0},{2,3},{3,2},{4,5},{5,4},{6,7},{7,6},{8,9},{9,8},{10,11... | collective-permute-start | bytes 393224 | tf_op jit(solution)/shard_map/ppermute | solution.py:346
  55.6 1.3 %collective-permute-start.26 = (bf16[1,2,2,128,128]{4,3,2,1,0:T(8,128)(2,1)S(1)}, bf16[1,2,2,128,128]{4,3,2,1,0:T(8,128)(2,1)S(1)}, u32[]{:S(2)}, u32[]{:S(2)}) collective-permute-start(bf16[1,2,2,128,128]{4,3,2,1,0:T(8,128)(2,1)S(1)} %collective-permute-done.24.rest_6_), channel_id=1, source_target_pairs={{0,1},{1,0},{2,3},{3,2},{4,5},{5,4},{6,7},{7,6},{8,9},{9,8},{10,11... | collective-permute-start | bytes 393224 | tf_op jit(solution)/shard_map/ppermute | solution.py:346
  55.7 5.8 %collective-permute-start.17 = (bf16[1,2,2,128,128]{4,3,2,1,0:T(8,128)(2,1)S(1)}, bf16[1,2,2,128,128]{4,3,2,1,0:T(8,128)(2,1)S(1)}, u32[]{:S(2)}, u32[]{:S(2)}) collective-permute-start(bf16[1,2,2,128,128]{4,3,2,1,0:T(8,128)(2,1)S(1)} %shard_map.88.rest_1_), channel_id=1, source_target_pairs={{0,2},{1,3},{2,0},{3,1},{4,6},{5,7},{6,4},{7,5},{8,10},{9,11},{10,... | collective-permute-start | bytes 393224 | tf_op jit(solution)/shard_map/ppermute | solution.py:346
  61.6 1.3 %collective-permute-start.28 = (bf16[1,2,2,128,128]{4,3,2,1,0:T(8,128)(2,1)S(1)}, bf16[1,2,2,128,128]{4,3,2,1,0:T(8,128)(2,1)S(1)}, u32[]{:S(2)}, u32[]{:S(2)}) collective-permute-start(bf16[1,2,2,128,128]{4,3,2,1,0:T(8,128)(2,1)S(1)} %collective-permute-done.17.rest_0_), channel_id=1, source_target_pairs={{0,1},{1,0},{2,3},{3,2},{4,5},{5,4},{6,7},{7,6},{8,9},{9,8},{10,11... | collective-permute-start | bytes 393224 | tf_op jit(solution)/shard_map/ppermute | solution.py:346

commit v6 on v5

--- a/solution.py
+++ b/solution.py
@@ -62,9 +62,10 @@
                     copies[-1].start()
         flying.append(copies)
 
-    for group in groups[:2]:
+    start(groups[0])
+    coef_copy.wait()
+    for group in groups[1:2]:
         start(group)
-    coef_copy.wait()
     dir_copy.wait()
     for number, group in enumerate(groups):
         for copy in flying[number]:

time: 65.4 us -> 65.3 us (level)
  no operation moved by 1% of the time
where the time goes in v6:
time: 65.3 us; the launch traced here: 65 us
  starting transfers between devices  33 us (51%)
  waiting for transfers between devices  15.8 us (24%)
  Pallas kernels  15 us (23%)
  local copies, waits for them, and re-layouts  0.89 us (1%)
    ppermute x21, starting transfers between devices, family(): return lax.ppermute(x, 'gy', [(i, i ^ rel) for i in range(ny)])  18.5 us
    ppermute x8, starting transfers between devices, partner(): return lax.ppermute(x, axes, [(i, i ^ moves[i & 1]) for i in range(size)])  14.5 us
    ppermute x21, waiting for transfers between devices, family(): return lax.ppermute(x, 'gy', [(i, i ^ rel) for i in range(ny)])  8.73 us
    ppermute x8, waiting for transfers between devices, partner(): return lax.ppermute(x, axes, [(i, i ^ moves[i & 1]) for i in range(size)])  7.06 us
    pallas_call x1, Pallas kernels, up(): pl.pallas_call(functools.partial(up_kernel, jobs), out_shape=shapes + [ja...  6.3 us
    pallas_call x2, Pallas kernels, down(): pl.pallas_call(functools.partial(down_kernel, jobs, last), out_shape=jax....  4.61 us
    pallas_call x1, Pallas kernels, couple(): pl.pallas_call(functools.partial(couple_kernel, sizes), out_shape=[jax.Sh...  3.63 us
  transfers between devices with their start and end apart: 29, of which 12 were waited for; matrix products, arithmetic and copies ran while one was open for 0% of the time, Pallas kernels for 4%

profile of v6, /device:TPU:0, one launch (start us, length us, event | category | flops | bytes accessed | tf_op | source)
XLA Modules:
  0.0 65.0 jit_solution(9425731187406300394)
XLA Ops:
  0.0 0.1 pad_add_fusion.at_ref
  0.1 6.3 %shard_map.73 = (bf16[3,2,2,128,128]{4,3,2,1,0:T(8,128)(2,1)S(1)}, bf16[5,2,2,128,128]{4,3,2,1,0:T(8,128)(2,1)S(1)}, bf16[1,2,2,128,128]{4,3,2,1,0:T(8,128)(2,1)...) custom-call(s32[3]{0:T(128)S(1)} %pad_add_fusion.at_ref, ...), custom_call_target="tpu_custom_call" | custom-call | flops 10000000000 | bytes 1000000 | tf_op jit(solution)/shard_map/pallas_call | solution.py:105
  6.4 0.5 collective-permute-start.1
  6.9 0.1 collective-permute-start
  7.0 1.3 %collective-permute-done.1.refs_1_ = bf16[3,2,2,128,128]{4,3,2,1,0:T(8,128)(2,1)S(1)} collective-permute-done((bf16[3,2,2,128,128]{4,3,2,1,0:T(8,128)(2,1)S(1)}, bf16[3,2,2,128,128]{4,3,2,1,0:T(8,128)(2,1)S(1)}, u32[]{:S(2)}, u32[]{:S(2)}) %collective-permute-start.1) | collective-permute-done | bytes 393248 | tf_op jit(solution)/shard_map/ppermute | solution.py:347
  8.4 2.9 %collective-permute-start.9 = (bf16[1,2,2,128,128]{4,3,2,1,0:T(8,128)(2,1)S(1)}, bf16[1,2,2,128,128]{4,3,2,1,0:T(8,128)(2,1)S(1)}, u32[]{:S(2)}, u32[]{:S(2)}) collective-permute-start(bf16[1,2,2,128,128]{4,3,2,1,0:T(8,128)(2,1)S(1)} %shard_map.75), channel_id=1, source_target_pairs={{0,2},{1,3},{2,0},{3,1},{4,6},{5,7},{6,4},{7,5},{8,10},{9,11},{10,... | collective-permute-start | bytes 393224 | tf_op jit(solution)/shard_map/ppermute | solution.py:347
  11.4 0.6 copy-done.3
  12.1 0.1 copy.8
  12.2 0.1 reshape.12
  12.3 0.1 collective-permute-start.2
  12.3 0.9 %collective-permute-start.6 = (bf16[1,2,2,128,128]{4,3,2,1,0:T(8,128)(2,1)S(1)}, bf16[1,2,2,128,128]{4,3,2,1,0:T(8,128)(2,1)S(1)}, u32[]{:S(2)}, u32[]{:S(2)}) collective-permute-start(bf16[1,2,2,128,128]{4,3,2,1,0:T(8,128)(2,1)S(1)} %shard_map.76), channel_id=1, source_target_pairs={{0,2},{1,3},{2,0},{3,1},{4,6},{5,7},{6,4},{7,5},{8,10},{9,11},{10,... | collective-permute-start | bytes 393224 | tf_op jit(solution)/shard_map/ppermute | solution.py:347
  13.2 1.2 %collective-permute-start.3 = (bf16[1,2,2,128,128]{4,3,2,1,0:T(8,128)(2,1)S(1)}, bf16[1,2,2,128,128]{4,3,2,1,0:T(8,128)(2,1)S(1)}, u32[]{:S(2)}, u32[]{:S(2)}) collective-permute-start(bf16[1,2,2,128,128]{4,3,2,1,0:T(8,128)(2,1)S(1)} %shard_map.77), channel_id=1, source_target_pairs={{0,2},{1,3},{2,0},{3,1},{4,6},{5,7},{6,4},{7,5},{8,10},{9,11},{10,... | collective-permute-start | bytes 393224 | tf_op jit(solution)/shard_map/ppermute | solution.py:347
  14.4 0.8 %collective-permute-start.12 = (bf16[1,2,2,128,128]{4,3,2,1,0:T(8,128)(2,1)S(1)}, bf16[1,2,2,128,128]{4,3,2,1,0:T(8,128)(2,1)S(1)}, u32[]{:S(2)}, u32[]{:S(2)}) collective-permute-start(bf16[1,2,2,128,128]{4,3,2,1,0:T(8,128)(2,1)S(1)} %shard_map.74), channel_id=1, source_target_pairs={{0,2},{1,3},{2,0},{3,1},{4,6},{5,7},{6,4},{7,5},{8,10},{9,11},{10,... | collective-permute-start | bytes 393224 | tf_op jit(solution)/shard_map/ppermute | solution.py:347
  15.3 2.7 %collective-permute-start.10 = (bf16[2,272,128]{2,1,0:T(8,128)(2,1)S(1)}, bf16[2,272,128]{2,1,0:T(8,128)(2,1)S(1)}, u32[]{:S(2)}, u32[]{:S(2)}) collective-permute-start(bf16[2,272,128]{2,1,0:T(8,128)(2,1)S(1)} %shard_map.82), channel_id=1, source_target_pairs={{0,16},{1,21},{2,18},{3,23},{4,20},{5,17},{6,22},{7,19},{8,24},{9,... | collective-permute-start | bytes 417800 | tf_op jit(solution)/shard_map/ppermute | solution.py:352
  18.1 0.6 collective-permute-done.6.refs_4_
  18.7 0.1 shard_map.80
  18.8 1.6 %collective-permute-start.7 = (bf16[2,272,128]{2,1,0:T(8,128)(2,1)S(1)}, bf16[2,272,128]{2,1,0:T(8,128)(2,1)S(1)}, u32[]{:S(2)}, u32[]{:S(2)}) collective-permute-start(bf16[2,272,128]{2,1,0:T(8,128)(2,1)S(1)} %shard_map.80), channel_id=1, source_target_pairs={{0,8},{1,13},{2,10},{3,15},{4,12},{5,9},{6,14},{7,11},{8,0},{9,5},... | collective-permute-start | bytes 417800 | tf_op jit(solution)/shard_map/ppermute | solution.py:352
  20.4 1.1 %collective-permute-done.3.refs_4_ = bf16[1,2,2,128,128]{4,3,2,1,0:T(8,128)(2,1)S(1)} collective-permute-done((bf16[1,2,2,128,128]{4,3,2,1,0:T(8,128)(2,1)S(1)}, bf16[1,2,2,128,128]{4,3,2,1,0:T(8,128)(2,1)S(1)}, u32[]{:S(2)}, u32[]{:S(2)}) %collective-permute-start.3) | collective-permute-done | bytes 131104 | tf_op jit(solution)/shard_map/ppermute | solution.py:347
  21.6 3.7 %collective-permute-start.4 = (bf16[2,272,128]{2,1,0:T(8,128)(2,1)S(1)}, bf16[2,272,128]{2,1,0:T(8,128)(2,1)S(1)}, u32[]{:S(2)}, u32[]{:S(2)}) collective-permute-start(bf16[2,272,128]{2,1,0:T(8,128)(2,1)S(1)} %shard_map.78), channel_id=1, source_target_pairs={{0,24},{1,29},{2,26},{3,31},{4,28},{5,25},{6,30},{7,27},{8,16},{9,... | collective-permute-start | bytes 417800 | tf_op jit(solution)/shard_map/ppermute | solution.py:352
  25.2 0.1 shard_map.84
  25.3 0.7 %collective-permute-start.13 = (bf16[2,272,128]{2,1,0:T(8,128)(2,1)S(1)}, bf16[2,272,128]{2,1,0:T(8,128)(2,1)S(1)}, u32[]{:S(2)}, u32[]{:S(2)}) collective-permute-start(bf16[2,272,128]{2,1,0:T(8,128)(2,1)S(1)} %shard_map.84), channel_id=1, source_target_pairs={{0,0},{1,5},{2,2},{3,7},{4,4},{5,1},{6,6},{7,3},{8,8},{9,13},{10,1... | collective-permute-start | bytes 417800 | tf_op jit(solution)/shard_map/ppermute | solution.py:352
  26.0 1.4 %collective-permute-start.11 = (bf16[1,272,128]{2,1,0:T(8,128)(2,1)S(1)}, bf16[1,272,128]{2,1,0:T(8,128)(2,1)S(1)}, u32[]{:S(2)}, u32[]{:S(2)}) collective-permute-start(bf16[1,272,128]{2,1,0:T(8,128)(2,1)S(1)} %shard_map.83), channel_id=1, source_target_pairs={{0,1},{1,0},{2,3},{3,2},{4,5},{5,4},{6,7},{7,6},{8,9},{9,8},{10,11... | collective-permute-start | bytes 208904 | tf_op jit(solution)/shard_map/ppermute | solution.py:347
  27.4 0.1 collective-permute-start.8
  27.5 2.2 %collective-permute-done.4.refs_0_ = bf16[2,272,128]{2,1,0:T(8,128)(2,1)S(1)} collective-permute-done((bf16[2,272,128]{2,1,0:T(8,128)(2,1)S(1)}, bf16[2,272,128]{2,1,0:T(8,128)(2,1)S(1)}, u32[]{:S(2)}, u32[]{:S(2)}) %collective-permute-start.4) | collective-permute-done | bytes 139296 | tf_op jit(solution)/shard_map/ppermute | solution.py:352
  29.7 1.3 %collective-permute-start.14 = (bf16[1,272,128]{2,1,0:T(8,128)(2,1)S(1)}, bf16[1,272,128]{2,1,0:T(8,128)(2,1)S(1)}, u32[]{:S(2)}, u32[]{:S(2)}) collective-permute-start(bf16[1,272,128]{2,1,0:T(8,128)(2,1)S(1)} %shard_map.85), channel_id=1, source_target_pairs={{0,1},{1,0},{2,3},{3,2},{4,5},{5,4},{6,7},{7,6},{8,9},{9,8},{10,11... | collective-permute-start | bytes 208904 | tf_op jit(solution)/shard_map/ppermute | solution.py:347
  31.0 0.9 %collective-permute-done.14.refs_7_ = bf16[1,272,128]{2,1,0:T(8,128)(2,1)S(1)} collective-permute-done((bf16[1,272,128]{2,1,0:T(8,128)(2,1)S(1)}, bf16[1,272,128]{2,1,0:T(8,128)(2,1)S(1)}, u32[]{:S(2)}, u32[]{:S(2)}) %collective-permute-start.14) | collective-permute-done | bytes 69664 | tf_op jit(solution)/shard_map/ppermute | solution.py:347
  31.9 3.6 %shard_map.86 = (bf16[4,2,128,128]{3,2,1,0:T(8,128)(2,1)S(1)}, bf16[4,2,128,128]{3,2,1,0:T(8,128)(2,1)S(1)}) custom-call(s32[3]{0:T(128)S(1)} %pad_add_fusion.at_ref, bf16[2,8,2,128,128]{4,3,2,1,0:T(8,128)(2,1)S(1)} %get-tuple-element.40.table_ref, bf16[16,128]{1,0:T(8,128)(2,1)S(1)} %pad.5.refs_0_.own_ref, ...), custom_call_target="tpu_custom_call" | custom-call | flops 10000000000 | bytes 1000000 | tf_op jit(solution)/shard_map/pallas_call | solution.py:263
  35.5 0.4 collective-permute-start.15
  36.0 1.2 %collective-permute-done.15.other_ref = bf16[4,2,128,128]{3,2,1,0:T(8,128)(2,1)S(1)} collective-permute-done((bf16[4,2,128,128]{3,2,1,0:T(8,128)(2,1)S(1)}, bf16[4,2,128,128]{3,2,1,0:T(8,128)(2,1)S(1)}, u32[]{:S(2)}, u32[]{:S(2)}) %collective-permute-start.15) | collective-permute-done | bytes 262176 | tf_op jit(solution)/shard_map/ppermute | solution.py:347
  37.2 1.7 %collective-permute-start.19 = (bf16[2,2,128,128]{3,2,1,0:T(8,128)(2,1)S(1)}, bf16[2,2,128,128]{3,2,1,0:T(8,128)(2,1)S(1)}, u32[]{:S(2)}, u32[]{:S(2)}) collective-permute-start(bf16[2,2,128,128]{3,2,1,0:T(8,128)(2,1)S(1)} %get-tuple-element.71), channel_id=1, source_target_pairs={{0,8},{1,13},{2,10},{3,15},{4,12},{5,9},{6,14},{7,11},{8,0},{9,5},... | collective-permute-start | bytes 393224 | tf_op jit(solution)/shard_map/ppermute | solution.py:352
  38.9 0.7 %collective-permute-start.20 = (bf16[2,2,128,128]{3,2,1,0:T(8,128)(2,1)S(1)}, bf16[2,2,128,128]{3,2,1,0:T(8,128)(2,1)S(1)}, u32[]{:S(2)}, u32[]{:S(2)}) collective-permute-start(bf16[2,2,128,128]{3,2,1,0:T(8,128)(2,1)S(1)} %get-tuple-element.72), channel_id=1, source_target_pairs={{0,0},{1,5},{2,2},{3,7},{4,4},{5,1},{6,6},{7,3},{8,8},{9,13},{10,1... | collective-permute-start | bytes 393224 | tf_op jit(solution)/shard_map/ppermute | solution.py:352
  39.5 3.4 %collective-permute-start.18 = (bf16[2,2,128,128]{3,2,1,0:T(8,128)(2,1)S(1)}, bf16[2,2,128,128]{3,2,1,0:T(8,128)(2,1)S(1)}, u32[]{:S(2)}, u32[]{:S(2)}) collective-permute-start(bf16[2,2,128,128]{3,2,1,0:T(8,128)(2,1)S(1)} %get-tuple-element.70), channel_id=1, source_target_pairs={{0,24},{1,29},{2,26},{3,31},{4,28},{5,25},{6,30},{7,27},{8,16},{9,... | collective-permute-start | bytes 393224 | tf_op jit(solution)/shard_map/ppermute | solution.py:352
  43.0 0.3 collective-permute-done.19.refs_0_
  43.3 1.2 %collective-permute-start.21 = (bf16[2,2,2,128,128]{4,3,2,1,0:T(8,128)(2,1)S(1)}, bf16[2,2,2,128,128]{4,3,2,1,0:T(8,128)(2,1)S(1)}, u32[]{:S(2)}, u32[]{:S(2)}) collective-permute-start(bf16[2,2,2,128,128]{4,3,2,1,0:T(8,128)(2,1)S(1)} %shard_map.90.rest_2_), channel_id=1, source_target_pairs={{0,2},{1,3},{2,0},{3,1},{4,6},{5,7},{6,4},{7,5},{8,10},{9,11},{10,... | collective-permute-start | bytes 786440 | tf_op jit(solution)/shard_map/ppermute | solution.py:347
  44.4 2.2 %collective-permute-start.22 = (bf16[2,2,2,128,128]{4,3,2,1,0:T(8,128)(2,1)S(1)}, bf16[2,2,2,128,128]{4,3,2,1,0:T(8,128)(2,1)S(1)}, u32[]{:S(2)}, u32[]{:S(2)}) collective-permute-start(bf16[2,2,2,128,128]{4,3,2,1,0:T(8,128)(2,1)S(1)} %shard_map.90.rest_2_), channel_id=1, source_target_pairs={{0,1},{1,0},{2,3},{3,2},{4,5},{5,4},{6,7},{7,6},{8,9},{9,8},{10,11... | collective-permute-start | bytes 786440 | tf_op jit(solution)/shard_map/ppermute | solution.py:347
  46.6 2.4 %collective-permute-done.18.refs_0_ = bf16[2,2,128,128]{3,2,1,0:T(8,128)(2,1)S(1)} collective-permute-done((bf16[2,2,128,128]{3,2,1,0:T(8,128)(2,1)S(1)}, bf16[2,2,128,128]{3,2,1,0:T(8,128)(2,1)S(1)}, u32[]{:S(2)}, u32[]{:S(2)}) %collective-permute-start.18) | collective-permute-done | bytes 131104 | tf_op jit(solution)/shard_map/ppermute | solution.py:352
  49.1 1.3 %collective-permute-start.24 = (bf16[1,2,2,128,128]{4,3,2,1,0:T(8,128)(2,1)S(1)}, bf16[1,2,2,128,128]{4,3,2,1,0:T(8,128)(2,1)S(1)}, u32[]{:S(2)}, u32[]{:S(2)}) collective-permute-start(bf16[1,2,2,128,128]{4,3,2,1,0:T(8,128)(2,1)S(1)} %shard_map.89.rest_0_), channel_id=1, source_target_pairs={{0,2},{1,3},{2,0},{3,1},{4,6},{5,7},{6,4},{7,5},{8,10},{9,11},{10,... | collective-permute-start | bytes 393224 | tf_op jit(solution)/shard_map/ppermute | solution.py:347
  50.4 1.0 %collective-permute-start.25 = (bf16[1,2,2,128,128]{4,3,2,1,0:T(8,128)(2,1)S(1)}, bf16[1,2,2,128,128]{4,3,2,1,0:T(8,128)(2,1)S(1)}, u32[]{:S(2)}, u32[]{:S(2)}) collective-permute-start(bf16[1,2,2,128,128]{4,3,2,1,0:T(8,128)(2,1)S(1)} %shard_map.89.rest_0_), channel_id=1, source_target_pairs={{0,1},{1,0},{2,3},{3,2},{4,5},{5,4},{6,7},{7,6},{8,9},{9,8},{10,11... | collective-permute-start | bytes 393224 | tf_op jit(solution)/shard_map/ppermute | solution.py:347
  51.4 1.3 %collective-permute-start.23 = (bf16[2,2,2,128,128]{4,3,2,1,0:T(8,128)(2,1)S(1)}, bf16[2,2,2,128,128]{4,3,2,1,0:T(8,128)(2,1)S(1)}, u32[]{:S(2)}, u32[]{:S(2)}) collective-permute-start(bf16[2,2,2,128,128]{4,3,2,1,0:T(8,128)(2,1)S(1)} %collective-permute-done.21.rest_3_), channel_id=1, source_target_pairs={{0,1},{1,0},{2,3},{3,2},{4,5},{5,4},{6,7},{7,6},{8,9},{9,8},{10,11... | collective-permute-start | bytes 786440 | tf_op jit(solution)/shard_map/ppermute | solution.py:347
  52.6 2.2 %collective-permute-done.16.refs_0_ = bf16[2,2,128,128]{3,2,1,0:T(8,128)(2,1)S(1)} collective-permute-done((bf16[2,2,128,128]{3,2,1,0:T(8,128)(2,1)S(1)}, bf16[2,2,128,128]{3,2,1,0:T(8,128)(2,1)S(1)}, u32[]{:S(2)}, u32[]{:S(2)}) %collective-permute-start.16) | collective-permute-done | bytes 131104 | tf_op jit(solution)/shard_map/ppermute | solution.py:352
  54.9 0.7 %collective-permute-start.27 = (bf16[1,2,2,128,128]{4,3,2,1,0:T(8,128)(2,1)S(1)}, bf16[1,2,2,128,128]{4,3,2,1,0:T(8,128)(2,1)S(1)}, u32[]{:S(2)}, u32[]{:S(2)}) collective-permute-start(bf16[1,2,2,128,128]{4,3,2,1,0:T(8,128)(2,1)S(1)} %shard_map.88.rest_1_), channel_id=1, source_target_pairs={{0,1},{1,0},{2,3},{3,2},{4,5},{5,4},{6,7},{7,6},{8,9},{9,8},{10,11... | collective-permute-start | bytes 393224 | tf_op jit(solution)/shard_map/ppermute | solution.py:347
  55.6 0.1 collective-permute-start.26
  55.6 1.1 %collective-permute-start.17 = (bf16[1,2,2,128,128]{4,3,2,1,0:T(8,128)(2,1)S(1)}, bf16[1,2,2,128,128]{4,3,2,1,0:T(8,128)(2,1)S(1)}, u32[]{:S(2)}, u32[]{:S(2)}) collective-permute-start(bf16[1,2,2,128,128]{4,3,2,1,0:T(8,128)(2,1)S(1)} %shard_map.88.rest_1_), channel_id=1, source_target_pairs={{0,2},{1,3},{2,0},{3,1},{4,6},{5,7},{6,4},{7,5},{8,10},{9,11},{10,... | collective-permute-start | bytes 393224 | tf_op jit(solution)/shard_map/ppermute | solution.py:347
  56.8 0.1 collective-permute-done.26.rest_8_
  56.9 2.4 %shard_map.91.rest_2_ = f32[2,16,128,128]{3,2,1,0:T(8,128)S(1)} custom-call(s32[3]{0:T(128)S(1)} %pad_add_fusion.at_ref, s32[2,64]{1,0:T(2,128)S(1)} %copy-done, bf16[2,2,4,4,2,2,128,128]{7,6,5,4,3,2,1,0:T(8,128)(2,1)S(1)} %bitcast.11, bf16[1,2,2,128,128]{4,3,2,1,0:T(8,128)(2,1)S(1)} %shard_map.89.rest_0_, ...), custom_call_target="tpu_custom_call" | custom-call | flops 10000000000 | bytes 1000000 | tf_op jit(solution)/shard_map/pallas_call | solution.py:314
  59.3 2.1 %collective-permute-done.17.rest_0_ = bf16[1,2,2,128,128]{4,3,2,1,0:T(8,128)(2,1)S(1)} collective-permute-done((bf16[1,2,2,128,128]{4,3,2,1,0:T(8,128)(2,1)S(1)}, bf16[1,2,2,128,128]{4,3,2,1,0:T(8,128)(2,1)S(1)}, u32[]{:S(2)}, u32[]{:S(2)}) %collective-permute-start.17) | collective-permute-done | bytes 131104 | tf_op jit(solution)/shard_map/ppermute | solution.py:347
  61.5 1.3 %collective-permute-done.28.rest_1_ = bf16[1,2,2,128,128]{4,3,2,1,0:T(8,128)(2,1)S(1)} collective-permute-done((bf16[1,2,2,128,128]{4,3,2,1,0:T(8,128)(2,1)S(1)}, bf16[1,2,2,128,128]{4,3,2,1,0:T(8,128)(2,1)S(1)}, u32[]{:S(2)}, u32[]{:S(2)}) %collective-permute-start.28) | collective-permute-done | bytes 131104 | tf_op jit(solution)/shard_map/ppermute | solution.py:347
  62.8 2.2 %shard_map.92 = bf16[2,16,128,128]{3,2,1,0:T(8,128)(2,1)} custom-call(s32[3]{0:T(128)S(1)} %pad_add_fusion.at_ref, s32[2,64]{1,0:T(2,128)S(1)} %copy-done, bf16[2,2,4,4,2,2,128,128]{7,6,5,4,3,2,1,0:T(8,128)(2,1)S(1)} %bitcast.12, bf16[1,2,2,128,128]{4,3,2,1,0:T(8,128)(2,1)S(1)} %collective-permute-done.17.rest_0_, ...), custom_call_target="tpu_custom_call" | custom-call | flops 10000000000 | bytes 1000000 | tf_op jit(solution)/shard_map/pallas_call | solution.py:314
  (52 shorter events, 0.5 us)
Async XLA Ops:
  6.4 1.9 %collective-permute-start.1 = (bf16[3,2,2,128,128]{4,3,2,1,0:T(8,128)(2,1)S(1)}, bf16[3,2,2,128,128]{4,3,2,1,0:T(8,128)(2,1)S(1)}, u32[]{:S(2)}, u32[]{:S(2)}) collective-permute-start(bf16[3,2,2,128,128]{4,3,2,1,0:T(8,128)(2,1)S(1)} %get-tuple-element.44), channel_id=1, source_target_pairs={{0,1},{1,0},{2,3},{3,2},{4,5},{5,4},{6,7},{7,6},{8,9},{9,8},{10,11... | collective-permute-start | bytes 1179656 | tf_op jit(solution)/shard_map/ppermute | solution.py:347
  6.9 4.4 %collective-permute-start = (bf16[5,2,2,128,128]{4,3,2,1,0:T(8,128)(2,1)S(1)}, bf16[5,2,2,128,128]{4,3,2,1,0:T(8,128)(2,1)S(1)}, u32[]{:S(2)}, u32[]{:S(2)}) collective-permute-start(bf16[5,2,2,128,128]{4,3,2,1,0:T(8,128)(2,1)S(1)} %get-tuple-element.42), channel_id=1, source_target_pairs={{0,1},{1,0},{2,3},{3,2},{4,5},{5,4},{6,7},{7,6},{8,9},{9,8},{10,11... | collective-permute-start | bytes 1966088 | tf_op jit(solution)/shard_map/ppermute | solution.py:347
  8.4 6.9 %collective-permute-start.9 = (bf16[1,2,2,128,128]{4,3,2,1,0:T(8,128)(2,1)S(1)}, bf16[1,2,2,128,128]{4,3,2,1,0:T(8,128)(2,1)S(1)}, u32[]{:S(2)}, u32[]{:S(2)}) collective-permute-start(bf16[1,2,2,128,128]{4,3,2,1,0:T(8,128)(2,1)S(1)} %shard_map.75), channel_id=1, source_target_pairs={{0,2},{1,3},{2,0},{3,1},{4,6},{5,7},{6,4},{7,5},{8,10},{9,11},{10,... | collective-permute-start | bytes 393224 | tf_op jit(solution)/shard_map/ppermute | solution.py:347
  11.3 0.7 %copy-start.3 = (s32[2,8]{1,0:T(2,128)S(1)}, s32[2,8]{1,0:T(2,128)}, u32[]{:S(2)}) copy-start(s32[2,8]{1,0:T(2,128)} %param.12) | copy-start | bytes 196
  11.3 0.7 %copy-start.1 = (s32[2,8,7]{1,0,2:T(2,128)S(1)}, s32[2,8,7]{1,0,2:T(2,128)}, u32[]{:S(2)}) copy-start(s32[2,8,7]{1,0,2:T(2,128)} %param.10) | copy-start | bytes 1348
  11.3 0.7 %copy-start.2 = (s32[2,8,7]{1,0,2:T(2,128)S(1)}, s32[2,8,7]{1,0,2:T(2,128)}, u32[]{:S(2)}) copy-start(s32[2,8,7]{1,0,2:T(2,128)} %param.11) | copy-start | bytes 1348
  12.3 3.0 %collective-permute-start.2 = (bf16[16,128]{1,0:T(8,128)(2,1)S(1)}, bf16[16,128]{1,0:T(8,128)(2,1)S(1)}, u32[]{:S(2)}, u32[]{:S(2)}) collective-permute-start(bf16[16,128]{1,0:T(8,128)(2,1)S(1)} %pad.5.refs_0_.own_ref), channel_id=1, source_target_pairs={{0,1},{1,0},{2,3},{3,2},{4,5},{5,4},{6,7},{7,6},{8,9},{9,8},{10,11... | collective-permute-start | bytes 12296 | tf_op jit(solution)/shard_map/ppermute | solution.py:347
  12.3 6.4 %collective-permute-start.6 = (bf16[1,2,2,128,128]{4,3,2,1,0:T(8,128)(2,1)S(1)}, bf16[1,2,2,128,128]{4,3,2,1,0:T(8,128)(2,1)S(1)}, u32[]{:S(2)}, u32[]{:S(2)}) collective-permute-start(bf16[1,2,2,128,128]{4,3,2,1,0:T(8,128)(2,1)S(1)} %shard_map.76), channel_id=1, source_target_pairs={{0,2},{1,3},{2,0},{3,1},{4,6},{5,7},{6,4},{7,5},{8,10},{9,11},{10,... | collective-permute-start | bytes 393224 | tf_op jit(solution)/shard_map/ppermute | solution.py:347
  13.2 8.3 %collective-permute-start.3 = (bf16[1,2,2,128,128]{4,3,2,1,0:T(8,128)(2,1)S(1)}, bf16[1,2,2,128,128]{4,3,2,1,0:T(8,128)(2,1)S(1)}, u32[]{:S(2)}, u32[]{:S(2)}) collective-permute-start(bf16[1,2,2,128,128]{4,3,2,1,0:T(8,128)(2,1)S(1)} %shard_map.77), channel_id=1, source_target_pairs={{0,2},{1,3},{2,0},{3,1},{4,6},{5,7},{6,4},{7,5},{8,10},{9,11},{10,... | collective-permute-start | bytes 393224 | tf_op jit(solution)/shard_map/ppermute | solution.py:347
  14.4 10.8 %collective-permute-start.12 = (bf16[1,2,2,128,128]{4,3,2,1,0:T(8,128)(2,1)S(1)}, bf16[1,2,2,128,128]{4,3,2,1,0:T(8,128)(2,1)S(1)}, u32[]{:S(2)}, u32[]{:S(2)}) collective-permute-start(bf16[1,2,2,128,128]{4,3,2,1,0:T(8,128)(2,1)S(1)} %shard_map.74), channel_id=1, source_target_pairs={{0,2},{1,3},{2,0},{3,1},{4,6},{5,7},{6,4},{7,5},{8,10},{9,11},{10,... | collective-permute-start | bytes 393224 | tf_op jit(solution)/shard_map/ppermute | solution.py:347
  15.3 10.7 %collective-permute-start.10 = (bf16[2,272,128]{2,1,0:T(8,128)(2,1)S(1)}, bf16[2,272,128]{2,1,0:T(8,128)(2,1)S(1)}, u32[]{:S(2)}, u32[]{:S(2)}) collective-permute-start(bf16[2,272,128]{2,1,0:T(8,128)(2,1)S(1)} %shard_map.82), channel_id=1, source_target_pairs={{0,16},{1,21},{2,18},{3,23},{4,20},{5,17},{6,22},{7,19},{8,24},{9,... | collective-permute-start | bytes 417800 | tf_op jit(solution)/shard_map/ppermute | solution.py:352
  18.8 8.7 %collective-permute-start.7 = (bf16[2,272,128]{2,1,0:T(8,128)(2,1)S(1)}, bf16[2,272,128]{2,1,0:T(8,128)(2,1)S(1)}, u32[]{:S(2)}, u32[]{:S(2)}) collective-permute-start(bf16[2,272,128]{2,1,0:T(8,128)(2,1)S(1)} %shard_map.80), channel_id=1, source_target_pairs={{0,8},{1,13},{2,10},{3,15},{4,12},{5,9},{6,14},{7,11},{8,0},{9,5},... | collective-permute-start | bytes 417800 | tf_op jit(solution)/shard_map/ppermute | solution.py:352
  21.6 8.1 %collective-permute-start.4 = (bf16[2,272,128]{2,1,0:T(8,128)(2,1)S(1)}, bf16[2,272,128]{2,1,0:T(8,128)(2,1)S(1)}, u32[]{:S(2)}, u32[]{:S(2)}) collective-permute-start(bf16[2,272,128]{2,1,0:T(8,128)(2,1)S(1)} %shard_map.78), channel_id=1, source_target_pairs={{0,24},{1,29},{2,26},{3,31},{4,28},{5,25},{6,30},{7,27},{8,16},{9,... | collective-permute-start | bytes 417800 | tf_op jit(solution)/shard_map/ppermute | solution.py:352
  25.3 4.4 %collective-permute-start.13 = (bf16[2,272,128]{2,1,0:T(8,128)(2,1)S(1)}, bf16[2,272,128]{2,1,0:T(8,128)(2,1)S(1)}, u32[]{:S(2)}, u32[]{:S(2)}) collective-permute-start(bf16[2,272,128]{2,1,0:T(8,128)(2,1)S(1)} %shard_map.84), channel_id=1, source_target_pairs={{0,0},{1,5},{2,2},{3,7},{4,4},{5,1},{6,6},{7,3},{8,8},{9,13},{10,1... | collective-permute-start | bytes 417800 | tf_op jit(solution)/shard_map/ppermute | solution.py:352
  26.0 5.0 %collective-permute-start.11 = (bf16[1,272,128]{2,1,0:T(8,128)(2,1)S(1)}, bf16[1,272,128]{2,1,0:T(8,128)(2,1)S(1)}, u32[]{:S(2)}, u32[]{:S(2)}) collective-permute-start(bf16[1,272,128]{2,1,0:T(8,128)(2,1)S(1)} %shard_map.83), channel_id=1, source_target_pairs={{0,1},{1,0},{2,3},{3,2},{4,5},{5,4},{6,7},{7,6},{8,9},{9,8},{10,11... | collective-permute-start | bytes 208904 | tf_op jit(solution)/shard_map/ppermute | solution.py:347
  27.4 3.6 %collective-permute-start.8 = (bf16[1,272,128]{2,1,0:T(8,128)(2,1)S(1)}, bf16[1,272,128]{2,1,0:T(8,128)(2,1)S(1)}, u32[]{:S(2)}, u32[]{:S(2)}) collective-permute-start(bf16[1,272,128]{2,1,0:T(8,128)(2,1)S(1)} %shard_map.81), channel_id=1, source_target_pairs={{0,1},{1,0},{2,3},{3,2},{4,5},{5,4},{6,7},{7,6},{8,9},{9,8},{10,11... | collective-permute-start | bytes 208904 | tf_op jit(solution)/shard_map/ppermute | solution.py:347
  29.7 1.3 %collective-permute-start.5 = (bf16[1,272,128]{2,1,0:T(8,128)(2,1)S(1)}, bf16[1,272,128]{2,1,0:T(8,128)(2,1)S(1)}, u32[]{:S(2)}, u32[]{:S(2)}) collective-permute-start(bf16[1,272,128]{2,1,0:T(8,128)(2,1)S(1)} %shard_map.79), channel_id=1, source_target_pairs={{0,1},{1,0},{2,3},{3,2},{4,5},{5,4},{6,7},{7,6},{8,9},{9,8},{10,11... | collective-permute-start | bytes 208904 | tf_op jit(solution)/shard_map/ppermute | solution.py:347
  29.7 2.2 %collective-permute-start.14 = (bf16[1,272,128]{2,1,0:T(8,128)(2,1)S(1)}, bf16[1,272,128]{2,1,0:T(8,128)(2,1)S(1)}, u32[]{:S(2)}, u32[]{:S(2)}) collective-permute-start(bf16[1,272,128]{2,1,0:T(8,128)(2,1)S(1)} %shard_map.85), channel_id=1, source_target_pairs={{0,1},{1,0},{2,3},{3,2},{4,5},{5,4},{6,7},{7,6},{8,9},{9,8},{10,11... | collective-permute-start | bytes 208904 | tf_op jit(solution)/shard_map/ppermute | solution.py:347
  35.5 1.6 %collective-permute-start.15 = (bf16[4,2,128,128]{3,2,1,0:T(8,128)(2,1)S(1)}, bf16[4,2,128,128]{3,2,1,0:T(8,128)(2,1)S(1)}, u32[]{:S(2)}, u32[]{:S(2)}) collective-permute-start(bf16[4,2,128,128]{3,2,1,0:T(8,128)(2,1)S(1)} %get-tuple-element.68), channel_id=1, source_target_pairs={{0,1},{1,0},{2,3},{3,2},{4,5},{5,4},{6,7},{7,6},{8,9},{9,8},{10,11... | collective-permute-start | bytes 786440 | tf_op jit(solution)/shard_map/ppermute | solution.py:347
  37.2 6.1 %collective-permute-start.19 = (bf16[2,2,128,128]{3,2,1,0:T(8,128)(2,1)S(1)}, bf16[2,2,128,128]{3,2,1,0:T(8,128)(2,1)S(1)}, u32[]{:S(2)}, u32[]{:S(2)}) collective-permute-start(bf16[2,2,128,128]{3,2,1,0:T(8,128)(2,1)S(1)} %get-tuple-element.71), channel_id=1, source_target_pairs={{0,8},{1,13},{2,10},{3,15},{4,12},{5,9},{6,14},{7,11},{8,0},{9,5},... | collective-permute-start | bytes 393224 | tf_op jit(solution)/shard_map/ppermute | solution.py:352
  38.9 4.4 %collective-permute-start.20 = (bf16[2,2,128,128]{3,2,1,0:T(8,128)(2,1)S(1)}, bf16[2,2,128,128]{3,2,1,0:T(8,128)(2,1)S(1)}, u32[]{:S(2)}, u32[]{:S(2)}) collective-permute-start(bf16[2,2,128,128]{3,2,1,0:T(8,128)(2,1)S(1)} %get-tuple-element.72), channel_id=1, source_target_pairs={{0,0},{1,5},{2,2},{3,7},{4,4},{5,1},{6,6},{7,3},{8,8},{9,13},{10,1... | collective-permute-start | bytes 393224 | tf_op jit(solution)/shard_map/ppermute | solution.py:352
  39.5 9.5 %collective-permute-start.18 = (bf16[2,2,128,128]{3,2,1,0:T(8,128)(2,1)S(1)}, bf16[2,2,128,128]{3,2,1,0:T(8,128)(2,1)S(1)}, u32[]{:S(2)}, u32[]{:S(2)}) collective-permute-start(bf16[2,2,128,128]{3,2,1,0:T(8,128)(2,1)S(1)} %get-tuple-element.70), channel_id=1, source_target_pairs={{0,24},{1,29},{2,26},{3,31},{4,28},{5,25},{6,30},{7,27},{8,16},{9,... | collective-permute-start | bytes 393224 | tf_op jit(solution)/shard_map/ppermute | solution.py:352
  43.0 11.9 %collective-permute-start.16 = (bf16[2,2,128,128]{3,2,1,0:T(8,128)(2,1)S(1)}, bf16[2,2,128,128]{3,2,1,0:T(8,128)(2,1)S(1)}, u32[]{:S(2)}, u32[]{:S(2)}) collective-permute-start(bf16[2,2,128,128]{3,2,1,0:T(8,128)(2,1)S(1)} %get-tuple-element.69), channel_id=1, source_target_pairs={{0,16},{1,21},{2,18},{3,23},{4,20},{5,17},{6,22},{7,19},{8,24},{9,... | collective-permute-start | bytes 393224 | tf_op jit(solution)/shard_map/ppermute | solution.py:352
  43.3 8.1 %collective-permute-start.21 = (bf16[2,2,2,128,128]{4,3,2,1,0:T(8,128)(2,1)S(1)}, bf16[2,2,2,128,128]{4,3,2,1,0:T(8,128)(2,1)S(1)}, u32[]{:S(2)}, u32[]{:S(2)}) collective-permute-start(bf16[2,2,2,128,128]{4,3,2,1,0:T(8,128)(2,1)S(1)} %shard_map.90.rest_2_), channel_id=1, source_target_pairs={{0,2},{1,3},{2,0},{3,1},{4,6},{5,7},{6,4},{7,5},{8,10},{9,11},{10,... | collective-permute-start | bytes 786440 | tf_op jit(solution)/shard_map/ppermute | solution.py:347
  44.4 12.4 %collective-permute-start.22 = (bf16[2,2,2,128,128]{4,3,2,1,0:T(8,128)(2,1)S(1)}, bf16[2,2,2,128,128]{4,3,2,1,0:T(8,128)(2,1)S(1)}, u32[]{:S(2)}, u32[]{:S(2)}) collective-permute-start(bf16[2,2,2,128,128]{4,3,2,1,0:T(8,128)(2,1)S(1)} %shard_map.90.rest_2_), channel_id=1, source_target_pairs={{0,1},{1,0},{2,3},{3,2},{4,5},{5,4},{6,7},{7,6},{8,9},{9,8},{10,11... | collective-permute-start | bytes 786440 | tf_op jit(solution)/shard_map/ppermute | solution.py:347
  49.0 7.9 %slice-start = ((s8[8388608]{0:T(1024)(128)(4,1)}), s8[4194304]{0:T(1024)(128)(4,1)S(1)}, s32[]{:S(2)}) async-start(s8[8388608]{0:T(1024)(128)(4,1)} %bitcast.9), calls=%async_computation | async-start | bytes 8388608
  49.0 7.9 %slice-start.1 = ((s8[8388608]{0:T(1024)(128)(4,1)}), s8[4194304]{0:T(1024)(128)(4,1)S(1)}, s32[]{:S(2)}) async-start(s8[8388608]{0:T(1024)(128)(4,1)} %bitcast.9), calls=%async_computation.1 | async-start | bytes 8388608
  49.0 7.9 %copy-start = (s32[2,64]{1,0:T(2,128)S(1)}, s32[2,64]{1,0:T(2,128)}, u32[]{:S(2)}) copy-start(s32[2,64]{1,0:T(2,128)} %dir_ref.3) | copy-start | bytes 1540
  49.1 6.5 %collective-permute-start.24 = (bf16[1,2,2,128,128]{4,3,2,1,0:T(8,128)(2,1)S(1)}, bf16[1,2,2,128,128]{4,3,2,1,0:T(8,128)(2,1)S(1)}, u32[]{:S(2)}, u32[]{:S(2)}) collective-permute-start(bf16[1,2,2,128,128]{4,3,2,1,0:T(8,128)(2,1)S(1)} %shard_map.89.rest_0_), channel_id=1, source_target_pairs={{0,2},{1,3},{2,0},{3,1},{4,6},{5,7},{6,4},{7,5},{8,10},{9,11},{10,... | collective-permute-start | bytes 393224 | tf_op jit(solution)/shard_map/ppermute | solution.py:347
  50.4 5.2 %collective-permute-start.25 = (bf16[1,2,2,128,128]{4,3,2,1,0:T(8,128)(2,1)S(1)}, bf16[1,2,2,128,128]{4,3,2,1,0:T(8,128)(2,1)S(1)}, u32[]{:S(2)}, u32[]{:S(2)}) collective-permute-start(bf16[1,2,2,128,128]{4,3,2,1,0:T(8,128)(2,1)S(1)} %shard_map.89.rest_0_), channel_id=1, source_target_pairs={{0,1},{1,0},{2,3},{3,2},{4,5},{5,4},{6,7},{7,6},{8,9},{9,8},{10,11... | collective-permute-start | bytes 393224 | tf_op jit(solution)/shard_map/ppermute | solution.py:347
  51.4 5.5 %collective-permute-start.23 = (bf16[2,2,2,128,128]{4,3,2,1,0:T(8,128)(2,1)S(1)}, bf16[2,2,2,128,128]{4,3,2,1,0:T(8,128)(2,1)S(1)}, u32[]{:S(2)}, u32[]{:S(2)}) collective-permute-start(bf16[2,2,2,128,128]{4,3,2,1,0:T(8,128)(2,1)S(1)} %collective-permute-done.21.rest_3_), channel_id=1, source_target_pairs={{0,1},{1,0},{2,3},{3,2},{4,5},{5,4},{6,7},{7,6},{8,9},{9,8},{10,11... | collective-permute-start | bytes 786440 | tf_op jit(solution)/shard_map/ppermute | solution.py:347
  54.9 1.9 %collective-permute-start.27 = (bf16[1,2,2,128,128]{4,3,2,1,0:T(8,128)(2,1)S(1)}, bf16[1,2,2,128,128]{4,3,2,1,0:T(8,128)(2,1)S(1)}, u32[]{:S(2)}, u32[]{:S(2)}) collective-permute-start(bf16[1,2,2,128,128]{4,3,2,1,0:T(8,128)(2,1)S(1)} %shard_map.88.rest_1_), channel_id=1, source_target_pairs={{0,1},{1,0},{2,3},{3,2},{4,5},{5,4},{6,7},{7,6},{8,9},{9,8},{10,11... | collective-permute-start | bytes 393224 | tf_op jit(solution)/shard_map/ppermute | solution.py:347
  55.6 1.3 %collective-permute-start.26 = (bf16[1,2,2,128,128]{4,3,2,1,0:T(8,128)(2,1)S(1)}, bf16[1,2,2,128,128]{4,3,2,1,0:T(8,128)(2,1)S(1)}, u32[]{:S(2)}, u32[]{:S(2)}) collective-permute-start(bf16[1,2,2,128,128]{4,3,2,1,0:T(8,128)(2,1)S(1)} %collective-permute-done.24.rest_6_), channel_id=1, source_target_pairs={{0,1},{1,0},{2,3},{3,2},{4,5},{5,4},{6,7},{7,6},{8,9},{9,8},{10,11... | collective-permute-start | bytes 393224 | tf_op jit(solution)/shard_map/ppermute | solution.py:347
  55.6 5.8 %collective-permute-start.17 = (bf16[1,2,2,128,128]{4,3,2,1,0:T(8,128)(2,1)S(1)}, bf16[1,2,2,128,128]{4,3,2,1,0:T(8,128)(2,1)S(1)}, u32[]{:S(2)}, u32[]{:S(2)}) collective-permute-start(bf16[1,2,2,128,128]{4,3,2,1,0:T(8,128)(2,1)S(1)} %shard_map.88.rest_1_), channel_id=1, source_target_pairs={{0,2},{1,3},{2,0},{3,1},{4,6},{5,7},{6,4},{7,5},{8,10},{9,11},{10,... | collective-permute-start | bytes 393224 | tf_op jit(solution)/shard_map/ppermute | solution.py:347
  61.5 1.3 %collective-permute-start.28 = (bf16[1,2,2,128,128]{4,3,2,1,0:T(8,128)(2,1)S(1)}, bf16[1,2,2,128,128]{4,3,2,1,0:T(8,128)(2,1)S(1)}, u32[]{:S(2)}, u32[]{:S(2)}) collective-permute-start(bf16[1,2,2,128,128]{4,3,2,1,0:T(8,128)(2,1)S(1)} %collective-permute-done.17.rest_0_), channel_id=1, source_target_pairs={{0,1},{1,0},{2,3},{3,2},{4,5},{5,4},{6,7},{7,6},{8,9},{9,8},{10,11... | collective-permute-start | bytes 393224 | tf_op jit(solution)/shard_map/ppermute | solution.py:347
